TPU v7x, 512 devices: a whole 4x8x8 slice. The times are simulated.
512 devices in a mesh: shard: 128 (over y, z, core), rep: 4 (over x).
Axes of the slice: x: 4, y: 8, z: 8, core: 2. Of those that a mesh axis runs over, the one named last changes fastest.
Arguments:
- embeds: bfloat16 [65536, 1024], P(('shard', 'rep')), may hold values from -25 to 25
- clusters: int32 [65536], P(('shard', 'rep')), may hold values from 0 to 511, as said below
- orders: int32 [65536], P(('shard', 'rep')), may hold values from 0 to 65535, each once
- owner_map: int32 [512], replicated, may hold values from 0 to 127, as said below
- neighbours: int32 [512, 2], replicated, may hold values from 0 to 511, as said below
Outputs:
- max_similarity: float32 [65536], P(('shard', 'rep'))
Inputs may be any that keep to these rules, and one draw needn't show every extreme that they name: The rows of one loader device (aligned blocks of 128 rows) put exactly 2 rows into the clusters of each of 64 owners (owner by owner_map) and none into the others; one owner receives 2 rows from every loader device. `owner_map`: every owner index owns exactly 4 clusters. `neighbours`: row c lists 2 different clusters other than c, each owned by the owner of c or by the owner one index below or above it, counted around the 128 owners.
All inputs are finite; a program needn't handle non-finite values.
Results may differ from a plain program's by a relative error of at most 0.00051.
Values may be sent and summed in bfloat16 or wider, within the bound.
No kernel may reach another device: no remote copies, remote signals or barrier semaphores. Data moves between devices by JAX's collectives and lax.ppermute only.
A program may use at most 64 MiB of HBM per device.

v0:
```python
import jax
import jax.numpy as jnp
from jax import lax
from jax.sharding import PartitionSpec as P


def with_halo(cells, sides, width):
    for axis, dim in sides:
        count = lax.axis_size(axis)
        head = lax.slice_in_dim(cells, 0, width, axis=dim)
        tail = lax.slice_in_dim(cells, cells.shape[dim] - width, cells.shape[dim], axis=dim)
        cells = jnp.concatenate(
            [
                lax.ppermute(tail, axis, [(i, (i + 1) % count) for i in range(count)]),
                cells,
                lax.ppermute(head, axis, [((i + 1) % count, i) for i in range(count)]),
            ],
            axis=dim,
        )
    return cells


def unit_of(embedded):
    scaled = embedded.astype(jnp.float32)
    mean_square = jnp.mean(scaled * scaled, axis=-1, keepdims=True)
    factor = lax.rsqrt(mean_square + 1e-06) * scaled.shape[-1] ** (-0.5)
    return (scaled * factor).astype(jnp.bfloat16)


def best_earlier(
    query_rows, query_order, query_cluster, key_rows, key_order, key_cluster, neighbours
):
    scores = lax.dot_general(
        query_rows, key_rows, (((1,), (1,)), ((), ())), preferred_element_type=jnp.float32
    )
    catalog = jnp.arange(neighbours.shape[0], dtype=jnp.int32)
    onehot = query_cluster[:, None] == catalog[None, :]
    related = key_cluster[None, :] == query_cluster[:, None]
    for column in range(neighbours.shape[1]):
        listed = jnp.sum(jnp.where(onehot, neighbours[None, :, column], 0), axis=1)
        related = related | (key_cluster[None, :] == listed[:, None])
    allowed = related & (key_order[None, :] >= 0) & (key_order[None, :] < query_order[:, None])
    return jnp.max(jnp.where(allowed, scores, jnp.float32(-1.0)), axis=1)


def body(embeds, clusters, orders, owner_map, neighbours):
    owner_count = lax.axis_size("shard")
    rows_here = embeds.shape[0]
    slot_size = rows_here // min(rows_here // 2, owner_count // 2)
    slot_total = owner_count * slot_size
    features = embeds.shape[1]
    unit_rows = unit_of(embeds)
    catalog = jnp.arange(owner_map.shape[0], dtype=jnp.int32)
    matched = clusters[:, None] == catalog[None, :]
    owner_index = jnp.sum(jnp.where(matched, owner_map[None, :], 0), axis=1)
    same_owner = owner_index[:, None] == owner_index[None, :]
    row_ids = jnp.arange(rows_here, dtype=jnp.int32)
    earlier = row_ids[:, None] > row_ids[None, :]
    slot_rank = jnp.sum((same_owner & earlier).astype(jnp.int32), axis=1)
    slot_index = owner_index * slot_size + slot_rank
    send_rows = jnp.zeros((slot_total, features), jnp.bfloat16).at[slot_index].set(unit_rows)
    send_order = jnp.full((slot_total,), -1, jnp.int32).at[slot_index].set(orders)
    send_cluster = jnp.zeros((slot_total,), jnp.int32).at[slot_index].set(clusters)
    got_rows, got_order, got_cluster = (
        lax.all_to_all(
            send_rows.reshape(owner_count, slot_size, features),
            "shard",
            split_axis=0,
            concat_axis=0,
            tiled=True,
        ),
        lax.all_to_all(
            send_order.reshape(owner_count, slot_size),
            "shard",
            split_axis=0,
            concat_axis=0,
            tiled=True,
        ),
        lax.all_to_all(
            send_cluster.reshape(owner_count, slot_size),
            "shard",
            split_axis=0,
            concat_axis=0,
            tiled=True,
        ),
    )
    query_rows = got_rows.reshape(slot_total, features)
    query_order = got_order.reshape(slot_total)
    query_cluster = got_cluster.reshape(slot_total)
    key_rows, key_order, key_cluster = (
        with_halo(query_rows, (("shard", 0),), slot_total),
        with_halo(query_order, (("shard", 0),), slot_total),
        with_halo(query_cluster, (("shard", 0),), slot_total),
    )
    share_fraction = lax.all_gather(
        (query_rows, query_order, query_cluster), "rep", axis=0, tiled=True
    )
    incomplete_value = best_earlier(
        share_fraction[0],
        share_fraction[1],
        share_fraction[2],
        key_rows,
        key_order,
        key_cluster,
        neighbours,
    )
    combined = lax.pmax(incomplete_value, "rep")
    own_best = lax.dynamic_slice_in_dim(combined, lax.axis_index("rep") * slot_total, slot_total)
    returned = lax.all_to_all(
        own_best.reshape(owner_count, slot_size), "shard", split_axis=0, concat_axis=0, tiled=True
    )
    return returned.reshape(slot_total)[slot_index]


def solution(mesh):
    placed = (P(("shard", "rep"), None), P(("shard", "rep")), P(("shard", "rep")), P(), P())
    return jax.shard_map(
        body, mesh=mesh, in_specs=placed, out_specs=P(("shard", "rep")), check_vma=False
    )
```

profile of v0, /device:TPU:1, one launch (start us, length us, event | category | flops | bytes accessed | tf_op | source)
XLA Modules:
  0.0 173.5 jit_solution(3920939407707783225)
XLA Ops:
  6.5 0.9 select_reduce_fusion.3
  7.4 0.2 convert_reduce_fusion
  7.6 1.1 fusion.8
  8.7 1.8 %scatter_custom_fusion.2 = bf16[256,1024]{1,0:T(8,128)(2,1)S(1)} fusion(s32[128]{0:T(128)S(1)} %fusion.15, bf16[128,1024]{1,0:T(8,128)(2,1)} %param.5, f32[128]{0:T(128)S(1)} %rsqrt_multiply_fusion, bf16[]{:T(256)} %constant.17.clone.1), kind=kCustom, calls=%fused_computation.18 | custom fusion | flops 393216 | bytes 786946 | tf_op jit(solution)/shard_map/scatter | solution.py:61
  10.5 0.0 copy-start
  10.5 0.2 reshape.104
  10.7 37.7 %all_to_all.32 = bf16[128,2,1024]{2,1,0:T(2,128)(2,1)S(1)} all-to-all(bf16[128,2,1024]{2,1,0:T(2,128)(2,1)S(1)} %reshape.104), channel_id=1, replica_groups=mesh['shard'=128,'rep'=4] {'shard'}, dimensions={0} | all-to-all | bytes 1048576 | tf_op jit(solution)/shard_map/all_to_all | solution.py:65
  48.4 1.0 reshape.105
  49.4 0.0 all-gather.4.cloned.1.call-update
  49.4 1.1 scatter_custom_fusion
  50.5 0.8 all_to_all.21
  51.3 7.2 %all-to-all-start = ((s32[128,1,2]{2,1,0:T(1,128)}), s32[128,1,2]{2,1,0:T(1,128)S(1)}, u32[]{:S(2)}, u32[]{:S(2)}) async-start(s32[128,1,2]{2,1,0:T(1,128)} %bitcast.2), calls=%async_computation | async-start | bytes 131072 | tf_op jit(solution)/shard_map/all_to_all | solution.py:79
  58.5 1.1 scatter_custom_fusion.1
  59.6 0.8 all_to_all.23
  60.4 9.8 %all-to-all-done = s32[128,1,2]{2,1,0:T(1,128)S(1)} async-done(((s32[128,1,2]{2,1,0:T(1,128)}), s32[128,1,2]{2,1,0:T(1,128)S(1)}, u32[]{:S(2)}, u32[]{:S(2)}) %all-to-all-start) | async-done | bytes 1056 | tf_op jit(solution)/shard_map/all_to_all | solution.py:79
  70.2 5.6 %all-to-all-start.1 = ((s32[128,1,2]{2,1,0:T(1,128)}), s32[128,1,2]{2,1,0:T(1,128)S(1)}, u32[]{:S(2)}, u32[]{:S(2)}) async-start(s32[128,1,2]{2,1,0:T(1,128)} %bitcast.6), calls=%async_computation.1 | async-start | bytes 131072 | tf_op jit(solution)/shard_map/all_to_all | solution.py:72
  75.9 0.5 broadcast.81
  76.4 0.8 reduce.14
  77.2 0.1 reshape.102
  77.3 2.9 %collective-permute-start.1 = (s32[256]{0:T(256)S(1)}, s32[256]{0:T(256)S(1)}, u32[]{:S(2)}, u32[]{:S(2)}) collective-permute-start(s32[256]{0:T(256)S(1)} %reshape.102), channel_id=1, source_target_pairs={{4,0},{8,4},{12,8},{16,12},{20,16},{24,20},{28,24},{32,28},{36,32}... | collective-permute-start | bytes 3080 | tf_op jit(solution)/shard_map/ppermute | solution.py:16
  80.2 2.6 %collective-permute-start = (s32[256]{0:T(256)S(1)}, s32[256]{0:T(256)S(1)}, u32[]{:S(2)}, u32[]{:S(2)}) collective-permute-start(s32[256]{0:T(256)S(1)} %reshape.102), channel_id=1, source_target_pairs={{0,4},{4,8},{8,12},{12,16},{16,20},{20,24},{24,28},{28,32},{32,36}... | collective-permute-start | bytes 3080 | tf_op jit(solution)/shard_map/ppermute | solution.py:14
  82.9 4.6 %all-to-all-done.1 = s32[128,1,2]{2,1,0:T(1,128)S(1)} async-done(((s32[128,1,2]{2,1,0:T(1,128)}), s32[128,1,2]{2,1,0:T(1,128)S(1)}, u32[]{:S(2)}, u32[]{:S(2)}) %all-to-all-start.1) | async-done | bytes 1056 | tf_op jit(solution)/shard_map/all_to_all | solution.py:72
  87.5 0.8 reduce.13
  88.3 0.1 reshape.103
  88.4 2.4 %collective-permute-start.3 = (s32[256]{0:T(256)S(1)}, s32[256]{0:T(256)S(1)}, u32[]{:S(2)}, u32[]{:S(2)}) collective-permute-start(s32[256]{0:T(256)S(1)} %reshape.103), channel_id=1, source_target_pairs={{4,0},{8,4},{12,8},{16,12},{20,16},{24,20},{28,24},{32,28},{36,32}... | collective-permute-start | bytes 3080 | tf_op jit(solution)/shard_map/ppermute | solution.py:16
  90.9 3.1 %collective-permute-start.2 = (s32[256]{0:T(256)S(1)}, s32[256]{0:T(256)S(1)}, u32[]{:S(2)}, u32[]{:S(2)}) collective-permute-start(s32[256]{0:T(256)S(1)} %reshape.103), channel_id=1, source_target_pairs={{0,4},{4,8},{8,12},{12,16},{16,20},{20,24},{24,28},{28,32},{32,36}... | collective-permute-start | bytes 3080 | tf_op jit(solution)/shard_map/ppermute | solution.py:14
  94.0 0.1 reshape.139
  94.2 0.1 reshape.141
  94.3 8.0 %all-gather = s32[4,1,256]{2,1,0:T(1,128)S(1)} all-gather(s32[1,1,256]{2,1,0:T(1,128)S(1)} %reshape.139), channel_id=1, replica_groups=mesh['shard'=128,'rep'=4] {'rep'}, dimensions={0}, use_global_device_ids=true | all-gather | bytes 5120 | tf_op jit(solution)/shard_map/all_gather | solution.py:95
  102.3 0.9 select_reduce_fusion.2
  103.2 5.2 %all-gather.1 = s32[4,1,256]{2,1,0:T(1,128)S(1)} all-gather(s32[1,1,256]{2,1,0:T(1,128)S(1)} %reshape.141), channel_id=1, replica_groups=mesh['shard'=128,'rep'=4] {'rep'}, dimensions={0}, use_global_device_ids=true | all-gather | bytes 5120 | tf_op jit(solution)/shard_map/all_gather | solution.py:95
  108.4 0.0 collective-permute-done.2
  108.4 8.3 %collective-permute-start.5 = (bf16[256,1024]{1,0:T(8,128)(2,1)}, bf16[256,1024]{1,0:T(8,128)(2,1)S(1)}, u32[]{:S(2)}, u32[]{:S(2)}) collective-permute-start(bf16[256,1024]{1,0:T(8,128)(2,1)} %reshape.105), channel_id=1, source_target_pairs={{4,0},{8,4},{12,8},{16,12},{20,16},{24,20},{28,24},{32,28},{36,32}... | collective-permute-start | bytes 1572872 | tf_op jit(solution)/shard_map/ppermute | solution.py:16
  116.8 2.1 %collective-permute-start.4 = (bf16[256,1024]{1,0:T(8,128)(2,1)}, bf16[256,1024]{1,0:T(8,128)(2,1)S(1)}, u32[]{:S(2)}, u32[]{:S(2)}) collective-permute-start(bf16[256,1024]{1,0:T(8,128)(2,1)} %reshape.105), channel_id=1, source_target_pairs={{0,4},{4,8},{8,12},{12,16},{16,20},{20,24},{24,28},{28,32},{32,36}... | collective-permute-start | bytes 1572872 | tf_op jit(solution)/shard_map/ppermute | solution.py:14
  118.9 0.0 collective-permute-done.3
  118.9 0.0 collective-permute-done.1
  119.0 1.9 %collective-permute-done.5 = bf16[256,1024]{1,0:T(8,128)(2,1)S(1)} collective-permute-done((bf16[256,1024]{1,0:T(8,128)(2,1)}, bf16[256,1024]{1,0:T(8,128)(2,1)S(1)}, u32[]{:S(2)}, u32[]{:S(2)}) %collective-permute-start.5) | collective-permute-done | bytes 524320 | tf_op jit(solution)/shard_map/ppermute | solution.py:16
  120.9 4.2 %collective-permute-done.4 = bf16[256,1024]{1,0:T(8,128)(2,1)S(1)} collective-permute-done((bf16[256,1024]{1,0:T(8,128)(2,1)}, bf16[256,1024]{1,0:T(8,128)(2,1)S(1)}, u32[]{:S(2)}, u32[]{:S(2)}) %collective-permute-start.4) | collective-permute-done | bytes 524320 | tf_op jit(solution)/shard_map/ppermute | solution.py:14
  125.1 4.0 %select_reduce_fusion = f32[1024]{0:T(1024)S(1)} fusion(bf16[1024,1024]{1,0:T(8,128)(2,1)} %all-gather.4.cloned.1.call-done, bf16[256,1024]{1,0:T(8,128)(2,1)S(1)} %collective-permute-done.5, bf16[256,1024]{1,0:T(8,128)(2,1)} %reshape.105, bf16[256,1024]{1,0:T(8,128)(2,1)S(1)} %collective-permute-done.4, s32[1024]{0:T(1024)S(1)} %bitcast.23, ...), kind=kOutput, calls=%fused_computation.4 | convolution fusion | flops 1623194624 | bytes 3697408 | tf_op jit(solution)/shard_map/dot_general | solution.py:33
  129.2 7.7 %pmax.7 = f32[1024]{0:T(1024)S(1)} all-reduce(f32[1024]{0:T(1024)S(1)} %select_reduce_fusion), channel_id=1, replica_groups=mesh['shard'=128,'rep'=4] {'rep'}, use_global_device_ids=true, to_apply=%region_9.10 | all-reduce | flops 1024 | bytes 8192 | tf_op jit(solution)/shard_map/pmax | solution.py:107
  136.9 0.1 dynamic_slice.3
  137.0 0.8 all_to_all.26
  137.8 14.2 %all-to-all-start.3 = ((f32[128,1,2]{2,1,0:T(1,128)}), f32[128,1,2]{2,1,0:T(1,128)S(1)}, u32[]{:S(2)}, u32[]{:S(2)}) async-start(f32[128,1,2]{2,1,0:T(1,128)} %bitcast.8), calls=%async_computation.3 | async-start | bytes 131072 | tf_op jit(solution)/shard_map/all_to_all | solution.py:109
  151.9 11.5 %all-to-all-done.3 = f32[128,1,2]{2,1,0:T(1,128)S(1)} async-done(((f32[128,1,2]{2,1,0:T(1,128)}), f32[128,1,2]{2,1,0:T(1,128)S(1)}, u32[]{:S(2)}, u32[]{:S(2)}) %all-to-all-start.3) | async-done | bytes 1056 | tf_op jit(solution)/shard_map/all_to_all | solution.py:109
  163.5 0.5 broadcast.83
  164.0 0.8 reduce.15
  164.8 0.1 reshape.106
  164.9 1.8 %gather_fusion = f32[128]{0:T(128)} fusion(f32[256]{0:T(256)S(1)} %reshape.106, s32[1024]{0:T(1024)S(1)} %pad_clamp_fusion), kind=kCustom, calls=%fused_computation | custom fusion | bytes 1536 | tf_op jit(solution)/shard_map/gather | solution.py:112
  (14 shorter events, 0.1 us)
Async XLA Ops:
  6.5 118.6 %all-gather.4.cloned.1.call-start = ((), (), s32[]{:S(2)}) async-start(), calls=%async_computation.4 | async-start | bytes 2621440 | tf_op jit(solution)/shard_map/all_gather | solution.py:95
  10.5 65.3 %copy-start = (s32[512,2]{0,1:T(2,128)S(1)}, s32[512,2]{0,1:T(2,128)}, u32[]{:S(2)}) copy-start(s32[512,2]{0,1:T(2,128)} %param.9) | copy-start | bytes 12292
  51.3 18.9 %all-to-all-start = ((s32[128,1,2]{2,1,0:T(1,128)}), s32[128,1,2]{2,1,0:T(1,128)S(1)}, u32[]{:S(2)}, u32[]{:S(2)}) async-start(s32[128,1,2]{2,1,0:T(1,128)} %bitcast.2), calls=%async_computation | async-start | bytes 131072 | tf_op jit(solution)/shard_map/all_to_all | solution.py:79
  70.2 17.3 %all-to-all-start.1 = ((s32[128,1,2]{2,1,0:T(1,128)}), s32[128,1,2]{2,1,0:T(1,128)S(1)}, u32[]{:S(2)}, u32[]{:S(2)}) async-start(s32[128,1,2]{2,1,0:T(1,128)} %bitcast.6), calls=%async_computation.1 | async-start | bytes 131072 | tf_op jit(solution)/shard_map/all_to_all | solution.py:72
  77.3 41.6 %collective-permute-start.1 = (s32[256]{0:T(256)S(1)}, s32[256]{0:T(256)S(1)}, u32[]{:S(2)}, u32[]{:S(2)}) collective-permute-start(s32[256]{0:T(256)S(1)} %reshape.102), channel_id=1, source_target_pairs={{4,0},{8,4},{12,8},{16,12},{20,16},{24,20},{28,24},{32,28},{36,32}... | collective-permute-start | bytes 3080 | tf_op jit(solution)/shard_map/ppermute | solution.py:16
  80.2 38.7 %collective-permute-start = (s32[256]{0:T(256)S(1)}, s32[256]{0:T(256)S(1)}, u32[]{:S(2)}, u32[]{:S(2)}) collective-permute-start(s32[256]{0:T(256)S(1)} %reshape.102), channel_id=1, source_target_pairs={{0,4},{4,8},{8,12},{12,16},{16,20},{20,24},{24,28},{28,32},{32,36}... | collective-permute-start | bytes 3080 | tf_op jit(solution)/shard_map/ppermute | solution.py:14
  88.4 30.5 %collective-permute-start.3 = (s32[256]{0:T(256)S(1)}, s32[256]{0:T(256)S(1)}, u32[]{:S(2)}, u32[]{:S(2)}) collective-permute-start(s32[256]{0:T(256)S(1)} %reshape.103), channel_id=1, source_target_pairs={{4,0},{8,4},{12,8},{16,12},{20,16},{24,20},{28,24},{32,28},{36,32}... | collective-permute-start | bytes 3080 | tf_op jit(solution)/shard_map/ppermute | solution.py:16
  90.9 17.6 %collective-permute-start.2 = (s32[256]{0:T(256)S(1)}, s32[256]{0:T(256)S(1)}, u32[]{:S(2)}, u32[]{:S(2)}) collective-permute-start(s32[256]{0:T(256)S(1)} %reshape.103), channel_id=1, source_target_pairs={{0,4},{4,8},{8,12},{12,16},{16,20},{20,24},{24,28},{28,32},{32,36}... | collective-permute-start | bytes 3080 | tf_op jit(solution)/shard_map/ppermute | solution.py:14
  108.4 12.4 %collective-permute-start.5 = (bf16[256,1024]{1,0:T(8,128)(2,1)}, bf16[256,1024]{1,0:T(8,128)(2,1)S(1)}, u32[]{:S(2)}, u32[]{:S(2)}) collective-permute-start(bf16[256,1024]{1,0:T(8,128)(2,1)} %reshape.105), channel_id=1, source_target_pairs={{4,0},{8,4},{12,8},{16,12},{20,16},{24,20},{28,24},{32,28},{36,32}... | collective-permute-start | bytes 1572872 | tf_op jit(solution)/shard_map/ppermute | solution.py:16
  116.8 8.3 %collective-permute-start.4 = (bf16[256,1024]{1,0:T(8,128)(2,1)}, bf16[256,1024]{1,0:T(8,128)(2,1)S(1)}, u32[]{:S(2)}, u32[]{:S(2)}) collective-permute-start(bf16[256,1024]{1,0:T(8,128)(2,1)} %reshape.105), channel_id=1, source_target_pairs={{0,4},{4,8},{8,12},{12,16},{16,20},{20,24},{24,28},{28,32},{32,36}... | collective-permute-start | bytes 1572872 | tf_op jit(solution)/shard_map/ppermute | solution.py:14
  137.8 25.7 %all-to-all-start.3 = ((f32[128,1,2]{2,1,0:T(1,128)}), f32[128,1,2]{2,1,0:T(1,128)S(1)}, u32[]{:S(2)}, u32[]{:S(2)}) async-start(f32[128,1,2]{2,1,0:T(1,128)} %bitcast.8), calls=%async_computation.3 | async-start | bytes 131072 | tf_op jit(solution)/shard_map/all_to_all | solution.py:109
Sparse Core Ops, SparseCore 0:
  49.5 29.7 all-gather.3
where the time goes:
time: 174 us
  blocking collectives  58.7 us (34%)
  starting transfers between devices  48.6 us (28%)
  waiting for transfers between devices  32.1 us (18%)
  between operations  13.7 us (8%)
  local copies, waits for them, and re-layouts  9.26 us (5%)
  other arithmetic  7.27 us (4%)
  matrix products  4.05 us (2%)
    all_to_all x1, blocking collectives, body(): lax.all_to_all(send_rows.reshape(owner_count, slot_size, features), 'shar...  37.7 us
    all_to_all x1, starting transfers between devices, body(): lax.all_to_all(own_best.reshape(owner_count, slot_size), 'shard', split_a...  14.2 us
    ppermute x3, starting transfers between devices, with_halo(): lax.ppermute(head, axis, [((i + 1) % count, i) for i in range(count)])  13.7 us
    all_gather x2, blocking collectives, body(): lax.all_gather((query_rows, query_order, query_cluster), 'rep', axis=0, t...  13.2 us
    all_to_all x1, waiting for transfers between devices, body(): lax.all_to_all(own_best.reshape(owner_count, slot_size), 'shard', split_a...  11.5 us
    all_to_all x1, waiting for transfers between devices, body(): lax.all_to_all(send_cluster.reshape(owner_count, slot_size), 'shard', spl...  9.78 us
    ppermute x3, starting transfers between devices, with_halo(): lax.ppermute(tail, axis, [(i, (i + 1) % count) for i in range(count)])  7.88 us
    pmax x1, blocking collectives, body(): combined = lax.pmax(incomplete_value, 'rep')  7.74 us
  transfers between devices with their start and end apart: 10, of which 5 were waited for; matrix products, arithmetic and copies ran while one was open for 3% of the time, Pallas kernels for 0%

commit v1 on v0

v1 whole, which is shorter than its diff:
```python
import jax
import jax.numpy as jnp
from jax import lax
from jax.experimental import pallas as pl
from jax.experimental.pallas import tpu as pltpu
from jax.sharding import PartitionSpec as P

AXES = ("shard", "rep")
Y, Z, X = 8, 8, 4
OWNERS = 128
LOAD = 128
D = 1024
LANES = 128
BLOCKS = D // LANES
ROWS_MSG = 24
WIDE = D + LANES
QUART = 2 * OWNERS
F32, BF16 = jnp.float32, jnp.bfloat16


def device_of(owner, core, half):
    step, bit = divmod(owner % OWNERS, 2)
    y, z = divmod(step, Z)
    if y % 2:
        z = Z - 1 - z
    pair = bit ^ (step & 1)
    return ((y * Z + z) * 2 + core) * X + 2 * pair + (half ^ pair)


QUARTERS = [(core, half) for core in range(2) for half in range(2)]
GROUPS = [[device_of(o, c, h) for o in range(OWNERS)] for c, h in QUARTERS]
EVERY = [[device_of(o, c, h) for o in range(OWNERS) for c, h in QUARTERS]]


def moves(shift, core, half):
    return [
        (device_of(o, c, h), device_of(o + shift, c ^ core, h ^ half))
        for o in range(OWNERS)
        for c, h in QUARTERS
    ]


X_SWAP = moves(0, 0, 1)
C_SWAP = moves(0, 1, 0)
UP = moves(1, 0, 0)
DOWN = moves(-1, 0, 0)


def iota(shape, dim):
    return lax.broadcasted_iota(jnp.int32, shape, dim)


def nt(a, b):
    return lax.dot_general(a, b, (((1,), (1,)), ((), ())), preferred_element_type=F32)


def ones_where(mask):
    return jnp.where(mask, 1.0, 0.0).astype(BF16)


def pack_kernel(x_ref, cl_ref, ord_ref, map_ref, nbr_ref, out_ref, place_ref, wide_ref):
    clusters = cl_ref[...]
    orders = ord_ref[...]
    count = map_ref.shape[1]
    onehot = ones_where(iota((count, LOAD), 0) == clusters)
    first, second = nbr_ref[0:1, :], nbr_ref[1:2, :]
    row = iota((16, count), 0)
    table = jnp.where(row == 0, map_ref[...], 0)
    for at, value in enumerate((first >> 8, first & 255, second >> 8, second & 255)):
        table = jnp.where(row == 4 + at, value, table)
    looked = jnp.dot(table.astype(F32).astype(BF16), onehot, preferred_element_type=F32)
    owner = looked[0:1, :]
    across = jnp.broadcast_to(owner, (LOAD, LOAD))
    below = across.T
    before = iota((LOAD, LOAD), 0) < iota((LOAD, LOAD), 1)
    rank = jnp.sum(jnp.where((across == below) & before, 1.0, 0.0), axis=0, keepdims=True)
    row = iota((16, LOAD), 0)
    meta = jnp.where(row == 8, 1.0, jnp.where((row >= 4) & (row < 8), looked, 0.0))
    for at, value in enumerate((orders >> 8, orders & 255, clusters >> 8, clusters & 255)):
        meta = jnp.where(row == at, value.astype(F32), meta)
    meta = jnp.concatenate([meta, jnp.zeros((LANES - 16, LOAD), F32)], axis=0).astype(BF16)

    scaled = x_ref[...].astype(F32)
    mean_square = jnp.mean(scaled * scaled, axis=-1, keepdims=True)
    factor = lax.rsqrt(mean_square + 1e-06) * D ** (-0.5)
    unit = (scaled * factor).astype(BF16)

    target = iota((OWNERS, LOAD), 0).astype(F32)
    for k in range(2):
        pick = ones_where((owner == target) & (rank == float(k)))
        rows = jnp.dot(pick, unit, preferred_element_type=F32)
        for b in range(BLOCKS):
            at = pl.ds(k * BLOCKS + b, OWNERS, stride=ROWS_MSG)
            wide_ref[at, :] = rows[:, b * LANES : (b + 1) * LANES]
        wide_ref[pl.ds(2 * BLOCKS + k, OWNERS, stride=ROWS_MSG), :] = nt(pick, meta)
    for j in range(2 * BLOCKS + 2, ROWS_MSG):
        wide_ref[pl.ds(j, OWNERS, stride=ROWS_MSG), :] = jnp.zeros((OWNERS, LANES), F32)
    out_ref[...] = wide_ref[...].astype(BF16)
    row = iota((8, LOAD), 0)
    place_ref[...] = jnp.where(row == 0, owner, rank)


def unpack_kernel(got_ref, out_ref, wide_ref):
    wide_ref[...] = got_ref[...].astype(F32)
    for k in range(2):
        here = pl.ds(k * OWNERS, OWNERS)
        for b in range(BLOCKS):
            at = pl.ds(k * BLOCKS + b, OWNERS, stride=ROWS_MSG)
            out_ref[here, pl.ds(b * LANES, LANES)] = wide_ref[at, :].astype(BF16)
        at = pl.ds(2 * BLOCKS + k, OWNERS, stride=ROWS_MSG)
        out_ref[here, pl.ds(D, LANES)] = wide_ref[at, :].astype(BF16)


def key_meta(key_ref):
    row, lane = iota((16, LANES), 0), iota((16, LANES), 1)
    take = jnp.where(lane == 2 * row, 256.0, jnp.where(lane == 2 * row + 1, 1.0, 0.0))
    take = jnp.where(row < 4, take, jnp.where((row == 4) & (lane == 8), 1.0, 0.0))
    got = nt(take.astype(BF16), key_ref[:, D:WIDE])
    order = jnp.where(got[4:5, :] > 0.0, got[0:1, :], 1e9)
    return order, got[1:2, :]


def score_kernel(own_ref, far_ref, core_ref, both_ref, low_ref, high_ref, out_ref):
    device = lax.axis_index("shard") * X + lax.axis_index("rep")
    x = device & 3
    quarter = ((device >> 2) & 1) * 2 + ((x >> 1) ^ (x & 1))
    keys = [(ref, *key_meta(ref)) for ref in (low_ref, own_ref, high_ref)]
    lane = iota((OWNERS, LANES), 1)
    for flip, query in enumerate((own_ref, far_ref, core_ref, both_ref)):
        meta = query[:, D:WIDE].astype(F32)
        order, cluster, first, second = (
            meta[:, 2 * j : 2 * j + 1] * 256.0 + meta[:, 2 * j + 1 : 2 * j + 2] for j in range(4)
        )
        best = None
        for key, key_order, key_cluster in keys:
            scores = nt(query[:, 0:D], key[:, 0:D])
            related = (key_cluster == cluster) | (key_cluster == first) | (key_cluster == second)
            allowed = related & (key_order < order)
            scores = jnp.where(allowed, scores, -1.0)
            best = scores if best is None else jnp.maximum(best, scores)
        best = jnp.max(best, axis=1, keepdims=True)
        pair = jnp.where(lane == 0, best[0:OWNERS, :], best[OWNERS:QUART, :])
        out_ref[pl.ds(quarter ^ flip, OWNERS, stride=4), :] = pair


def pick_kernel(got_ref, place_ref, out_ref):
    best = got_ref[pl.ds(0, OWNERS, stride=4), :]
    for q in range(1, 4):
        best = jnp.maximum(best, got_ref[pl.ds(q, OWNERS, stride=4), :])
    owner, rank = place_ref[0:1, :], place_ref[1:2, :]
    mine = owner == iota((OWNERS, LOAD), 0).astype(F32)
    values = jnp.where(rank == 0.0, best[:, 0:1], best[:, 1:2])
    out_ref[...] = jnp.max(jnp.where(mine, values, -2.0), axis=0, keepdims=True)


def call(kernel, outs, scratch=(), flops=0, size=1 << 20):
    return pl.pallas_call(
        kernel,
        out_shape=outs,
        scratch_shapes=list(scratch),
        compiler_params=pltpu.CompilerParams(vmem_limit_bytes=24 << 20),
        cost_estimate=pl.CostEstimate(flops=flops, bytes_accessed=size, transcendentals=0),
    )


def shape(dims, dtype):
    return jax.ShapeDtypeStruct(dims, dtype)


def body(embeds, clusters, orders, owner_map, neighbours):
    wire = OWNERS * ROWS_MSG
    scratch = [pltpu.VMEM((wire, LANES), F32)]
    packed, place = call(
        pack_kernel, [shape((wire, LANES), BF16), shape((8, LOAD), F32)], scratch, 10**8
    )(
        embeds,
        clusters.reshape(1, LOAD),
        orders.reshape(1, LOAD),
        owner_map.reshape(1, -1),
        neighbours.T,
    )
    got = lax.all_to_all(
        packed.reshape(OWNERS, ROWS_MSG, LANES),
        AXES,
        0,
        0,
        axis_index_groups=GROUPS,
        tiled=True,
    )
    own = call(unpack_kernel, shape((QUART, WIDE), BF16), scratch)(got.reshape(wire, LANES))
    far = lax.ppermute(own, AXES, X_SWAP)
    low = lax.ppermute(own, AXES, UP)
    high = lax.ppermute(own, AXES, DOWN)
    core = lax.ppermute(own, AXES, C_SWAP)
    both = lax.ppermute(far, AXES, C_SWAP)
    best = call(score_kernel, shape((4 * OWNERS, LANES), F32), (), 16 * 10**8)(
        own, far, core, both, low, high
    )
    back = lax.all_to_all(
        best.reshape(4 * OWNERS, 1, LANES), AXES, 0, 0, axis_index_groups=EVERY, tiled=True
    )
    return call(pick_kernel, shape((1, LOAD), F32))(
        back.reshape(4 * OWNERS, LANES), place
    ).reshape(LOAD)


def solution(mesh):
    placed = (P(AXES, None), P(AXES), P(AXES), P(), P())
    return jax.shard_map(body, mesh=mesh, in_specs=placed, out_specs=P(AXES), check_vma=False)
```

time: 174 us -> 103 us (0.59)
  waiting for transfers between devices: 32.1 us -> 1.63 us
  starting transfers between devices: 48.6 us -> 19.5 us
  blocking collectives: 58.7 us -> 76.1 us
  between operations: 13.7 us -> 0.1 us
  local copies, waits for them, and re-layouts: 9.26 us -> 1.64 us
  other arithmetic: 7.27 us -> 0 us
  Pallas kernels: 0 us -> 4.08 us
  matrix products: 4.05 us -> 0 us
    all_to_all x1 -> x2, blocking collectives: 37.7 us -> 76.1 us  [the longest x1 45.7 us: body(): lax.all_to_all(packed.reshape(OWNERS, ROWS_MSG, LANES), AXES, 0, 0, axis_...]
    all_to_all x3 -> x0, starting transfers between devices: 27 us -> none  [the longest x1 14.2 us: body(): lax.all_to_all(own_best.reshape(owner_count, slot_size), 'shard', split_a...]
    all_to_all x3 -> x0, waiting for transfers between devices: 25.9 us -> none  [the longest x1 11.5 us: body(): lax.all_to_all(own_best.reshape(owner_count, slot_size), 'shard', split_a...]
    all_gather x2 -> x0, blocking collectives: 13.2 us -> none  [body(): lax.all_gather((query_rows, query_order, query_cluster), 'rep', axis=0, t...]
    pmax x1 -> x0, blocking collectives: 7.74 us -> none  [body(): combined = lax.pmax(incomplete_value, 'rep')]
    ppermute x6 -> x5, waiting for transfers between devices: 6.16 us -> 1.63 us  [the longest x1 1.58 us: body(): both = lax.ppermute(far, AXES, C_SWAP)]
    pallas_call x0 -> x4, Pallas kernels: none -> 4.08 us  [the longest x1 2.36 us: body(): call(score_kernel, shape((4 * OWNERS, LANES), F32), (), 16 * 10 ** 8)]
    dot_general x1 -> x0, matrix products: 4.05 us -> none  [best_earlier(): lax.dot_general(query_rows, key_rows, (((1,), (1,)), ((), ())), preferred...]
  transfers between devices with their start and end apart: 10 -> 5, of which waited for: 5 -> 1; matrix products, arithmetic and copies ran while one was open for 3% -> 0% of each run, Pallas kernels for 0% -> 0%
where the time goes in v1:
time: 103 us
  blocking collectives  76.1 us (74%)
  starting transfers between devices  19.5 us (19%)
  Pallas kernels  4.08 us (4%)
  local copies, waits for them, and re-layouts  1.64 us (2%)
  waiting for transfers between devices  1.63 us (2%)
    all_to_all x1, blocking collectives, body(): lax.all_to_all(packed.reshape(OWNERS, ROWS_MSG, LANES), AXES, 0, 0, axis_...  45.7 us
    all_to_all x1, blocking collectives, body(): lax.all_to_all(best.reshape(4 * OWNERS, 1, LANES), AXES, 0, 0, axis_index...  30.4 us
    ppermute x1, starting transfers between devices, body(): both = lax.ppermute(far, AXES, C_SWAP)  5.7 us
    ppermute x1, starting transfers between devices, body(): core = lax.ppermute(own, AXES, C_SWAP)  5.35 us
    ppermute x1, starting transfers between devices, body(): low = lax.ppermute(own, AXES, UP)  3.88 us
    ppermute x1, starting transfers between devices, body(): high = lax.ppermute(own, AXES, DOWN)  2.61 us
    pallas_call x1, Pallas kernels, body(): call(score_kernel, shape((4 * OWNERS, LANES), F32), (), 16 * 10 ** 8)  2.36 us
  transfers between devices with their start and end apart: 5, of which 1 were waited for; matrix products, arithmetic and copies ran while one was open for 0% of the time, Pallas kernels for 0%

profile of v1, /device:TPU:1, one launch (start us, length us, event | category | flops | bytes accessed | tf_op | source)
XLA Modules:
  0.0 103.0 jit_solution(7318863767659852019)
XLA Ops:
  0.0 0.0 copy-start.1
  0.0 0.0 copy-start.2
  0.0 0.0 copy-start.3
  0.0 0.0 copy-start.4
  0.0 0.7 copy-done.1
  0.7 0.0 copy-done.2
  0.7 0.0 copy-done.3
  0.7 0.0 copy-done.4
  0.7 0.0 copy-start
  0.7 0.9 copy-done
  1.7 0.8 shard_map.55
  2.4 45.7 %all_to_all.10 = bf16[128,24,128]{2,1,0:T(8,128)(2,1)S(1)} all-to-all(bf16[128,24,128]{2,1,0:T(8,128)(2,1)S(1)} %bitcast.13), channel_id=1, replica_groups={{0,3,11,8,16,19,27,24,32,35,43,40,48,51,59,56,120,123,115,112,104,107,9..., dimensions={0} | all-to-all | bytes 1572864 | tf_op jit(solution)/shard_map/all_to_all | solution.py:182
  48.2 0.3 shard_map.56.own_ref
  48.5 1.9 %collective-permute-start = (bf16[256,1152]{1,0:T(8,128)(2,1)S(1)}, bf16[256,1152]{1,0:T(8,128)(2,1)S(1)}, u32[]{:S(2)}, u32[]{:S(2)}) collective-permute-start(bf16[256,1152]{1,0:T(8,128)(2,1)S(1)} %shard_map.56.own_ref), channel_id=1, source_target_pairs={{0,1},{1,0},{4,5},{5,4},{3,2},{2,3},{7,6},{6,7},{11,10},{10,11},{1... | collective-permute-start | bytes 1769480 | tf_op jit(solution)/shard_map/ppermute | solution.py:191
  50.4 2.6 %collective-permute-start.4 = (bf16[256,1152]{1,0:T(8,128)(2,1)S(1)}, bf16[256,1152]{1,0:T(8,128)(2,1)S(1)}, u32[]{:S(2)}, u32[]{:S(2)}) collective-permute-start(bf16[256,1152]{1,0:T(8,128)(2,1)S(1)} %shard_map.56.own_ref), channel_id=1, source_target_pairs={{0,448},{1,449},{4,452},{5,453},{3,0},{2,1},{7,4},{6,5},{11,3},{10... | collective-permute-start | bytes 1769480 | tf_op jit(solution)/shard_map/ppermute | solution.py:193
  53.0 3.9 %collective-permute-start.3 = (bf16[256,1152]{1,0:T(8,128)(2,1)S(1)}, bf16[256,1152]{1,0:T(8,128)(2,1)S(1)}, u32[]{:S(2)}, u32[]{:S(2)}) collective-permute-start(bf16[256,1152]{1,0:T(8,128)(2,1)S(1)} %shard_map.56.own_ref), channel_id=1, source_target_pairs={{0,3},{1,2},{4,7},{5,6},{3,11},{2,10},{7,15},{6,14},{11,8},{10,9},... | collective-permute-start | bytes 1769480 | tf_op jit(solution)/shard_map/ppermute | solution.py:192
  56.9 5.3 %collective-permute-start.1 = (bf16[256,1152]{1,0:T(8,128)(2,1)S(1)}, bf16[256,1152]{1,0:T(8,128)(2,1)S(1)}, u32[]{:S(2)}, u32[]{:S(2)}) collective-permute-start(bf16[256,1152]{1,0:T(8,128)(2,1)S(1)} %shard_map.56.own_ref), channel_id=1, source_target_pairs={{0,4},{1,5},{4,0},{5,1},{3,7},{2,6},{7,3},{6,2},{11,15},{10,14},{1... | collective-permute-start | bytes 1769480 | tf_op jit(solution)/shard_map/ppermute | solution.py:194
  62.3 0.0 collective-permute-done.far_ref
  62.3 5.7 %collective-permute-start.2 = (bf16[256,1152]{1,0:T(8,128)(2,1)S(1)}, bf16[256,1152]{1,0:T(8,128)(2,1)S(1)}, u32[]{:S(2)}, u32[]{:S(2)}) collective-permute-start(bf16[256,1152]{1,0:T(8,128)(2,1)S(1)} %collective-permute-done.far_ref), channel_id=1, source_target_pairs={{0,4},{1,5},{4,0},{5,1},{3,7},{2,6},{7,3},{6,2},{11,15},{10,14},{1... | collective-permute-start | bytes 1769480 | tf_op jit(solution)/shard_map/ppermute | solution.py:195
  68.0 0.0 collective-permute-done.4.high_ref
  68.0 0.0 collective-permute-done.3.low_ref
  68.1 0.0 collective-permute-done.1.core_ref
  68.1 1.6 %collective-permute-done.2.both_ref = bf16[256,1152]{1,0:T(8,128)(2,1)S(1)} collective-permute-done((bf16[256,1152]{1,0:T(8,128)(2,1)S(1)}, bf16[256,1152]{1,0:T(8,128)(2,1)S(1)}, u32[]{:S(2)}, u32[]{:S(2)}) %collective-permute-start.2) | collective-permute-done | bytes 589856 | tf_op jit(solution)/shard_map/ppermute | solution.py:195
  69.6 2.4 %shard_map.57 = f32[512,128]{1,0:T(8,128)S(1)} custom-call(bf16[256,1152]{1,0:T(8,128)(2,1)S(1)} %shard_map.56.own_ref, bf16[256,1152]{1,0:T(8,128)(2,1)S(1)} %collective-permute-done.far_ref, bf16[256,1152]{1,0:T(8,128)(2,1)S(1)} %collective-permute-done.1.core_ref, bf16[256,1152]{1,0:T(8,128)(2,1)S(1)} %collective-permute-done.2.both_ref, ...), custom_call_target="tpu_custom_call" | custom-call | flops 1600000000 | bytes 1048576 | tf_op jit(solution)/shard_map/pallas_call | solution.py:196
  72.0 30.4 %all_to_all.11 = f32[512,1,128]{2,1,0:T(1,128)S(1)} all-to-all(f32[512,1,128]{2,1,0:T(1,128)S(1)} %bitcast.14), channel_id=1, replica_groups={{0,1,4,5,3,2,7,6,11,10,15,14,8,9,12,13,16,17,20,21,19,18,23,22,27,26,31..., dimensions={0} | all-to-all | bytes 524288 | tf_op jit(solution)/shard_map/all_to_all | solution.py:199
  102.4 0.6 shard_map.58
Async XLA Ops:
  0.0 0.7 copy-start.1
  0.0 0.7 copy-start.2
  0.0 0.7 copy-start.3
  0.0 0.7 copy-start.4
  0.7 1.0 copy-start
  48.5 13.8 %collective-permute-start = (bf16[256,1152]{1,0:T(8,128)(2,1)S(1)}, bf16[256,1152]{1,0:T(8,128)(2,1)S(1)}, u32[]{:S(2)}, u32[]{:S(2)}) collective-permute-start(bf16[256,1152]{1,0:T(8,128)(2,1)S(1)} %shard_map.56.own_ref), channel_id=1, source_target_pairs={{0,1},{1,0},{4,5},{5,4},{3,2},{2,3},{7,6},{6,7},{11,10},{10,11},{1... | collective-permute-start | bytes 1769480 | tf_op jit(solution)/shard_map/ppermute | solution.py:191
  50.4 17.6 %collective-permute-start.4 = (bf16[256,1152]{1,0:T(8,128)(2,1)S(1)}, bf16[256,1152]{1,0:T(8,128)(2,1)S(1)}, u32[]{:S(2)}, u32[]{:S(2)}) collective-permute-start(bf16[256,1152]{1,0:T(8,128)(2,1)S(1)} %shard_map.56.own_ref), channel_id=1, source_target_pairs={{0,448},{1,449},{4,452},{5,453},{3,0},{2,1},{7,4},{6,5},{11,3},{10... | collective-permute-start | bytes 1769480 | tf_op jit(solution)/shard_map/ppermute | solution.py:193
  53.0 15.0 %collective-permute-start.3 = (bf16[256,1152]{1,0:T(8,128)(2,1)S(1)}, bf16[256,1152]{1,0:T(8,128)(2,1)S(1)}, u32[]{:S(2)}, u32[]{:S(2)}) collective-permute-start(bf16[256,1152]{1,0:T(8,128)(2,1)S(1)} %shard_map.56.own_ref), channel_id=1, source_target_pairs={{0,3},{1,2},{4,7},{5,6},{3,11},{2,10},{7,15},{6,14},{11,8},{10,9},... | collective-permute-start | bytes 1769480 | tf_op jit(solution)/shard_map/ppermute | solution.py:192
  56.9 11.1 %collective-permute-start.1 = (bf16[256,1152]{1,0:T(8,128)(2,1)S(1)}, bf16[256,1152]{1,0:T(8,128)(2,1)S(1)}, u32[]{:S(2)}, u32[]{:S(2)}) collective-permute-start(bf16[256,1152]{1,0:T(8,128)(2,1)S(1)} %shard_map.56.own_ref), channel_id=1, source_target_pairs={{0,4},{1,5},{4,0},{5,1},{3,7},{2,6},{7,3},{6,2},{11,15},{10,14},{1... | collective-permute-start | bytes 1769480 | tf_op jit(solution)/shard_map/ppermute | solution.py:194
  62.3 7.3 %collective-permute-start.2 = (bf16[256,1152]{1,0:T(8,128)(2,1)S(1)}, bf16[256,1152]{1,0:T(8,128)(2,1)S(1)}, u32[]{:S(2)}, u32[]{:S(2)}) collective-permute-start(bf16[256,1152]{1,0:T(8,128)(2,1)S(1)} %collective-permute-done.far_ref), channel_id=1, source_target_pairs={{0,4},{1,5},{4,0},{5,1},{3,7},{2,6},{7,3},{6,2},{11,15},{10,14},{1... | collective-permute-start | bytes 1769480 | tf_op jit(solution)/shard_map/ppermute | solution.py:195

commit v2 on v1

--- a/solution.py
+++ b/solution.py
@@ -11,8 +11,6 @@
 LOAD = 128
 D = 1024
 LANES = 128
-BLOCKS = D // LANES
-ROWS_MSG = 24
 WIDE = D + LANES
 QUART = 2 * OWNERS
 F32, BF16 = jnp.float32, jnp.bfloat16
@@ -58,7 +56,7 @@
     return jnp.where(mask, 1.0, 0.0).astype(BF16)
 
 
-def pack_kernel(x_ref, cl_ref, ord_ref, map_ref, nbr_ref, out_ref, place_ref, wide_ref):
+def pack_kernel(x_ref, cl_ref, ord_ref, map_ref, nbr_ref, out_ref, place_ref):
     clusters = cl_ref[...]
     orders = ord_ref[...]
     count = map_ref.shape[1]
@@ -85,30 +83,13 @@
     factor = lax.rsqrt(mean_square + 1e-06) * D ** (-0.5)
     unit = (scaled * factor).astype(BF16)
 
-    target = iota((OWNERS, LOAD), 0).astype(F32)
-    for k in range(2):
-        pick = ones_where((owner == target) & (rank == float(k)))
-        rows = jnp.dot(pick, unit, preferred_element_type=F32)
-        for b in range(BLOCKS):
-            at = pl.ds(k * BLOCKS + b, OWNERS, stride=ROWS_MSG)
-            wide_ref[at, :] = rows[:, b * LANES : (b + 1) * LANES]
-        wide_ref[pl.ds(2 * BLOCKS + k, OWNERS, stride=ROWS_MSG), :] = nt(pick, meta)
-    for j in range(2 * BLOCKS + 2, ROWS_MSG):
-        wide_ref[pl.ds(j, OWNERS, stride=ROWS_MSG), :] = jnp.zeros((OWNERS, LANES), F32)
-    out_ref[...] = wide_ref[...].astype(BF16)
+    slot = iota((QUART, LOAD), 0)
+    pick = (owner == (slot >> 1).astype(F32)) & (rank == (slot & 1).astype(F32))
+    pick = ones_where(pick)
+    out_ref[:, 0:D] = jnp.dot(pick, unit, preferred_element_type=F32).astype(BF16)
+    out_ref[:, D:WIDE] = nt(pick, meta).astype(BF16)
     row = iota((8, LOAD), 0)
     place_ref[...] = jnp.where(row == 0, owner, rank)
-
-
-def unpack_kernel(got_ref, out_ref, wide_ref):
-    wide_ref[...] = got_ref[...].astype(F32)
-    for k in range(2):
-        here = pl.ds(k * OWNERS, OWNERS)
-        for b in range(BLOCKS):
-            at = pl.ds(k * BLOCKS + b, OWNERS, stride=ROWS_MSG)
-            out_ref[here, pl.ds(b * LANES, LANES)] = wide_ref[at, :].astype(BF16)
-        at = pl.ds(2 * BLOCKS + k, OWNERS, stride=ROWS_MSG)
-        out_ref[here, pl.ds(D, LANES)] = wide_ref[at, :].astype(BF16)
 
 
 def key_meta(key_ref):
@@ -120,7 +101,7 @@
     return order, got[1:2, :]
 
 
-def score_kernel(own_ref, far_ref, core_ref, both_ref, low_ref, high_ref, out_ref):
+def score_kernel(own_ref, far_ref, core_ref, both_ref, low_ref, high_ref, out_ref, turn_ref):
     device = lax.axis_index("shard") * X + lax.axis_index("rep")
     x = device & 3
     quarter = ((device >> 2) & 1) * 2 + ((x >> 1) ^ (x & 1))
@@ -139,7 +120,9 @@
             scores = jnp.where(allowed, scores, -1.0)
             best = scores if best is None else jnp.maximum(best, scores)
         best = jnp.max(best, axis=1, keepdims=True)
-        pair = jnp.where(lane == 0, best[0:OWNERS, :], best[OWNERS:QUART, :])
+        turn_ref[...] = jnp.broadcast_to(best, (QUART, LANES))
+        even = turn_ref[pl.ds(0, OWNERS, stride=2), :]
+        pair = jnp.where(lane == 0, even, turn_ref[pl.ds(1, OWNERS, stride=2), :])
         out_ref[pl.ds(quarter ^ flip, OWNERS, stride=4), :] = pair
 
 
@@ -168,10 +151,8 @@
 
 
 def body(embeds, clusters, orders, owner_map, neighbours):
-    wire = OWNERS * ROWS_MSG
-    scratch = [pltpu.VMEM((wire, LANES), F32)]
     packed, place = call(
-        pack_kernel, [shape((wire, LANES), BF16), shape((8, LOAD), F32)], scratch, 10**8
+        pack_kernel, [shape((QUART, WIDE), BF16), shape((8, LOAD), F32)], (), 10**8
     )(
         embeds,
         clusters.reshape(1, LOAD),
@@ -180,20 +161,15 @@
         neighbours.T,
     )
     got = lax.all_to_all(
-        packed.reshape(OWNERS, ROWS_MSG, LANES),
-        AXES,
-        0,
-        0,
-        axis_index_groups=GROUPS,
-        tiled=True,
+        packed.reshape(OWNERS, 2, WIDE), AXES, 0, 0, axis_index_groups=GROUPS, tiled=True
     )
-    own = call(unpack_kernel, shape((QUART, WIDE), BF16), scratch)(got.reshape(wire, LANES))
+    own = got.reshape(QUART, WIDE)
     far = lax.ppermute(own, AXES, X_SWAP)
     low = lax.ppermute(own, AXES, UP)
     high = lax.ppermute(own, AXES, DOWN)
     core = lax.ppermute(own, AXES, C_SWAP)
     both = lax.ppermute(far, AXES, C_SWAP)
-    best = call(score_kernel, shape((4 * OWNERS, LANES), F32), (), 16 * 10**8)(
+    best = call(score_kernel, shape((4 * OWNERS, LANES), F32), [pltpu.VMEM((QUART, LANES), F32)], 16 * 10**8)(
         own, far, core, both, low, high
     )
     back = lax.all_to_all(

time: 103 us -> 98.8 us (0.959)
  blocking collectives: 76.1 us -> 71.5 us
    all_to_all x1, blocking collectives: 45.7 us -> 41.1 us  [body(): lax.all_to_all(packed.reshape(OWNERS, 2, WIDE), AXES, 0, 0, axis_index_gr...]
    pallas_call x3 -> x2, Pallas kernels: 3.45 us -> 2.98 us  [the longest x1 2.42 us: body(): call(score_kernel, shape((4 * OWNERS, LANES), F32), [pltpu.VMEM((QUART, L...]
where the time goes in v2:
time: 98.8 us; the launch traced here: 98.4 us
  blocking collectives  71.5 us (72%)
  starting transfers between devices  19.5 us (20%)
  Pallas kernels  3.61 us (4%)
  local copies, waits for them, and re-layouts  2.08 us (2%)
  waiting for transfers between devices  1.59 us (2%)
    all_to_all x1, blocking collectives, body(): lax.all_to_all(packed.reshape(OWNERS, 2, WIDE), AXES, 0, 0, axis_index_gr...  41.1 us
    all_to_all x1, blocking collectives, body(): lax.all_to_all(best.reshape(4 * OWNERS, 1, LANES), AXES, 0, 0, axis_index...  30.4 us
    ppermute x1, starting transfers between devices, body(): core = lax.ppermute(own, AXES, C_SWAP)  5.78 us
    ppermute x1, starting transfers between devices, body(): both = lax.ppermute(far, AXES, C_SWAP)  5.29 us
    ppermute x1, starting transfers between devices, body(): low = lax.ppermute(own, AXES, UP)  3.47 us
    ppermute x1, starting transfers between devices, body(): high = lax.ppermute(own, AXES, DOWN)  3.03 us
    pallas_call x1, Pallas kernels, body(): call(score_kernel, shape((4 * OWNERS, LANES), F32), [pltpu.VMEM((QUART, L...  2.42 us
  transfers between devices with their start and end apart: 5, of which 1 were waited for; matrix products, arithmetic and copies ran while one was open for 0% of the time, Pallas kernels for 0%

profile of v2, /device:TPU:1, one launch (start us, length us, event | category | flops | bytes accessed | tf_op | source)
XLA Modules:
  0.0 98.4 jit_solution(492986929558537194)
XLA Ops:
  0.0 0.0 copy-start.1
  0.0 0.0 copy-start.2
  0.0 0.0 copy-start.3
  0.0 0.0 copy-start.4
  0.0 0.7 copy-done.1
  0.7 0.0 copy-done.2
  0.7 0.0 copy-done.3
  0.7 0.0 copy-done.4
  0.7 0.0 copy-start
  0.7 0.9 copy-done
  1.7 0.6 shard_map.55
  2.2 0.2 reshape.27
  2.5 41.1 %all_to_all.10 = bf16[128,2,1152]{2,1,0:T(2,128)(2,1)S(1)} all-to-all(bf16[128,2,1152]{2,1,0:T(2,128)(2,1)S(1)} %reshape.27), channel_id=1, replica_groups={{0,3,11,8,16,19,27,24,32,35,43,40,48,51,59,56,120,123,115,112,104,107,9..., dimensions={0} | all-to-all | bytes 1179648 | tf_op jit(solution)/shard_map/all_to_all | solution.py:163
  43.6 0.2 reshape.28.own_ref
  43.8 1.9 %collective-permute-start = (bf16[256,1152]{1,0:T(8,128)(2,1)S(1)}, bf16[256,1152]{1,0:T(8,128)(2,1)S(1)}, u32[]{:S(2)}, u32[]{:S(2)}) collective-permute-start(bf16[256,1152]{1,0:T(8,128)(2,1)S(1)} %reshape.28.own_ref), channel_id=1, source_target_pairs={{0,1},{1,0},{4,5},{5,4},{3,2},{2,3},{7,6},{6,7},{11,10},{10,11},{1... | collective-permute-start | bytes 1769480 | tf_op jit(solution)/shard_map/ppermute | solution.py:167
  45.7 3.0 %collective-permute-start.4 = (bf16[256,1152]{1,0:T(8,128)(2,1)S(1)}, bf16[256,1152]{1,0:T(8,128)(2,1)S(1)}, u32[]{:S(2)}, u32[]{:S(2)}) collective-permute-start(bf16[256,1152]{1,0:T(8,128)(2,1)S(1)} %reshape.28.own_ref), channel_id=1, source_target_pairs={{0,448},{1,449},{4,452},{5,453},{3,0},{2,1},{7,4},{6,5},{11,3},{10... | collective-permute-start | bytes 1769480 | tf_op jit(solution)/shard_map/ppermute | solution.py:169
  48.8 3.5 %collective-permute-start.3 = (bf16[256,1152]{1,0:T(8,128)(2,1)S(1)}, bf16[256,1152]{1,0:T(8,128)(2,1)S(1)}, u32[]{:S(2)}, u32[]{:S(2)}) collective-permute-start(bf16[256,1152]{1,0:T(8,128)(2,1)S(1)} %reshape.28.own_ref), channel_id=1, source_target_pairs={{0,3},{1,2},{4,7},{5,6},{3,11},{2,10},{7,15},{6,14},{11,8},{10,9},... | collective-permute-start | bytes 1769480 | tf_op jit(solution)/shard_map/ppermute | solution.py:168
  52.2 5.8 %collective-permute-start.1 = (bf16[256,1152]{1,0:T(8,128)(2,1)S(1)}, bf16[256,1152]{1,0:T(8,128)(2,1)S(1)}, u32[]{:S(2)}, u32[]{:S(2)}) collective-permute-start(bf16[256,1152]{1,0:T(8,128)(2,1)S(1)} %reshape.28.own_ref), channel_id=1, source_target_pairs={{0,4},{1,5},{4,0},{5,1},{3,7},{2,6},{7,3},{6,2},{11,15},{10,14},{1... | collective-permute-start | bytes 1769480 | tf_op jit(solution)/shard_map/ppermute | solution.py:170
  58.0 0.0 collective-permute-done.far_ref
  58.0 5.3 %collective-permute-start.2 = (bf16[256,1152]{1,0:T(8,128)(2,1)S(1)}, bf16[256,1152]{1,0:T(8,128)(2,1)S(1)}, u32[]{:S(2)}, u32[]{:S(2)}) collective-permute-start(bf16[256,1152]{1,0:T(8,128)(2,1)S(1)} %collective-permute-done.far_ref), channel_id=1, source_target_pairs={{0,4},{1,5},{4,0},{5,1},{3,7},{2,6},{7,3},{6,2},{11,15},{10,14},{1... | collective-permute-start | bytes 1769480 | tf_op jit(solution)/shard_map/ppermute | solution.py:171
  63.3 0.0 collective-permute-done.4.high_ref
  63.4 0.0 collective-permute-done.3.low_ref
  63.4 0.0 collective-permute-done.1.core_ref
  63.4 1.6 %collective-permute-done.2.both_ref = bf16[256,1152]{1,0:T(8,128)(2,1)S(1)} collective-permute-done((bf16[256,1152]{1,0:T(8,128)(2,1)S(1)}, bf16[256,1152]{1,0:T(8,128)(2,1)S(1)}, u32[]{:S(2)}, u32[]{:S(2)}) %collective-permute-start.2) | collective-permute-done | bytes 589856 | tf_op jit(solution)/shard_map/ppermute | solution.py:171
  65.0 2.4 %shard_map.56 = f32[512,128]{1,0:T(8,128)S(1)} custom-call(bf16[256,1152]{1,0:T(8,128)(2,1)S(1)} %reshape.28.own_ref, bf16[256,1152]{1,0:T(8,128)(2,1)S(1)} %collective-permute-done.far_ref, bf16[256,1152]{1,0:T(8,128)(2,1)S(1)} %collective-permute-done.1.core_ref, bf16[256,1152]{1,0:T(8,128)(2,1)S(1)} %collective-permute-done.2.both_ref, ...), custom_call_target="tpu_custom_call" | custom-call | flops 1600000000 | bytes 1048576 | tf_op jit(solution)/shard_map/pallas_call | solution.py:172
  67.4 30.4 %all_to_all.11 = f32[512,1,128]{2,1,0:T(1,128)S(1)} all-to-all(f32[512,1,128]{2,1,0:T(1,128)S(1)} %bitcast.10), channel_id=1, replica_groups={{0,1,4,5,3,2,7,6,11,10,15,14,8,9,12,13,16,17,20,21,19,18,23,22,27,26,31..., dimensions={0} | all-to-all | bytes 524288 | tf_op jit(solution)/shard_map/all_to_all | solution.py:175
  97.8 0.6 shard_map.57
Async XLA Ops:
  0.0 0.7 copy-start.1
  0.0 0.7 copy-start.2
  0.0 0.7 copy-start.3
  0.0 0.7 copy-start.4
  0.7 1.0 copy-start
  43.8 14.2 %collective-permute-start = (bf16[256,1152]{1,0:T(8,128)(2,1)S(1)}, bf16[256,1152]{1,0:T(8,128)(2,1)S(1)}, u32[]{:S(2)}, u32[]{:S(2)}) collective-permute-start(bf16[256,1152]{1,0:T(8,128)(2,1)S(1)} %reshape.28.own_ref), channel_id=1, source_target_pairs={{0,1},{1,0},{4,5},{5,4},{3,2},{2,3},{7,6},{6,7},{11,10},{10,11},{1... | collective-permute-start | bytes 1769480 | tf_op jit(solution)/shard_map/ppermute | solution.py:167
  45.7 17.6 %collective-permute-start.4 = (bf16[256,1152]{1,0:T(8,128)(2,1)S(1)}, bf16[256,1152]{1,0:T(8,128)(2,1)S(1)}, u32[]{:S(2)}, u32[]{:S(2)}) collective-permute-start(bf16[256,1152]{1,0:T(8,128)(2,1)S(1)} %reshape.28.own_ref), channel_id=1, source_target_pairs={{0,448},{1,449},{4,452},{5,453},{3,0},{2,1},{7,4},{6,5},{11,3},{10... | collective-permute-start | bytes 1769480 | tf_op jit(solution)/shard_map/ppermute | solution.py:169
  48.8 14.6 %collective-permute-start.3 = (bf16[256,1152]{1,0:T(8,128)(2,1)S(1)}, bf16[256,1152]{1,0:T(8,128)(2,1)S(1)}, u32[]{:S(2)}, u32[]{:S(2)}) collective-permute-start(bf16[256,1152]{1,0:T(8,128)(2,1)S(1)} %reshape.28.own_ref), channel_id=1, source_target_pairs={{0,3},{1,2},{4,7},{5,6},{3,11},{2,10},{7,15},{6,14},{11,8},{10,9},... | collective-permute-start | bytes 1769480 | tf_op jit(solution)/shard_map/ppermute | solution.py:168
  52.2 11.1 %collective-permute-start.1 = (bf16[256,1152]{1,0:T(8,128)(2,1)S(1)}, bf16[256,1152]{1,0:T(8,128)(2,1)S(1)}, u32[]{:S(2)}, u32[]{:S(2)}) collective-permute-start(bf16[256,1152]{1,0:T(8,128)(2,1)S(1)} %reshape.28.own_ref), channel_id=1, source_target_pairs={{0,4},{1,5},{4,0},{5,1},{3,7},{2,6},{7,3},{6,2},{11,15},{10,14},{1... | collective-permute-start | bytes 1769480 | tf_op jit(solution)/shard_map/ppermute | solution.py:170
  58.0 6.9 %collective-permute-start.2 = (bf16[256,1152]{1,0:T(8,128)(2,1)S(1)}, bf16[256,1152]{1,0:T(8,128)(2,1)S(1)}, u32[]{:S(2)}, u32[]{:S(2)}) collective-permute-start(bf16[256,1152]{1,0:T(8,128)(2,1)S(1)} %collective-permute-done.far_ref), channel_id=1, source_target_pairs={{0,4},{1,5},{4,0},{5,1},{3,7},{2,6},{7,3},{6,2},{11,15},{10,14},{1... | collective-permute-start | bytes 1769480 | tf_op jit(solution)/shard_map/ppermute | solution.py:171

commit v3 on v2

--- a/solution.py
+++ b/solution.py
@@ -40,7 +40,6 @@
 
 X_SWAP = moves(0, 0, 1)
 C_SWAP = moves(0, 1, 0)
-UP = moves(1, 0, 0)
 DOWN = moves(-1, 0, 0)
 
 
@@ -98,31 +97,48 @@
     take = jnp.where(row < 4, take, jnp.where((row == 4) & (lane == 8), 1.0, 0.0))
     got = nt(take.astype(BF16), key_ref[:, D:WIDE])
     order = jnp.where(got[4:5, :] > 0.0, got[0:1, :], 1e9)
-    return order, got[1:2, :]
-
-
-def score_kernel(own_ref, far_ref, core_ref, both_ref, low_ref, high_ref, out_ref, turn_ref):
+    return order, got[1:2, :], got[2:3, :], got[3:4, :]
+
+
+def masked(scores, query, key):
+    order, cluster, first, second = query
+    related = (key[1] == cluster) | (key[1] == first) | (key[1] == second)
+    return jnp.where(related & (key[0] < order), scores, -1.0)
+
+
+def score_kernel(own_ref, far_ref, core_ref, both_ref, high_ref, out_ref, turn_ref, top_ref):
     device = lax.axis_index("shard") * X + lax.axis_index("rep")
     x = device & 3
     quarter = ((device >> 2) & 1) * 2 + ((x >> 1) ^ (x & 1))
-    keys = [(ref, *key_meta(ref)) for ref in (low_ref, own_ref, high_ref)]
+    own_key, high_key = key_meta(own_ref), key_meta(high_ref)
     lane = iota((OWNERS, LANES), 1)
-    for flip, query in enumerate((own_ref, far_ref, core_ref, both_ref)):
-        meta = query[:, D:WIDE].astype(F32)
+
+    def halves(ref):
+        return ref[pl.ds(0, OWNERS, stride=2), :], ref[pl.ds(1, OWNERS, stride=2), :]
+
+    upper = None
+    for flip, query in ((3, both_ref), (2, core_ref), (1, far_ref), (0, own_ref)):
+        digits = query[:, D:WIDE].astype(F32)
         order, cluster, first, second = (
-            meta[:, 2 * j : 2 * j + 1] * 256.0 + meta[:, 2 * j + 1 : 2 * j + 2] for j in range(4)
+            digits[:, 2 * j : 2 * j + 1] * 256.0 + digits[:, 2 * j + 1 : 2 * j + 2]
+            for j in range(4)
         )
-        best = None
-        for key, key_order, key_cluster in keys:
-            scores = nt(query[:, 0:D], key[:, 0:D])
-            related = (key_cluster == cluster) | (key_cluster == first) | (key_cluster == second)
-            allowed = related & (key_order < order)
-            scores = jnp.where(allowed, scores, -1.0)
-            best = scores if best is None else jnp.maximum(best, scores)
+        order = jnp.where(digits[:, 8:9] > 0.0, order, 1e9)
+        meta = (order, cluster, first, second)
+        rows = query[:, 0:D]
+        best = masked(nt(rows, own_ref[:, 0:D]), meta, own_key)
+        scores = nt(rows, high_ref[:, 0:D])
+        best = jnp.maximum(best, masked(scores, meta, high_key))
         best = jnp.max(best, axis=1, keepdims=True)
+        over = jnp.max(masked(scores, high_key, meta), axis=0, keepdims=True)
+        upper = over if upper is None else jnp.maximum(upper, over)
         turn_ref[...] = jnp.broadcast_to(best, (QUART, LANES))
-        even = turn_ref[pl.ds(0, OWNERS, stride=2), :]
-        pair = jnp.where(lane == 0, even, turn_ref[pl.ds(1, OWNERS, stride=2), :])
+        even, odd = halves(turn_ref)
+        pair = jnp.where(lane == 0, even, jnp.where(lane == 1, odd, -1.0))
+        if flip == 0:
+            top_ref[...] = jnp.broadcast_to(upper, (LANES, QUART)).T
+            even, odd = halves(top_ref)
+            pair = jnp.where(lane == 2, even, jnp.where(lane == 3, odd, pair))
         out_ref[pl.ds(quarter ^ flip, OWNERS, stride=4), :] = pair
 
 
@@ -132,7 +148,12 @@
         best = jnp.maximum(best, got_ref[pl.ds(q, OWNERS, stride=4), :])
     owner, rank = place_ref[0:1, :], place_ref[1:2, :]
     mine = owner == iota((OWNERS, LOAD), 0).astype(F32)
-    values = jnp.where(rank == 0.0, best[:, 0:1], best[:, 1:2])
+    lower = pltpu.roll(best, 1, 0)
+    values = jnp.where(
+        rank == 0.0,
+        jnp.maximum(best[:, 0:1], lower[:, 2:3]),
+        jnp.maximum(best[:, 1:2], lower[:, 3:4]),
+    )
     out_ref[...] = jnp.max(jnp.where(mine, values, -2.0), axis=0, keepdims=True)
 
 
@@ -165,12 +186,12 @@
     )
     own = got.reshape(QUART, WIDE)
     far = lax.ppermute(own, AXES, X_SWAP)
-    low = lax.ppermute(own, AXES, UP)
     high = lax.ppermute(own, AXES, DOWN)
     core = lax.ppermute(own, AXES, C_SWAP)
     both = lax.ppermute(far, AXES, C_SWAP)
-    best = call(score_kernel, shape((4 * OWNERS, LANES), F32), [pltpu.VMEM((QUART, LANES), F32)], 16 * 10**8)(
-        own, far, core, both, low, high
+    turn = [pltpu.VMEM((QUART, LANES), F32)] * 2
+    best = call(score_kernel, shape((4 * OWNERS, LANES), F32), turn, 11 * 10**8)(
+        own, far, core, both, high
     )
     back = lax.all_to_all(
         best.reshape(4 * OWNERS, 1, LANES), AXES, 0, 0, axis_index_groups=EVERY, tiled=True

time: 98.8 us -> 95.2 us (0.964)
  blocking collectives: 71.5 us -> 67.6 us
  starting transfers between devices: 19.5 us -> 16.6 us
  waiting for transfers between devices: 1.59 us -> 4.46 us
    all_to_all x1, blocking collectives: 30.4 us -> 26.5 us  [body(): lax.all_to_all(best.reshape(4 * OWNERS, 1, LANES), AXES, 0, 0, axis_index...]
    ppermute x1 -> x0, starting transfers between devices: 3.47 us -> none  [body(): low = lax.ppermute(own, AXES, UP)]
    ppermute x1, waiting for transfers between devices: 0.01 us -> 2.87 us  [body(): far = lax.ppermute(own, AXES, X_SWAP)]
  transfers between devices with their start and end apart: 5 -> 4, of which waited for: 1 -> 2; matrix products, arithmetic and copies ran while one was open for 0% -> 0% of each run, Pallas kernels for 0% -> 0%
where the time goes in v3:
time: 95.2 us; the launch traced here: 94.9 us
  blocking collectives  67.6 us (71%)
  starting transfers between devices  16.6 us (17%)
  waiting for transfers between devices  4.46 us (5%)
  Pallas kernels  3.97 us (4%)
  local copies, waits for them, and re-layouts  2.08 us (2%)
    all_to_all x1, blocking collectives, body(): lax.all_to_all(packed.reshape(OWNERS, 2, WIDE), AXES, 0, 0, axis_index_gr...  41.1 us
    all_to_all x1, blocking collectives, body(): lax.all_to_all(best.reshape(4 * OWNERS, 1, LANES), AXES, 0, 0, axis_index...  26.5 us
    ppermute x1, starting transfers between devices, body(): both = lax.ppermute(far, AXES, C_SWAP)  6.14 us
    ppermute x1, starting transfers between devices, body(): core = lax.ppermute(own, AXES, C_SWAP)  5.56 us
    ppermute x1, starting transfers between devices, body(): high = lax.ppermute(own, AXES, DOWN)  3.03 us
    ppermute x1, waiting for transfers between devices, body(): far = lax.ppermute(own, AXES, X_SWAP)  2.87 us
    pallas_call x1, Pallas kernels, body(): call(score_kernel, shape((4 * OWNERS, LANES), F32), turn, 11 * 10 ** 8)  2.7 us
    ppermute x1, starting transfers between devices, body(): far = lax.ppermute(own, AXES, X_SWAP)  1.92 us
  transfers between devices with their start and end apart: 4, of which 2 were waited for; matrix products, arithmetic and copies ran while one was open for 0% of the time, Pallas kernels for 0%

profile of v3, /device:TPU:1, one launch (start us, length us, event | category | flops | bytes accessed | tf_op | source)
XLA Modules:
  0.0 94.9 jit_solution(16305957489799470997)
XLA Ops:
  0.0 0.0 copy-start.1
  0.0 0.0 copy-start.2
  0.0 0.0 copy-start.3
  0.0 0.0 copy-start.4
  0.0 0.7 copy-done.1
  0.7 0.0 copy-done.2
  0.7 0.0 copy-done.3
  0.7 0.0 copy-done.4
  0.7 0.0 copy-start
  0.7 0.9 %copy-done = bf16[128,1024]{1,0:T(8,128)(2,1)S(1)} copy-done((bf16[128,1024]{1,0:T(8,128)(2,1)S(1)}, bf16[128,1024]{1,0:T(8,128)(2,1)}, u32[]{:S(2)}) %copy-start) | copy-done | bytes 262168
  1.7 0.6 shard_map.55
  2.2 0.2 reshape.27
  2.5 41.1 %all_to_all.10 = bf16[128,2,1152]{2,1,0:T(2,128)(2,1)S(1)} all-to-all(bf16[128,2,1152]{2,1,0:T(2,128)(2,1)S(1)} %reshape.27), channel_id=1, replica_groups={{0,3,11,8,16,19,27,24,32,35,43,40,48,51,59,56,120,123,115,112,104,107,9..., dimensions={0} | all-to-all | bytes 1179648 | tf_op jit(solution)/shard_map/all_to_all | solution.py:184
  43.6 0.2 reshape.28.own_ref
  43.8 1.9 %collective-permute-start = (bf16[256,1152]{1,0:T(8,128)(2,1)S(1)}, bf16[256,1152]{1,0:T(8,128)(2,1)S(1)}, u32[]{:S(2)}, u32[]{:S(2)}) collective-permute-start(bf16[256,1152]{1,0:T(8,128)(2,1)S(1)} %reshape.28.own_ref), channel_id=1, source_target_pairs={{0,1},{1,0},{4,5},{5,4},{3,2},{2,3},{7,6},{6,7},{11,10},{10,11},{1... | collective-permute-start | bytes 1769480 | tf_op jit(solution)/shard_map/ppermute | solution.py:188
  45.7 3.0 %collective-permute-start.3 = (bf16[256,1152]{1,0:T(8,128)(2,1)S(1)}, bf16[256,1152]{1,0:T(8,128)(2,1)S(1)}, u32[]{:S(2)}, u32[]{:S(2)}) collective-permute-start(bf16[256,1152]{1,0:T(8,128)(2,1)S(1)} %reshape.28.own_ref), channel_id=1, source_target_pairs={{0,448},{1,449},{4,452},{5,453},{3,0},{2,1},{7,4},{6,5},{11,3},{10... | collective-permute-start | bytes 1769480 | tf_op jit(solution)/shard_map/ppermute | solution.py:189
  48.8 5.6 %collective-permute-start.1 = (bf16[256,1152]{1,0:T(8,128)(2,1)S(1)}, bf16[256,1152]{1,0:T(8,128)(2,1)S(1)}, u32[]{:S(2)}, u32[]{:S(2)}) collective-permute-start(bf16[256,1152]{1,0:T(8,128)(2,1)S(1)} %reshape.28.own_ref), channel_id=1, source_target_pairs={{0,4},{1,5},{4,0},{5,1},{3,7},{2,6},{7,3},{6,2},{11,15},{10,14},{1... | collective-permute-start | bytes 1769480 | tf_op jit(solution)/shard_map/ppermute | solution.py:190
  54.3 2.9 %collective-permute-done.far_ref = bf16[256,1152]{1,0:T(8,128)(2,1)S(1)} collective-permute-done((bf16[256,1152]{1,0:T(8,128)(2,1)S(1)}, bf16[256,1152]{1,0:T(8,128)(2,1)S(1)}, u32[]{:S(2)}, u32[]{:S(2)}) %collective-permute-start) | collective-permute-done | bytes 589856 | tf_op jit(solution)/shard_map/ppermute | solution.py:188
  57.2 6.1 %collective-permute-start.2 = (bf16[256,1152]{1,0:T(8,128)(2,1)S(1)}, bf16[256,1152]{1,0:T(8,128)(2,1)S(1)}, u32[]{:S(2)}, u32[]{:S(2)}) collective-permute-start(bf16[256,1152]{1,0:T(8,128)(2,1)S(1)} %collective-permute-done.far_ref), channel_id=1, source_target_pairs={{0,4},{1,5},{4,0},{5,1},{3,7},{2,6},{7,3},{6,2},{11,15},{10,14},{1... | collective-permute-start | bytes 1769480 | tf_op jit(solution)/shard_map/ppermute | solution.py:191
  63.3 0.0 collective-permute-done.3.high_ref
  63.4 0.0 collective-permute-done.1.core_ref
  63.4 1.6 %collective-permute-done.2.both_ref = bf16[256,1152]{1,0:T(8,128)(2,1)S(1)} collective-permute-done((bf16[256,1152]{1,0:T(8,128)(2,1)S(1)}, bf16[256,1152]{1,0:T(8,128)(2,1)S(1)}, u32[]{:S(2)}, u32[]{:S(2)}) %collective-permute-start.2) | collective-permute-done | bytes 589856 | tf_op jit(solution)/shard_map/ppermute | solution.py:191
  65.0 2.7 %shard_map.56 = f32[512,128]{1,0:T(8,128)S(1)} custom-call(bf16[256,1152]{1,0:T(8,128)(2,1)S(1)} %reshape.28.own_ref, bf16[256,1152]{1,0:T(8,128)(2,1)S(1)} %collective-permute-done.far_ref, bf16[256,1152]{1,0:T(8,128)(2,1)S(1)} %collective-permute-done.1.core_ref, bf16[256,1152]{1,0:T(8,128)(2,1)S(1)} %collective-permute-done.2.both_ref, ...), custom_call_target="tpu_custom_call" | custom-call | flops 1100000000 | bytes 1048576 | tf_op jit(solution)/shard_map/pallas_call | solution.py:193
  67.7 26.5 %all_to_all.11 = f32[512,1,128]{2,1,0:T(1,128)S(1)} all-to-all(f32[512,1,128]{2,1,0:T(1,128)S(1)} %bitcast.10), channel_id=1, replica_groups={{0,1,4,5,3,2,7,6,11,10,15,14,8,9,12,13,16,17,20,21,19,18,23,22,27,26,31..., dimensions={0} | all-to-all | bytes 524288 | tf_op jit(solution)/shard_map/all_to_all | solution.py:196
  94.2 0.7 shard_map.57
Async XLA Ops:
  0.0 0.7 copy-start.1
  0.0 0.7 copy-start.2
  0.0 0.7 copy-start.3
  0.0 0.7 copy-start.4
  0.7 1.0 %copy-start = (bf16[128,1024]{1,0:T(8,128)(2,1)S(1)}, bf16[128,1024]{1,0:T(8,128)(2,1)}, u32[]{:S(2)}) copy-start(bf16[128,1024]{1,0:T(8,128)(2,1)} %x_ref.1) | copy-start | bytes 786436
  43.8 13.4 %collective-permute-start = (bf16[256,1152]{1,0:T(8,128)(2,1)S(1)}, bf16[256,1152]{1,0:T(8,128)(2,1)S(1)}, u32[]{:S(2)}, u32[]{:S(2)}) collective-permute-start(bf16[256,1152]{1,0:T(8,128)(2,1)S(1)} %reshape.28.own_ref), channel_id=1, source_target_pairs={{0,1},{1,0},{4,5},{5,4},{3,2},{2,3},{7,6},{6,7},{11,10},{10,11},{1... | collective-permute-start | bytes 1769480 | tf_op jit(solution)/shard_map/ppermute | solution.py:188
  45.7 17.6 %collective-permute-start.3 = (bf16[256,1152]{1,0:T(8,128)(2,1)S(1)}, bf16[256,1152]{1,0:T(8,128)(2,1)S(1)}, u32[]{:S(2)}, u32[]{:S(2)}) collective-permute-start(bf16[256,1152]{1,0:T(8,128)(2,1)S(1)} %reshape.28.own_ref), channel_id=1, source_target_pairs={{0,448},{1,449},{4,452},{5,453},{3,0},{2,1},{7,4},{6,5},{11,3},{10... | collective-permute-start | bytes 1769480 | tf_op jit(solution)/shard_map/ppermute | solution.py:189
  48.8 14.6 %collective-permute-start.1 = (bf16[256,1152]{1,0:T(8,128)(2,1)S(1)}, bf16[256,1152]{1,0:T(8,128)(2,1)S(1)}, u32[]{:S(2)}, u32[]{:S(2)}) collective-permute-start(bf16[256,1152]{1,0:T(8,128)(2,1)S(1)} %reshape.28.own_ref), channel_id=1, source_target_pairs={{0,4},{1,5},{4,0},{5,1},{3,7},{2,6},{7,3},{6,2},{11,15},{10,14},{1... | collective-permute-start | bytes 1769480 | tf_op jit(solution)/shard_map/ppermute | solution.py:190
  57.2 7.8 %collective-permute-start.2 = (bf16[256,1152]{1,0:T(8,128)(2,1)S(1)}, bf16[256,1152]{1,0:T(8,128)(2,1)S(1)}, u32[]{:S(2)}, u32[]{:S(2)}) collective-permute-start(bf16[256,1152]{1,0:T(8,128)(2,1)S(1)} %collective-permute-done.far_ref), channel_id=1, source_target_pairs={{0,4},{1,5},{4,0},{5,1},{3,7},{2,6},{7,3},{6,2},{11,15},{10,14},{1... | collective-permute-start | bytes 1769480 | tf_op jit(solution)/shard_map/ppermute | solution.py:191

commit v4 on v3

--- a/solution.py
+++ b/solution.py
@@ -106,40 +106,63 @@
     return jnp.where(related & (key[0] < order), scores, -1.0)
 
 
-def score_kernel(own_ref, far_ref, core_ref, both_ref, high_ref, out_ref, turn_ref, top_ref):
+def my_quarter():
     device = lax.axis_index("shard") * X + lax.axis_index("rep")
     x = device & 3
-    quarter = ((device >> 2) & 1) * 2 + ((x >> 1) ^ (x & 1))
+    return ((device >> 2) & 1) * 2 + ((x >> 1) ^ (x & 1))
+
+
+def halves(ref):
+    return ref[pl.ds(0, OWNERS, stride=2), :], ref[pl.ds(1, OWNERS, stride=2), :]
+
+
+def score_part(query, own_ref, own_key, high_ref, high_key, turn_ref):
+    digits = query[:, D:WIDE].astype(F32)
+    order, cluster, first, second = (
+        digits[:, 2 * j : 2 * j + 1] * 256.0 + digits[:, 2 * j + 1 : 2 * j + 2] for j in range(4)
+    )
+    order = jnp.where(digits[:, 8:9] > 0.0, order, 1e9)
+    meta = (order, cluster, first, second)
+    rows = query[:, 0:D]
+    best = masked(nt(rows, own_ref[:, 0:D]), meta, own_key)
+    scores = nt(rows, high_ref[:, 0:D])
+    best = jnp.maximum(best, masked(scores, meta, high_key))
+    best = jnp.max(best, axis=1, keepdims=True)
+    upper = jnp.max(masked(scores, high_key, meta), axis=0, keepdims=True)
+    turn_ref[...] = jnp.broadcast_to(best, (QUART, LANES))
+    even, odd = halves(turn_ref)
+    lane = iota((OWNERS, LANES), 1)
+    return jnp.where(lane == 0, even, jnp.where(lane == 1, odd, -1.0)), upper
+
+
+def early_kernel(own_ref, far_ref, core_ref, high_ref, out_ref, upper_ref, turn_ref):
     own_key, high_key = key_meta(own_ref), key_meta(high_ref)
+    upper = None
+    for flip, query in enumerate((own_ref, far_ref, core_ref)):
+        pair, over = score_part(query, own_ref, own_key, high_ref, high_key, turn_ref)
+        out_ref[pl.ds(flip * OWNERS, OWNERS), :] = pair
+        upper = over if upper is None else jnp.maximum(upper, over)
+    upper_ref[...] = jnp.broadcast_to(upper, (8, QUART))
+
+
+def late_kernel(
+    own_ref, both_ref, high_ref, early_ref, upper_ref, out_ref, turn_ref, top_ref
+):
+    quarter = my_quarter()
+    own_key, high_key = key_meta(own_ref), key_meta(high_ref)
+    pair, upper = score_part(both_ref, own_ref, own_key, high_ref, high_key, turn_ref)
+    out_ref[pl.ds(quarter ^ 3, OWNERS, stride=4), :] = pair
+    for flip in (1, 2):
+        out_ref[pl.ds(quarter ^ flip, OWNERS, stride=4), :] = early_ref[
+            pl.ds(flip * OWNERS, OWNERS), :
+        ]
+    upper = jnp.maximum(upper, upper_ref[0:1, :])
+    top_ref[...] = jnp.broadcast_to(upper, (LANES, QUART)).T
+    even, odd = halves(top_ref)
     lane = iota((OWNERS, LANES), 1)
-
-    def halves(ref):
-        return ref[pl.ds(0, OWNERS, stride=2), :], ref[pl.ds(1, OWNERS, stride=2), :]
-
-    upper = None
-    for flip, query in ((3, both_ref), (2, core_ref), (1, far_ref), (0, own_ref)):
-        digits = query[:, D:WIDE].astype(F32)
-        order, cluster, first, second = (
-            digits[:, 2 * j : 2 * j + 1] * 256.0 + digits[:, 2 * j + 1 : 2 * j + 2]
-            for j in range(4)
-        )
-        order = jnp.where(digits[:, 8:9] > 0.0, order, 1e9)
-        meta = (order, cluster, first, second)
-        rows = query[:, 0:D]
-        best = masked(nt(rows, own_ref[:, 0:D]), meta, own_key)
-        scores = nt(rows, high_ref[:, 0:D])
-        best = jnp.maximum(best, masked(scores, meta, high_key))
-        best = jnp.max(best, axis=1, keepdims=True)
-        over = jnp.max(masked(scores, high_key, meta), axis=0, keepdims=True)
-        upper = over if upper is None else jnp.maximum(upper, over)
-        turn_ref[...] = jnp.broadcast_to(best, (QUART, LANES))
-        even, odd = halves(turn_ref)
-        pair = jnp.where(lane == 0, even, jnp.where(lane == 1, odd, -1.0))
-        if flip == 0:
-            top_ref[...] = jnp.broadcast_to(upper, (LANES, QUART)).T
-            even, odd = halves(top_ref)
-            pair = jnp.where(lane == 2, even, jnp.where(lane == 3, odd, pair))
-        out_ref[pl.ds(quarter ^ flip, OWNERS, stride=4), :] = pair
+    pair = early_ref[pl.ds(0, OWNERS), :]
+    pair = jnp.where(lane == 2, even, jnp.where(lane == 3, odd, pair))
+    out_ref[pl.ds(quarter, OWNERS, stride=4), :] = pair
 
 
 def pick_kernel(got_ref, place_ref, out_ref):
@@ -190,8 +213,14 @@
     core = lax.ppermute(own, AXES, C_SWAP)
     both = lax.ppermute(far, AXES, C_SWAP)
     turn = [pltpu.VMEM((QUART, LANES), F32)] * 2
-    best = call(score_kernel, shape((4 * OWNERS, LANES), F32), turn, 11 * 10**8)(
-        own, far, core, both, high
+    early, upper = call(
+        early_kernel,
+        [shape((3 * OWNERS, LANES), F32), shape((8, QUART), F32)],
+        turn[:1],
+        8 * 10**8,
+    )(own, far, core, high)
+    best = call(late_kernel, shape((4 * OWNERS, LANES), F32), turn, 3 * 10**8)(
+        own, both, high, early, upper
     )
     back = lax.all_to_all(
         best.reshape(4 * OWNERS, 1, LANES), AXES, 0, 0, axis_index_groups=EVERY, tiled=True

time: 95.2 us -> 99.7 us (1.047)
  waiting for transfers between devices: 4.46 us -> 8.81 us
    ppermute x1, waiting for transfers between devices: 0.01 us -> 5.66 us  [body(): high = lax.ppermute(own, AXES, DOWN)]
    ppermute x1, waiting for transfers between devices: 1.59 us -> 0.01 us  [body(): both = lax.ppermute(far, AXES, C_SWAP)]
    pallas_call x1 -> x2, Pallas kernels: 2.7 us -> 2.76 us  [the longest x1 1.87 us: body(): call(early_kernel, [shape((3 * OWNERS, LANES), F32), shape((8, QUART), F3...]
  transfers between devices with their start and end apart: 4 -> 4, of which waited for: 2 -> 2; matrix products, arithmetic and copies ran while one was open for 0% -> 0% of each run, Pallas kernels for 0% -> 2%
where the time goes in v4:
time: 99.7 us; the launch traced here: 99.4 us
  blocking collectives  68 us (68%)
  starting transfers between devices  16.4 us (16%)
  waiting for transfers between devices  8.81 us (9%)
  Pallas kernels  4.03 us (4%)
  local copies, waits for them, and re-layouts  2.08 us (2%)
    all_to_all x1, blocking collectives, body(): lax.all_to_all(packed.reshape(OWNERS, 2, WIDE), AXES, 0, 0, axis_index_gr...  41.1 us
    all_to_all x1, blocking collectives, body(): lax.all_to_all(best.reshape(4 * OWNERS, 1, LANES), AXES, 0, 0, axis_index...  26.9 us
    ppermute x1, starting transfers between devices, body(): both = lax.ppermute(far, AXES, C_SWAP)  6.14 us
    ppermute x1, waiting for transfers between devices, body(): high = lax.ppermute(own, AXES, DOWN)  5.66 us
    ppermute x1, starting transfers between devices, body(): core = lax.ppermute(own, AXES, C_SWAP)  5.22 us
    ppermute x1, waiting for transfers between devices, body(): far = lax.ppermute(own, AXES, X_SWAP)  3.15 us
    ppermute x1, starting transfers between devices, body(): high = lax.ppermute(own, AXES, DOWN)  3.08 us
  transfers between devices with their start and end apart: 4, of which 2 were waited for; matrix products, arithmetic and copies ran while one was open for 0% of the time, Pallas kernels for 2%

profile of v4, /device:TPU:1, one launch (start us, length us, event | category | flops | bytes accessed | tf_op | source)
XLA Modules:
  0.0 99.4 jit_solution(493933257796080381)
XLA Ops:
  0.0 0.0 copy-start.1
  0.0 0.0 copy-start.2
  0.0 0.0 copy-start.3
  0.0 0.0 copy-start.4
  0.0 0.7 copy-done.1
  0.7 0.0 copy-done.2
  0.7 0.0 copy-done.3
  0.7 0.0 copy-done.4
  0.7 0.0 copy-start
  0.7 0.9 copy-done
  1.7 0.6 shard_map.55
  2.2 0.2 reshape.27
  2.5 41.1 %all_to_all.10 = bf16[128,2,1152]{2,1,0:T(2,128)(2,1)S(1)} all-to-all(bf16[128,2,1152]{2,1,0:T(2,128)(2,1)S(1)} %reshape.27), channel_id=1, replica_groups={{0,3,11,8,16,19,27,24,32,35,43,40,48,51,59,56,120,123,115,112,104,107,9..., dimensions={0} | all-to-all | bytes 1179648 | tf_op jit(solution)/shard_map/all_to_all | solution.py:207
  43.6 0.2 reshape.28.own_ref
  43.8 1.9 %collective-permute-start = (bf16[256,1152]{1,0:T(8,128)(2,1)S(1)}, bf16[256,1152]{1,0:T(8,128)(2,1)S(1)}, u32[]{:S(2)}, u32[]{:S(2)}) collective-permute-start(bf16[256,1152]{1,0:T(8,128)(2,1)S(1)} %reshape.28.own_ref), channel_id=1, source_target_pairs={{0,1},{1,0},{4,5},{5,4},{3,2},{2,3},{7,6},{6,7},{11,10},{10,11},{1... | collective-permute-start | bytes 1769480 | tf_op jit(solution)/shard_map/ppermute | solution.py:211
  45.7 5.2 %collective-permute-start.3 = (bf16[256,1152]{1,0:T(8,128)(2,1)S(1)}, bf16[256,1152]{1,0:T(8,128)(2,1)S(1)}, u32[]{:S(2)}, u32[]{:S(2)}) collective-permute-start(bf16[256,1152]{1,0:T(8,128)(2,1)S(1)} %reshape.28.own_ref), channel_id=1, source_target_pairs={{0,4},{1,5},{4,0},{5,1},{3,7},{2,6},{7,3},{6,2},{11,15},{10,14},{1... | collective-permute-start | bytes 1769480 | tf_op jit(solution)/shard_map/ppermute | solution.py:213
  51.0 3.1 %collective-permute-start.2 = (bf16[256,1152]{1,0:T(8,128)(2,1)S(1)}, bf16[256,1152]{1,0:T(8,128)(2,1)S(1)}, u32[]{:S(2)}, u32[]{:S(2)}) collective-permute-start(bf16[256,1152]{1,0:T(8,128)(2,1)S(1)} %reshape.28.own_ref), channel_id=1, source_target_pairs={{0,448},{1,449},{4,452},{5,453},{3,0},{2,1},{7,4},{6,5},{11,3},{10... | collective-permute-start | bytes 1769480 | tf_op jit(solution)/shard_map/ppermute | solution.py:212
  54.1 3.1 %collective-permute-done.far_ref = bf16[256,1152]{1,0:T(8,128)(2,1)S(1)} collective-permute-done((bf16[256,1152]{1,0:T(8,128)(2,1)S(1)}, bf16[256,1152]{1,0:T(8,128)(2,1)S(1)}, u32[]{:S(2)}, u32[]{:S(2)}) %collective-permute-start) | collective-permute-done | bytes 589856 | tf_op jit(solution)/shard_map/ppermute | solution.py:211
  57.2 6.1 %collective-permute-start.1 = (bf16[256,1152]{1,0:T(8,128)(2,1)S(1)}, bf16[256,1152]{1,0:T(8,128)(2,1)S(1)}, u32[]{:S(2)}, u32[]{:S(2)}) collective-permute-start(bf16[256,1152]{1,0:T(8,128)(2,1)S(1)} %collective-permute-done.far_ref), channel_id=1, source_target_pairs={{0,4},{1,5},{4,0},{5,1},{3,7},{2,6},{7,3},{6,2},{11,15},{10,14},{1... | collective-permute-start | bytes 1769480 | tf_op jit(solution)/shard_map/ppermute | solution.py:214
  63.3 0.0 collective-permute-done.3.core_ref
  63.4 5.7 %collective-permute-done.2.high_ref = bf16[256,1152]{1,0:T(8,128)(2,1)S(1)} collective-permute-done((bf16[256,1152]{1,0:T(8,128)(2,1)S(1)}, bf16[256,1152]{1,0:T(8,128)(2,1)S(1)}, u32[]{:S(2)}, u32[]{:S(2)}) %collective-permute-start.2) | collective-permute-done | bytes 589856 | tf_op jit(solution)/shard_map/ppermute | solution.py:212
  69.0 1.9 %shard_map.56 = (f32[384,128]{1,0:T(8,128)S(1)}, f32[8,256]{1,0:T(8,128)S(1)}) custom-call(bf16[256,1152]{1,0:T(8,128)(2,1)S(1)} %reshape.28.own_ref, bf16[256,1152]{1,0:T(8,128)(2,1)S(1)} %collective-permute-done.far_ref, bf16[256,1152]{1,0:T(8,128)(2,1)S(1)} %collective-permute-done.3.core_ref, bf16[256,1152]{1,0:T(8,128)(2,1)S(1)} %collective-permute-done.2.high_ref), custom_call_target="tpu_custom_call" | custom-call | flops 800000000 | bytes 1048576 | tf_op jit(solution)/shard_map/pallas_call | solution.py:216
  70.9 0.0 collective-permute-done.1.both_ref
  70.9 0.9 shard_map.57
  71.8 26.9 %all_to_all.11 = f32[512,1,128]{2,1,0:T(1,128)S(1)} all-to-all(f32[512,1,128]{2,1,0:T(1,128)S(1)} %bitcast.9), channel_id=1, replica_groups={{0,1,4,5,3,2,7,6,11,10,15,14,8,9,12,13,16,17,20,21,19,18,23,22,27,26,31..., dimensions={0} | all-to-all | bytes 524288 | tf_op jit(solution)/shard_map/all_to_all | solution.py:225
  98.7 0.7 shard_map.58
Async XLA Ops:
  0.0 0.7 copy-start.1
  0.0 0.7 copy-start.2
  0.0 0.7 copy-start.3
  0.0 0.7 copy-start.4
  0.7 1.0 copy-start
  43.8 13.4 %collective-permute-start = (bf16[256,1152]{1,0:T(8,128)(2,1)S(1)}, bf16[256,1152]{1,0:T(8,128)(2,1)S(1)}, u32[]{:S(2)}, u32[]{:S(2)}) collective-permute-start(bf16[256,1152]{1,0:T(8,128)(2,1)S(1)} %reshape.28.own_ref), channel_id=1, source_target_pairs={{0,1},{1,0},{4,5},{5,4},{3,2},{2,3},{7,6},{6,7},{11,10},{10,11},{1... | collective-permute-start | bytes 1769480 | tf_op jit(solution)/shard_map/ppermute | solution.py:211
  45.7 17.6 %collective-permute-start.3 = (bf16[256,1152]{1,0:T(8,128)(2,1)S(1)}, bf16[256,1152]{1,0:T(8,128)(2,1)S(1)}, u32[]{:S(2)}, u32[]{:S(2)}) collective-permute-start(bf16[256,1152]{1,0:T(8,128)(2,1)S(1)} %reshape.28.own_ref), channel_id=1, source_target_pairs={{0,4},{1,5},{4,0},{5,1},{3,7},{2,6},{7,3},{6,2},{11,15},{10,14},{1... | collective-permute-start | bytes 1769480 | tf_op jit(solution)/shard_map/ppermute | solution.py:213
  51.0 18.1 %collective-permute-start.2 = (bf16[256,1152]{1,0:T(8,128)(2,1)S(1)}, bf16[256,1152]{1,0:T(8,128)(2,1)S(1)}, u32[]{:S(2)}, u32[]{:S(2)}) collective-permute-start(bf16[256,1152]{1,0:T(8,128)(2,1)S(1)} %reshape.28.own_ref), channel_id=1, source_target_pairs={{0,448},{1,449},{4,452},{5,453},{3,0},{2,1},{7,4},{6,5},{11,3},{10... | collective-permute-start | bytes 1769480 | tf_op jit(solution)/shard_map/ppermute | solution.py:212
  57.2 13.7 %collective-permute-start.1 = (bf16[256,1152]{1,0:T(8,128)(2,1)S(1)}, bf16[256,1152]{1,0:T(8,128)(2,1)S(1)}, u32[]{:S(2)}, u32[]{:S(2)}) collective-permute-start(bf16[256,1152]{1,0:T(8,128)(2,1)S(1)} %collective-permute-done.far_ref), channel_id=1, source_target_pairs={{0,4},{1,5},{4,0},{5,1},{3,7},{2,6},{7,3},{6,2},{11,15},{10,14},{1... | collective-permute-start | bytes 1769480 | tf_op jit(solution)/shard_map/ppermute | solution.py:214

commit v5 on v4

--- a/solution.py
+++ b/solution.py
@@ -135,10 +135,10 @@
     return jnp.where(lane == 0, even, jnp.where(lane == 1, odd, -1.0)), upper
 
 
-def early_kernel(own_ref, far_ref, core_ref, high_ref, out_ref, upper_ref, turn_ref):
+def early_kernel(own_ref, far_ref, high_ref, out_ref, upper_ref, turn_ref):
     own_key, high_key = key_meta(own_ref), key_meta(high_ref)
     upper = None
-    for flip, query in enumerate((own_ref, far_ref, core_ref)):
+    for flip, query in enumerate((own_ref, far_ref)):
         pair, over = score_part(query, own_ref, own_key, high_ref, high_key, turn_ref)
         out_ref[pl.ds(flip * OWNERS, OWNERS), :] = pair
         upper = over if upper is None else jnp.maximum(upper, over)
@@ -146,17 +146,17 @@
 
 
 def late_kernel(
-    own_ref, both_ref, high_ref, early_ref, upper_ref, out_ref, turn_ref, top_ref
+    own_ref, core_ref, both_ref, high_ref, early_ref, upper_ref, out_ref, turn_ref, top_ref
 ):
     quarter = my_quarter()
     own_key, high_key = key_meta(own_ref), key_meta(high_ref)
-    pair, upper = score_part(both_ref, own_ref, own_key, high_ref, high_key, turn_ref)
-    out_ref[pl.ds(quarter ^ 3, OWNERS, stride=4), :] = pair
-    for flip in (1, 2):
-        out_ref[pl.ds(quarter ^ flip, OWNERS, stride=4), :] = early_ref[
-            pl.ds(flip * OWNERS, OWNERS), :
-        ]
-    upper = jnp.maximum(upper, upper_ref[0:1, :])
+    upper = upper_ref[0:1, :]
+    for flip, query in ((2, core_ref), (3, both_ref)):
+        pair, over = score_part(query, own_ref, own_key, high_ref, high_key, turn_ref)
+        out_ref[pl.ds(quarter ^ flip, OWNERS, stride=4), :] = pair
+        upper = jnp.maximum(upper, over)
+    pair = early_ref[pl.ds(OWNERS, OWNERS), :]
+    out_ref[pl.ds(quarter ^ 1, OWNERS, stride=4), :] = pair
     top_ref[...] = jnp.broadcast_to(upper, (LANES, QUART)).T
     even, odd = halves(top_ref)
     lane = iota((OWNERS, LANES), 1)
@@ -215,12 +215,12 @@
     turn = [pltpu.VMEM((QUART, LANES), F32)] * 2
     early, upper = call(
         early_kernel,
-        [shape((3 * OWNERS, LANES), F32), shape((8, QUART), F32)],
+        [shape((2 * OWNERS, LANES), F32), shape((8, QUART), F32)],
         turn[:1],
-        8 * 10**8,
-    )(own, far, core, high)
-    best = call(late_kernel, shape((4 * OWNERS, LANES), F32), turn, 3 * 10**8)(
-        own, both, high, early, upper
+        6 * 10**8,
+    )(own, far, high)
+    best = call(late_kernel, shape((4 * OWNERS, LANES), F32), turn, 6 * 10**8)(
+        own, core, both, high, early, upper
     )
     back = lax.all_to_all(
         best.reshape(4 * OWNERS, 1, LANES), AXES, 0, 0, axis_index_groups=EVERY, tiled=True

time: 99.7 us -> 94.5 us (0.948)
  waiting for transfers between devices: 8.81 us -> 3.32 us
    ppermute x1, waiting for transfers between devices: 5.66 us -> 0.01 us  [body(): high = lax.ppermute(own, AXES, DOWN)]
  transfers between devices with their start and end apart: 4 -> 4, of which waited for: 2 -> 2; matrix products, arithmetic and copies ran while one was open for 0% -> 0% of each run, Pallas kernels for 2% -> 1%
where the time goes in v5:
time: 94.5 us; the launch traced here: 94.2 us
  blocking collectives  68.4 us (72%)
  starting transfers between devices  16.6 us (18%)
  Pallas kernels  3.63 us (4%)
  waiting for transfers between devices  3.32 us (4%)
  local copies, waits for them, and re-layouts  2.08 us (2%)
    all_to_all x1, blocking collectives, body(): lax.all_to_all(packed.reshape(OWNERS, 2, WIDE), AXES, 0, 0, axis_index_gr...  41.1 us
    all_to_all x1, blocking collectives, body(): lax.all_to_all(best.reshape(4 * OWNERS, 1, LANES), AXES, 0, 0, axis_index...  27.3 us
    ppermute x1, starting transfers between devices, body(): both = lax.ppermute(far, AXES, C_SWAP)  6.14 us
    ppermute x1, starting transfers between devices, body(): core = lax.ppermute(own, AXES, C_SWAP)  5.56 us
    ppermute x1, starting transfers between devices, body(): high = lax.ppermute(own, AXES, DOWN)  3.03 us
    ppermute x1, waiting for transfers between devices, body(): far = lax.ppermute(own, AXES, X_SWAP)  2.87 us
    ppermute x1, starting transfers between devices, body(): far = lax.ppermute(own, AXES, X_SWAP)  1.92 us
  transfers between devices with their start and end apart: 4, of which 2 were waited for; matrix products, arithmetic and copies ran while one was open for 0% of the time, Pallas kernels for 1%

profile of v5, /device:TPU:1, one launch (start us, length us, event | category | flops | bytes accessed | tf_op | source)
XLA Modules:
  0.0 94.2 jit_solution(15221841444536687465)
XLA Ops:
  0.0 0.0 copy-start.1
  0.0 0.0 copy-start.2
  0.0 0.0 copy-start.3
  0.0 0.0 copy-start.4
  0.0 0.7 copy-done.1
  0.7 0.0 copy-done.2
  0.7 0.0 copy-done.3
  0.7 0.0 copy-done.4
  0.7 0.0 copy-start
  0.7 0.9 %copy-done = bf16[128,1024]{1,0:T(8,128)(2,1)S(1)} copy-done((bf16[128,1024]{1,0:T(8,128)(2,1)S(1)}, bf16[128,1024]{1,0:T(8,128)(2,1)}, u32[]{:S(2)}) %copy-start) | copy-done | bytes 262168
  1.7 0.6 shard_map.55
  2.2 0.2 reshape.27
  2.5 41.1 %all_to_all.10 = bf16[128,2,1152]{2,1,0:T(2,128)(2,1)S(1)} all-to-all(bf16[128,2,1152]{2,1,0:T(2,128)(2,1)S(1)} %reshape.27), channel_id=1, replica_groups={{0,3,11,8,16,19,27,24,32,35,43,40,48,51,59,56,120,123,115,112,104,107,9..., dimensions={0} | all-to-all | bytes 1179648 | tf_op jit(solution)/shard_map/all_to_all | solution.py:207
  43.6 0.2 reshape.28.own_ref
  43.8 1.9 %collective-permute-start.1 = (bf16[256,1152]{1,0:T(8,128)(2,1)S(1)}, bf16[256,1152]{1,0:T(8,128)(2,1)S(1)}, u32[]{:S(2)}, u32[]{:S(2)}) collective-permute-start(bf16[256,1152]{1,0:T(8,128)(2,1)S(1)} %reshape.28.own_ref), channel_id=1, source_target_pairs={{0,1},{1,0},{4,5},{5,4},{3,2},{2,3},{7,6},{6,7},{11,10},{10,11},{1... | collective-permute-start | bytes 1769480 | tf_op jit(solution)/shard_map/ppermute | solution.py:211
  45.7 3.0 %collective-permute-start.3 = (bf16[256,1152]{1,0:T(8,128)(2,1)S(1)}, bf16[256,1152]{1,0:T(8,128)(2,1)S(1)}, u32[]{:S(2)}, u32[]{:S(2)}) collective-permute-start(bf16[256,1152]{1,0:T(8,128)(2,1)S(1)} %reshape.28.own_ref), channel_id=1, source_target_pairs={{0,448},{1,449},{4,452},{5,453},{3,0},{2,1},{7,4},{6,5},{11,3},{10... | collective-permute-start | bytes 1769480 | tf_op jit(solution)/shard_map/ppermute | solution.py:212
  48.8 5.6 %collective-permute-start = (bf16[256,1152]{1,0:T(8,128)(2,1)S(1)}, bf16[256,1152]{1,0:T(8,128)(2,1)S(1)}, u32[]{:S(2)}, u32[]{:S(2)}) collective-permute-start(bf16[256,1152]{1,0:T(8,128)(2,1)S(1)} %reshape.28.own_ref), channel_id=1, source_target_pairs={{0,4},{1,5},{4,0},{5,1},{3,7},{2,6},{7,3},{6,2},{11,15},{10,14},{1... | collective-permute-start | bytes 1769480 | tf_op jit(solution)/shard_map/ppermute | solution.py:213
  54.3 2.9 %collective-permute-done.1.far_ref = bf16[256,1152]{1,0:T(8,128)(2,1)S(1)} collective-permute-done((bf16[256,1152]{1,0:T(8,128)(2,1)S(1)}, bf16[256,1152]{1,0:T(8,128)(2,1)S(1)}, u32[]{:S(2)}, u32[]{:S(2)}) %collective-permute-start.1) | collective-permute-done | bytes 589856 | tf_op jit(solution)/shard_map/ppermute | solution.py:211
  57.2 6.1 %collective-permute-start.2 = (bf16[256,1152]{1,0:T(8,128)(2,1)S(1)}, bf16[256,1152]{1,0:T(8,128)(2,1)S(1)}, u32[]{:S(2)}, u32[]{:S(2)}) collective-permute-start(bf16[256,1152]{1,0:T(8,128)(2,1)S(1)} %collective-permute-done.1.far_ref), channel_id=1, source_target_pairs={{0,4},{1,5},{4,0},{5,1},{3,7},{2,6},{7,3},{6,2},{11,15},{10,14},{1... | collective-permute-start | bytes 1769480 | tf_op jit(solution)/shard_map/ppermute | solution.py:214
  63.3 0.0 collective-permute-done.3.high_ref
  63.4 1.1 %shard_map.56 = (f32[256,128]{1,0:T(8,128)S(1)}, f32[8,256]{1,0:T(8,128)S(1)}) custom-call(bf16[256,1152]{1,0:T(8,128)(2,1)S(1)} %reshape.28.own_ref, bf16[256,1152]{1,0:T(8,128)(2,1)S(1)} %collective-permute-done.1.far_ref, bf16[256,1152]{1,0:T(8,128)(2,1)S(1)} %collective-permute-done.3.high_ref), custom_call_target="tpu_custom_call" | custom-call | flops 600000000 | bytes 1048576 | tf_op jit(solution)/shard_map/pallas_call | solution.py:216
  64.5 0.0 collective-permute-done.core_ref
  64.5 0.4 collective-permute-done.2.both_ref
  65.0 1.2 %shard_map.57 = f32[512,128]{1,0:T(8,128)S(1)} custom-call(bf16[256,1152]{1,0:T(8,128)(2,1)S(1)} %reshape.28.own_ref, bf16[256,1152]{1,0:T(8,128)(2,1)S(1)} %collective-permute-done.core_ref, bf16[256,1152]{1,0:T(8,128)(2,1)S(1)} %collective-permute-done.2.both_ref, bf16[256,1152]{1,0:T(8,128)(2,1)S(1)} %collective-permute-done.3.high_ref, ...), custom_call_target="tpu_custom_call" | custom-call | flops 600000000 | bytes 1048576 | tf_op jit(solution)/shard_map/pallas_call | solution.py:222
  66.2 27.3 %all_to_all.11 = f32[512,1,128]{2,1,0:T(1,128)S(1)} all-to-all(f32[512,1,128]{2,1,0:T(1,128)S(1)} %bitcast.10), channel_id=1, replica_groups={{0,1,4,5,3,2,7,6,11,10,15,14,8,9,12,13,16,17,20,21,19,18,23,22,27,26,31..., dimensions={0} | all-to-all | bytes 524288 | tf_op jit(solution)/shard_map/all_to_all | solution.py:225
  93.4 0.7 shard_map.58
Async XLA Ops:
  0.0 0.7 copy-start.1
  0.0 0.7 copy-start.2
  0.0 0.7 copy-start.3
  0.0 0.7 copy-start.4
  0.7 1.0 %copy-start = (bf16[128,1024]{1,0:T(8,128)(2,1)S(1)}, bf16[128,1024]{1,0:T(8,128)(2,1)}, u32[]{:S(2)}) copy-start(bf16[128,1024]{1,0:T(8,128)(2,1)} %x_ref.1) | copy-start | bytes 786436
  43.8 13.4 %collective-permute-start.1 = (bf16[256,1152]{1,0:T(8,128)(2,1)S(1)}, bf16[256,1152]{1,0:T(8,128)(2,1)S(1)}, u32[]{:S(2)}, u32[]{:S(2)}) collective-permute-start(bf16[256,1152]{1,0:T(8,128)(2,1)S(1)} %reshape.28.own_ref), channel_id=1, source_target_pairs={{0,1},{1,0},{4,5},{5,4},{3,2},{2,3},{7,6},{6,7},{11,10},{10,11},{1... | collective-permute-start | bytes 1769480 | tf_op jit(solution)/shard_map/ppermute | solution.py:211
  45.7 17.6 %collective-permute-start.3 = (bf16[256,1152]{1,0:T(8,128)(2,1)S(1)}, bf16[256,1152]{1,0:T(8,128)(2,1)S(1)}, u32[]{:S(2)}, u32[]{:S(2)}) collective-permute-start(bf16[256,1152]{1,0:T(8,128)(2,1)S(1)} %reshape.28.own_ref), channel_id=1, source_target_pairs={{0,448},{1,449},{4,452},{5,453},{3,0},{2,1},{7,4},{6,5},{11,3},{10... | collective-permute-start | bytes 1769480 | tf_op jit(solution)/shard_map/ppermute | solution.py:212
  48.8 15.7 %collective-permute-start = (bf16[256,1152]{1,0:T(8,128)(2,1)S(1)}, bf16[256,1152]{1,0:T(8,128)(2,1)S(1)}, u32[]{:S(2)}, u32[]{:S(2)}) collective-permute-start(bf16[256,1152]{1,0:T(8,128)(2,1)S(1)} %reshape.28.own_ref), channel_id=1, source_target_pairs={{0,4},{1,5},{4,0},{5,1},{3,7},{2,6},{7,3},{6,2},{11,15},{10,14},{1... | collective-permute-start | bytes 1769480 | tf_op jit(solution)/shard_map/ppermute | solution.py:213
  57.2 7.8 %collective-permute-start.2 = (bf16[256,1152]{1,0:T(8,128)(2,1)S(1)}, bf16[256,1152]{1,0:T(8,128)(2,1)S(1)}, u32[]{:S(2)}, u32[]{:S(2)}) collective-permute-start(bf16[256,1152]{1,0:T(8,128)(2,1)S(1)} %collective-permute-done.1.far_ref), channel_id=1, source_target_pairs={{0,4},{1,5},{4,0},{5,1},{3,7},{2,6},{7,3},{6,2},{11,15},{10,14},{1... | collective-permute-start | bytes 1769480 | tf_op jit(solution)/shard_map/ppermute | solution.py:214

commit v6 on v5

--- a/solution.py
+++ b/solution.py
@@ -55,7 +55,22 @@
     return jnp.where(mask, 1.0, 0.0).astype(BF16)
 
 
-def pack_kernel(x_ref, cl_ref, ord_ref, map_ref, nbr_ref, out_ref, place_ref):
+def pack_kernel(
+    x_hbm, cl_hbm, ord_hbm, map_hbm, nbr_hbm, out_ref, place_ref,
+    x_ref, cl_ref, ord_ref, map_ref, nbr_ref, sems,
+):
+    pairs = (
+        (cl_hbm, cl_ref),
+        (map_hbm, map_ref),
+        (nbr_hbm, nbr_ref),
+        (ord_hbm, ord_ref),
+        (x_hbm, x_ref),
+    )
+    copies = [pltpu.make_async_copy(a, b, sems.at[j]) for j, (a, b) in enumerate(pairs)]
+    for copy in copies[::-1]:
+        copy.start()
+    for copy in copies[:4]:
+        copy.wait()
     clusters = cl_ref[...]
     orders = ord_ref[...]
     count = map_ref.shape[1]
@@ -77,6 +92,7 @@
         meta = jnp.where(row == at, value.astype(F32), meta)
     meta = jnp.concatenate([meta, jnp.zeros((LANES - 16, LOAD), F32)], axis=0).astype(BF16)
 
+    copies[4].wait()
     scaled = x_ref[...].astype(F32)
     mean_square = jnp.mean(scaled * scaled, axis=-1, keepdims=True)
     factor = lax.rsqrt(mean_square + 1e-06) * D ** (-0.5)
@@ -180,9 +196,10 @@
     out_ref[...] = jnp.max(jnp.where(mine, values, -2.0), axis=0, keepdims=True)
 
 
-def call(kernel, outs, scratch=(), flops=0, size=1 << 20):
+def call(kernel, outs, scratch=(), flops=0, size=1 << 20, **more):
     return pl.pallas_call(
         kernel,
+        **more,
         out_shape=outs,
         scratch_shapes=list(scratch),
         compiler_params=pltpu.CompilerParams(vmem_limit_bytes=24 << 20),
@@ -195,15 +212,20 @@
 
 
 def body(embeds, clusters, orders, owner_map, neighbours):
-    packed, place = call(
-        pack_kernel, [shape((QUART, WIDE), BF16), shape((8, LOAD), F32)], (), 10**8
-    )(
+    held = (
         embeds,
         clusters.reshape(1, LOAD),
         orders.reshape(1, LOAD),
         owner_map.reshape(1, -1),
         neighbours.T,
     )
+    packed, place = call(
+        pack_kernel,
+        [shape((QUART, WIDE), BF16), shape((8, LOAD), F32)],
+        [pltpu.VMEM(a.shape, a.dtype) for a in held] + [pltpu.SemaphoreType.DMA((5,))],
+        10**8,
+        in_specs=[pl.BlockSpec(memory_space=pltpu.HBM)] * 5,
+    )(*held)
     got = lax.all_to_all(
         packed.reshape(OWNERS, 2, WIDE), AXES, 0, 0, axis_index_groups=GROUPS, tiled=True
     )

time: 94.5 us -> 94.7 us (level)
  no operation moved by 1% of the time
where the time goes in v6:
time: 94.7 us; the launch traced here: 94.4 us
  blocking collectives  68.4 us (72%)
  starting transfers between devices  16.6 us (18%)
  Pallas kernels  3.86 us (4%)
  waiting for transfers between devices  3.32 us (4%)
  local copies, waits for them, and re-layouts  2.08 us (2%)
    all_to_all x1, blocking collectives, body(): lax.all_to_all(packed.reshape(OWNERS, 2, WIDE), AXES, 0, 0, axis_index_gr...  41.1 us
    all_to_all x1, blocking collectives, body(): lax.all_to_all(best.reshape(4 * OWNERS, 1, LANES), AXES, 0, 0, axis_index...  27.3 us
    ppermute x1, starting transfers between devices, body(): both = lax.ppermute(far, AXES, C_SWAP)  6.14 us
    ppermute x1, starting transfers between devices, body(): core = lax.ppermute(own, AXES, C_SWAP)  5.57 us
    ppermute x1, starting transfers between devices, body(): high = lax.ppermute(own, AXES, DOWN)  3.02 us
    ppermute x1, waiting for transfers between devices, body(): far = lax.ppermute(own, AXES, X_SWAP)  2.87 us
    ppermute x1, starting transfers between devices, body(): far = lax.ppermute(own, AXES, X_SWAP)  1.92 us
  transfers between devices with their start and end apart: 4, of which 2 were waited for; matrix products, arithmetic and copies ran while one was open for 0% of the time, Pallas kernels for 1%

profile of v6, /device:TPU:1, one launch (start us, length us, event | category | flops | bytes accessed | tf_op | source)
XLA Modules:
  0.0 94.4 jit_solution(1280362115748177328)
XLA Ops:
  0.0 0.0 copy-start.1
  0.0 0.0 copy-start.2
  0.0 0.0 copy-start.3
  0.0 0.0 copy-start.4
  0.0 0.7 copy-done.1
  0.7 0.0 copy-done.2
  0.7 0.0 copy-done.3
  0.7 0.0 copy-done.4
  0.7 0.0 copy-start
  0.7 0.9 %copy-done = bf16[128,1024]{1,0:T(8,128)(2,1)S(1)} copy-done((bf16[128,1024]{1,0:T(8,128)(2,1)S(1)}, bf16[128,1024]{1,0:T(8,128)(2,1)}, u32[]{:S(2)}) %copy-start) | copy-done | bytes 262168
  1.7 0.8 shard_map.55
  2.5 0.2 reshape.27
  2.7 41.1 %all_to_all.10 = bf16[128,2,1152]{2,1,0:T(2,128)(2,1)S(1)} all-to-all(bf16[128,2,1152]{2,1,0:T(2,128)(2,1)S(1)} %reshape.27), channel_id=1, replica_groups={{0,3,11,8,16,19,27,24,32,35,43,40,48,51,59,56,120,123,115,112,104,107,9..., dimensions={0} | all-to-all | bytes 1179648 | tf_op jit(solution)/shard_map/all_to_all | solution.py:229
  43.8 0.2 reshape.28.own_ref
  44.0 1.9 %collective-permute-start.1 = (bf16[256,1152]{1,0:T(8,128)(2,1)S(1)}, bf16[256,1152]{1,0:T(8,128)(2,1)S(1)}, u32[]{:S(2)}, u32[]{:S(2)}) collective-permute-start(bf16[256,1152]{1,0:T(8,128)(2,1)S(1)} %reshape.28.own_ref), channel_id=1, source_target_pairs={{0,1},{1,0},{4,5},{5,4},{3,2},{2,3},{7,6},{6,7},{11,10},{10,11},{1... | collective-permute-start | bytes 1769480 | tf_op jit(solution)/shard_map/ppermute | solution.py:233
  46.0 3.0 %collective-permute-start.3 = (bf16[256,1152]{1,0:T(8,128)(2,1)S(1)}, bf16[256,1152]{1,0:T(8,128)(2,1)S(1)}, u32[]{:S(2)}, u32[]{:S(2)}) collective-permute-start(bf16[256,1152]{1,0:T(8,128)(2,1)S(1)} %reshape.28.own_ref), channel_id=1, source_target_pairs={{0,448},{1,449},{4,452},{5,453},{3,0},{2,1},{7,4},{6,5},{11,3},{10... | collective-permute-start | bytes 1769480 | tf_op jit(solution)/shard_map/ppermute | solution.py:234
  49.0 5.6 %collective-permute-start = (bf16[256,1152]{1,0:T(8,128)(2,1)S(1)}, bf16[256,1152]{1,0:T(8,128)(2,1)S(1)}, u32[]{:S(2)}, u32[]{:S(2)}) collective-permute-start(bf16[256,1152]{1,0:T(8,128)(2,1)S(1)} %reshape.28.own_ref), channel_id=1, source_target_pairs={{0,4},{1,5},{4,0},{5,1},{3,7},{2,6},{7,3},{6,2},{11,15},{10,14},{1... | collective-permute-start | bytes 1769480 | tf_op jit(solution)/shard_map/ppermute | solution.py:235
  54.6 2.9 %collective-permute-done.1.far_ref = bf16[256,1152]{1,0:T(8,128)(2,1)S(1)} collective-permute-done((bf16[256,1152]{1,0:T(8,128)(2,1)S(1)}, bf16[256,1152]{1,0:T(8,128)(2,1)S(1)}, u32[]{:S(2)}, u32[]{:S(2)}) %collective-permute-start.1) | collective-permute-done | bytes 589856 | tf_op jit(solution)/shard_map/ppermute | solution.py:233
  57.4 6.1 %collective-permute-start.2 = (bf16[256,1152]{1,0:T(8,128)(2,1)S(1)}, bf16[256,1152]{1,0:T(8,128)(2,1)S(1)}, u32[]{:S(2)}, u32[]{:S(2)}) collective-permute-start(bf16[256,1152]{1,0:T(8,128)(2,1)S(1)} %collective-permute-done.1.far_ref), channel_id=1, source_target_pairs={{0,4},{1,5},{4,0},{5,1},{3,7},{2,6},{7,3},{6,2},{11,15},{10,14},{1... | collective-permute-start | bytes 1769480 | tf_op jit(solution)/shard_map/ppermute | solution.py:236
  63.6 0.0 collective-permute-done.3.high_ref
  63.6 1.1 %shard_map.56 = (f32[256,128]{1,0:T(8,128)S(1)}, f32[8,256]{1,0:T(8,128)S(1)}) custom-call(bf16[256,1152]{1,0:T(8,128)(2,1)S(1)} %reshape.28.own_ref, bf16[256,1152]{1,0:T(8,128)(2,1)S(1)} %collective-permute-done.1.far_ref, bf16[256,1152]{1,0:T(8,128)(2,1)S(1)} %collective-permute-done.3.high_ref), custom_call_target="tpu_custom_call" | custom-call | flops 600000000 | bytes 1048576 | tf_op jit(solution)/shard_map/pallas_call | solution.py:238
  64.7 0.0 collective-permute-done.core_ref
  64.7 0.4 collective-permute-done.2.both_ref
  65.2 1.2 %shard_map.57 = f32[512,128]{1,0:T(8,128)S(1)} custom-call(bf16[256,1152]{1,0:T(8,128)(2,1)S(1)} %reshape.28.own_ref, bf16[256,1152]{1,0:T(8,128)(2,1)S(1)} %collective-permute-done.core_ref, bf16[256,1152]{1,0:T(8,128)(2,1)S(1)} %collective-permute-done.2.both_ref, bf16[256,1152]{1,0:T(8,128)(2,1)S(1)} %collective-permute-done.3.high_ref, ...), custom_call_target="tpu_custom_call" | custom-call | flops 600000000 | bytes 1048576 | tf_op jit(solution)/shard_map/pallas_call | solution.py:244
  66.4 27.3 %all_to_all.11 = f32[512,1,128]{2,1,0:T(1,128)S(1)} all-to-all(f32[512,1,128]{2,1,0:T(1,128)S(1)} %bitcast.10), channel_id=1, replica_groups={{0,1,4,5,3,2,7,6,11,10,15,14,8,9,12,13,16,17,20,21,19,18,23,22,27,26,31..., dimensions={0} | all-to-all | bytes 524288 | tf_op jit(solution)/shard_map/all_to_all | solution.py:247
  93.7 0.7 shard_map.58
Async XLA Ops:
  0.0 0.7 copy-start.1
  0.0 0.7 copy-start.2
  0.0 0.7 copy-start.3
  0.0 0.7 copy-start.4
  0.7 1.0 %copy-start = (bf16[128,1024]{1,0:T(8,128)(2,1)S(1)}, bf16[128,1024]{1,0:T(8,128)(2,1)}, u32[]{:S(2)}) copy-start(bf16[128,1024]{1,0:T(8,128)(2,1)} %x_hbm.1) | copy-start | bytes 786436
  44.0 13.4 %collective-permute-start.1 = (bf16[256,1152]{1,0:T(8,128)(2,1)S(1)}, bf16[256,1152]{1,0:T(8,128)(2,1)S(1)}, u32[]{:S(2)}, u32[]{:S(2)}) collective-permute-start(bf16[256,1152]{1,0:T(8,128)(2,1)S(1)} %reshape.28.own_ref), channel_id=1, source_target_pairs={{0,1},{1,0},{4,5},{5,4},{3,2},{2,3},{7,6},{6,7},{11,10},{10,11},{1... | collective-permute-start | bytes 1769480 | tf_op jit(solution)/shard_map/ppermute | solution.py:233
  46.0 17.6 %collective-permute-start.3 = (bf16[256,1152]{1,0:T(8,128)(2,1)S(1)}, bf16[256,1152]{1,0:T(8,128)(2,1)S(1)}, u32[]{:S(2)}, u32[]{:S(2)}) collective-permute-start(bf16[256,1152]{1,0:T(8,128)(2,1)S(1)} %reshape.28.own_ref), channel_id=1, source_target_pairs={{0,448},{1,449},{4,452},{5,453},{3,0},{2,1},{7,4},{6,5},{11,3},{10... | collective-permute-start | bytes 1769480 | tf_op jit(solution)/shard_map/ppermute | solution.py:234
  49.0 15.7 %collective-permute-start = (bf16[256,1152]{1,0:T(8,128)(2,1)S(1)}, bf16[256,1152]{1,0:T(8,128)(2,1)S(1)}, u32[]{:S(2)}, u32[]{:S(2)}) collective-permute-start(bf16[256,1152]{1,0:T(8,128)(2,1)S(1)} %reshape.28.own_ref), channel_id=1, source_target_pairs={{0,4},{1,5},{4,0},{5,1},{3,7},{2,6},{7,3},{6,2},{11,15},{10,14},{1... | collective-permute-start | bytes 1769480 | tf_op jit(solution)/shard_map/ppermute | solution.py:235
  57.4 7.8 %collective-permute-start.2 = (bf16[256,1152]{1,0:T(8,128)(2,1)S(1)}, bf16[256,1152]{1,0:T(8,128)(2,1)S(1)}, u32[]{:S(2)}, u32[]{:S(2)}) collective-permute-start(bf16[256,1152]{1,0:T(8,128)(2,1)S(1)} %collective-permute-done.1.far_ref), channel_id=1, source_target_pairs={{0,4},{1,5},{4,0},{5,1},{3,7},{2,6},{7,3},{6,2},{11,15},{10,14},{1... | collective-permute-start | bytes 1769480 | tf_op jit(solution)/shard_map/ppermute | solution.py:236

commit v7 on v5

--- a/solution.py
+++ b/solution.py
@@ -13,6 +13,7 @@
 LANES = 128
 WIDE = D + LANES
 QUART = 2 * OWNERS
+CHIPS = OWNERS // 2
 F32, BF16 = jnp.float32, jnp.bfloat16
 
 
@@ -26,8 +27,7 @@
 
 
 QUARTERS = [(core, half) for core in range(2) for half in range(2)]
-GROUPS = [[device_of(o, c, h) for o in range(OWNERS)] for c, h in QUARTERS]
-EVERY = [[device_of(o, c, h) for o in range(OWNERS) for c, h in QUARTERS]]
+GROUPS = [sorted(device_of(o, c, h) for o in range(OWNERS)) for c, h in QUARTERS]
 
 
 def moves(shift, core, half):
@@ -41,6 +41,13 @@
 X_SWAP = moves(0, 0, 1)
 C_SWAP = moves(0, 1, 0)
 DOWN = moves(-1, 0, 0)
+
+
+def rank_of(owner):
+    step = owner >> 1
+    y = step >> 3
+    z = (step & 7) ^ (7 * (y & 1))
+    return ((y * Z + z) << 1) | ((owner ^ step) & 1)
 
 
 def iota(shape, dim):
@@ -62,7 +69,9 @@
     onehot = ones_where(iota((count, LOAD), 0) == clusters)
     first, second = nbr_ref[0:1, :], nbr_ref[1:2, :]
     row = iota((16, count), 0)
-    table = jnp.where(row == 0, map_ref[...], 0)
+    owners = map_ref[...]
+    table = jnp.where(row == 0, rank_of(owners), 0)
+    table = jnp.where(row == 1, rank_of((owners + OWNERS - 1) & (OWNERS - 1)), table)
     for at, value in enumerate((first >> 8, first & 255, second >> 8, second & 255)):
         table = jnp.where(row == 4 + at, value, table)
     looked = jnp.dot(table.astype(F32).astype(BF16), onehot, preferred_element_type=F32)
@@ -88,7 +97,7 @@
     out_ref[:, 0:D] = jnp.dot(pick, unit, preferred_element_type=F32).astype(BF16)
     out_ref[:, D:WIDE] = nt(pick, meta).astype(BF16)
     row = iota((8, LOAD), 0)
-    place_ref[...] = jnp.where(row == 0, owner, rank)
+    place_ref[...] = jnp.where(row == 0, owner, jnp.where(row == 1, looked[1:2, :], rank))
 
 
 def key_meta(key_ref):
@@ -106,14 +115,23 @@
     return jnp.where(related & (key[0] < order), scores, -1.0)
 
 
-def my_quarter():
+def place_rows(out_ref, flip, pairs):
     device = lax.axis_index("shard") * X + lax.axis_index("rep")
-    x = device & 3
-    return ((device >> 2) & 1) * 2 + ((x >> 1) ^ (x & 1))
-
-
-def halves(ref):
-    return ref[pl.ds(0, OWNERS, stride=2), :], ref[pl.ds(1, OWNERS, stride=2), :]
+    core = ((device >> 2) & 1) ^ (flip >> 1)
+    half = ((device >> 1) & 1) ^ (device & 1) ^ (flip & 1)
+    for pair, values in enumerate(pairs):
+        at = 4 * core + 2 * pair + (half ^ pair)
+        out_ref[pl.ds(at, CHIPS, stride=8), :] = values
+
+
+def lanes_of(ref, first, base):
+    lane = iota((CHIPS, LANES), 1)
+    out = []
+    for pair in range(2):
+        even, odd = (ref[pl.ds(2 * pair + k, CHIPS, stride=4), :] for k in range(2))
+        rest = base[pair] if base is not None else -1.0
+        out.append(jnp.where(lane == first, even, jnp.where(lane == first + 1, odd, rest)))
+    return out
 
 
 def score_part(query, own_ref, own_key, high_ref, high_key, turn_ref):
@@ -130,17 +148,16 @@
     best = jnp.max(best, axis=1, keepdims=True)
     upper = jnp.max(masked(scores, high_key, meta), axis=0, keepdims=True)
     turn_ref[...] = jnp.broadcast_to(best, (QUART, LANES))
-    even, odd = halves(turn_ref)
-    lane = iota((OWNERS, LANES), 1)
-    return jnp.where(lane == 0, even, jnp.where(lane == 1, odd, -1.0)), upper
+    return lanes_of(turn_ref, 0, None), upper
 
 
 def early_kernel(own_ref, far_ref, high_ref, out_ref, upper_ref, turn_ref):
     own_key, high_key = key_meta(own_ref), key_meta(high_ref)
     upper = None
     for flip, query in enumerate((own_ref, far_ref)):
-        pair, over = score_part(query, own_ref, own_key, high_ref, high_key, turn_ref)
-        out_ref[pl.ds(flip * OWNERS, OWNERS), :] = pair
+        pairs, over = score_part(query, own_ref, own_key, high_ref, high_key, turn_ref)
+        for pair, values in enumerate(pairs):
+            out_ref[pl.ds((2 * flip + pair) * CHIPS, CHIPS), :] = values
         upper = over if upper is None else jnp.maximum(upper, over)
     upper_ref[...] = jnp.broadcast_to(upper, (8, QUART))
 
@@ -148,36 +165,35 @@
 def late_kernel(
     own_ref, core_ref, both_ref, high_ref, early_ref, upper_ref, out_ref, turn_ref, top_ref
 ):
-    quarter = my_quarter()
     own_key, high_key = key_meta(own_ref), key_meta(high_ref)
     upper = upper_ref[0:1, :]
     for flip, query in ((2, core_ref), (3, both_ref)):
-        pair, over = score_part(query, own_ref, own_key, high_ref, high_key, turn_ref)
-        out_ref[pl.ds(quarter ^ flip, OWNERS, stride=4), :] = pair
+        pairs, over = score_part(query, own_ref, own_key, high_ref, high_key, turn_ref)
+        place_rows(out_ref, flip, pairs)
         upper = jnp.maximum(upper, over)
-    pair = early_ref[pl.ds(OWNERS, OWNERS), :]
-    out_ref[pl.ds(quarter ^ 1, OWNERS, stride=4), :] = pair
+    own, far = (
+        [early_ref[pl.ds((2 * flip + pair) * CHIPS, CHIPS), :] for pair in range(2)]
+        for flip in range(2)
+    )
+    place_rows(out_ref, 1, far)
     top_ref[...] = jnp.broadcast_to(upper, (LANES, QUART)).T
-    even, odd = halves(top_ref)
-    lane = iota((OWNERS, LANES), 1)
-    pair = early_ref[pl.ds(0, OWNERS), :]
-    pair = jnp.where(lane == 2, even, jnp.where(lane == 3, odd, pair))
-    out_ref[pl.ds(quarter, OWNERS, stride=4), :] = pair
+    place_rows(out_ref, 0, lanes_of(top_ref, 2, own))
 
 
 def pick_kernel(got_ref, place_ref, out_ref):
-    best = got_ref[pl.ds(0, OWNERS, stride=4), :]
-    for q in range(1, 4):
-        best = jnp.maximum(best, got_ref[pl.ds(q, OWNERS, stride=4), :])
-    owner, rank = place_ref[0:1, :], place_ref[1:2, :]
-    mine = owner == iota((OWNERS, LOAD), 0).astype(F32)
-    lower = pltpu.roll(best, 1, 0)
-    values = jnp.where(
-        rank == 0.0,
-        jnp.maximum(best[:, 0:1], lower[:, 2:3]),
-        jnp.maximum(best[:, 1:2], lower[:, 3:4]),
-    )
-    out_ref[...] = jnp.max(jnp.where(mine, values, -2.0), axis=0, keepdims=True)
+    owner, lower, rank = place_ref[0:1, :], place_ref[1:2, :], place_ref[2:3, :]
+    found = jnp.full((1, LOAD), -1.0, F32)
+    for pair in range(2):
+        best = None
+        for at in (0, 1, 4, 5):
+            part = got_ref[pl.ds(2 * pair + at, CHIPS, stride=8), :]
+            best = part if best is None else jnp.maximum(best, part)
+        here = (iota((CHIPS, LOAD), 0) * 2 + pair).astype(F32)
+        for target, lane in ((owner, 0), (lower, 2)):
+            values = jnp.where(rank == 0.0, best[:, lane : lane + 1], best[:, lane + 1 : lane + 2])
+            values = jnp.where(target == here, values, -1.0)
+            found = jnp.maximum(found, jnp.max(values, axis=0, keepdims=True))
+    out_ref[...] = found
 
 
 def call(kernel, outs, scratch=(), flops=0, size=1 << 20):
@@ -222,9 +238,7 @@
     best = call(late_kernel, shape((4 * OWNERS, LANES), F32), turn, 6 * 10**8)(
         own, core, both, high, early, upper
     )
-    back = lax.all_to_all(
-        best.reshape(4 * OWNERS, 1, LANES), AXES, 0, 0, axis_index_groups=EVERY, tiled=True
-    )
+    back = lax.all_to_all(best.reshape(4 * OWNERS, 1, LANES), AXES, 0, 0, tiled=True)
     return call(pick_kernel, shape((1, LOAD), F32))(
         back.reshape(4 * OWNERS, LANES), place
     ).reshape(LOAD)

time: 94.5 us -> 93.1 us (0.985)
  blocking collectives: 68.4 us -> 67.1 us
    ppermute x1, starting transfers between devices: 3.03 us -> 2.07 us  [body(): high = lax.ppermute(own, AXES, DOWN)]
where the time goes in v7:
time: 93.1 us; the launch traced here: 92.8 us
  blocking collectives  67.1 us (72%)
  starting transfers between devices  16.3 us (18%)
  waiting for transfers between devices  3.71 us (4%)
  Pallas kernels  3.61 us (4%)
  local copies, waits for them, and re-layouts  2.08 us (2%)
    all_to_all x1, blocking collectives, body(): lax.all_to_all(packed.reshape(OWNERS, 2, WIDE), AXES, 0, 0, axis_index_gr...  40.3 us
    all_to_all x1, blocking collectives, body(): lax.all_to_all(best.reshape(4 * OWNERS, 1, LANES), AXES, 0, 0, tiled=True)  26.7 us
    ppermute x1, starting transfers between devices, body(): both = lax.ppermute(far, AXES, C_SWAP)  6.23 us
    ppermute x1, starting transfers between devices, body(): core = lax.ppermute(own, AXES, C_SWAP)  6.03 us
    ppermute x1, waiting for transfers between devices, body(): far = lax.ppermute(own, AXES, X_SWAP)  3.26 us
    ppermute x1, starting transfers between devices, body(): high = lax.ppermute(own, AXES, DOWN)  2.07 us
    ppermute x1, starting transfers between devices, body(): far = lax.ppermute(own, AXES, X_SWAP)  1.92 us
  transfers between devices with their start and end apart: 4, of which 2 were waited for; matrix products, arithmetic and copies ran while one was open for 0% of the time, Pallas kernels for 1%

profile of v7, /device:TPU:1, one launch (start us, length us, event | category | flops | bytes accessed | tf_op | source)
XLA Modules:
  0.0 92.8 jit_solution(17559856236879388157)
XLA Ops:
  0.0 0.0 copy-start.1
  0.0 0.0 copy-start.2
  0.0 0.0 copy-start.3
  0.0 0.0 copy-start.4
  0.0 0.7 copy-done.1
  0.7 0.0 copy-done.2
  0.7 0.0 copy-done.3
  0.7 0.0 copy-done.4
  0.7 0.0 copy-start
  0.7 0.9 %copy-done = bf16[128,1024]{1,0:T(8,128)(2,1)S(1)} copy-done((bf16[128,1024]{1,0:T(8,128)(2,1)S(1)}, bf16[128,1024]{1,0:T(8,128)(2,1)}, u32[]{:S(2)}) %copy-start) | copy-done | bytes 262168
  1.7 0.6 shard_map.55
  2.2 0.2 reshape.27
  2.5 40.3 %all_to_all.10 = bf16[128,2,1152]{2,1,0:T(2,128)(2,1)S(1)} all-to-all(bf16[128,2,1152]{2,1,0:T(2,128)(2,1)S(1)} %reshape.27), channel_id=1, replica_groups={{0,3,8,11,16,19,24,27,32,35,40,43,48,51,56,59,64,67,72,75,80,83,88,91,9..., dimensions={0} | all-to-all | bytes 1179648 | tf_op jit(solution)/shard_map/all_to_all | solution.py:223
  42.8 0.2 reshape.28.own_ref
  43.0 1.9 %collective-permute-start.1 = (bf16[256,1152]{1,0:T(8,128)(2,1)S(1)}, bf16[256,1152]{1,0:T(8,128)(2,1)S(1)}, u32[]{:S(2)}, u32[]{:S(2)}) collective-permute-start(bf16[256,1152]{1,0:T(8,128)(2,1)S(1)} %reshape.28.own_ref), channel_id=1, source_target_pairs={{0,1},{1,0},{4,5},{5,4},{3,2},{2,3},{7,6},{6,7},{11,10},{10,11},{1... | collective-permute-start | bytes 1769480 | tf_op jit(solution)/shard_map/ppermute | solution.py:227
  44.9 2.1 %collective-permute-start.3 = (bf16[256,1152]{1,0:T(8,128)(2,1)S(1)}, bf16[256,1152]{1,0:T(8,128)(2,1)S(1)}, u32[]{:S(2)}, u32[]{:S(2)}) collective-permute-start(bf16[256,1152]{1,0:T(8,128)(2,1)S(1)} %reshape.28.own_ref), channel_id=1, source_target_pairs={{0,448},{1,449},{4,452},{5,453},{3,0},{2,1},{7,4},{6,5},{11,3},{10... | collective-permute-start | bytes 1769480 | tf_op jit(solution)/shard_map/ppermute | solution.py:228
  47.0 6.0 %collective-permute-start = (bf16[256,1152]{1,0:T(8,128)(2,1)S(1)}, bf16[256,1152]{1,0:T(8,128)(2,1)S(1)}, u32[]{:S(2)}, u32[]{:S(2)}) collective-permute-start(bf16[256,1152]{1,0:T(8,128)(2,1)S(1)} %reshape.28.own_ref), channel_id=1, source_target_pairs={{0,4},{1,5},{4,0},{5,1},{3,7},{2,6},{7,3},{6,2},{11,15},{10,14},{1... | collective-permute-start | bytes 1769480 | tf_op jit(solution)/shard_map/ppermute | solution.py:229
  53.1 3.3 %collective-permute-done.1.far_ref = bf16[256,1152]{1,0:T(8,128)(2,1)S(1)} collective-permute-done((bf16[256,1152]{1,0:T(8,128)(2,1)S(1)}, bf16[256,1152]{1,0:T(8,128)(2,1)S(1)}, u32[]{:S(2)}, u32[]{:S(2)}) %collective-permute-start.1) | collective-permute-done | bytes 589856 | tf_op jit(solution)/shard_map/ppermute | solution.py:227
  56.3 6.2 %collective-permute-start.2 = (bf16[256,1152]{1,0:T(8,128)(2,1)S(1)}, bf16[256,1152]{1,0:T(8,128)(2,1)S(1)}, u32[]{:S(2)}, u32[]{:S(2)}) collective-permute-start(bf16[256,1152]{1,0:T(8,128)(2,1)S(1)} %collective-permute-done.1.far_ref), channel_id=1, source_target_pairs={{0,4},{1,5},{4,0},{5,1},{3,7},{2,6},{7,3},{6,2},{11,15},{10,14},{1... | collective-permute-start | bytes 1769480 | tf_op jit(solution)/shard_map/ppermute | solution.py:230
  62.6 0.0 collective-permute-done.3.high_ref
  62.6 1.1 %shard_map.56 = (f32[256,128]{1,0:T(8,128)S(1)}, f32[8,256]{1,0:T(8,128)S(1)}) custom-call(bf16[256,1152]{1,0:T(8,128)(2,1)S(1)} %reshape.28.own_ref, bf16[256,1152]{1,0:T(8,128)(2,1)S(1)} %collective-permute-done.1.far_ref, bf16[256,1152]{1,0:T(8,128)(2,1)S(1)} %collective-permute-done.3.high_ref), custom_call_target="tpu_custom_call" | custom-call | flops 600000000 | bytes 1048576 | tf_op jit(solution)/shard_map/pallas_call | solution.py:232
  63.7 0.0 collective-permute-done.core_ref
  63.7 0.4 collective-permute-done.2.both_ref
  64.2 1.2 %shard_map.57 = f32[512,128]{1,0:T(8,128)S(1)} custom-call(bf16[256,1152]{1,0:T(8,128)(2,1)S(1)} %reshape.28.own_ref, bf16[256,1152]{1,0:T(8,128)(2,1)S(1)} %collective-permute-done.core_ref, bf16[256,1152]{1,0:T(8,128)(2,1)S(1)} %collective-permute-done.2.both_ref, bf16[256,1152]{1,0:T(8,128)(2,1)S(1)} %collective-permute-done.3.high_ref, ...), custom_call_target="tpu_custom_call" | custom-call | flops 600000000 | bytes 1048576 | tf_op jit(solution)/shard_map/pallas_call | solution.py:238
  65.4 26.7 %all_to_all.11 = f32[512,1,128]{2,1,0:T(1,128)S(1)} all-to-all(f32[512,1,128]{2,1,0:T(1,128)S(1)} %bitcast.10), channel_id=1, replica_groups=mesh['shard'=128,'rep'=4] {'shard','rep'}, dimensions={0} | all-to-all | bytes 524288 | tf_op jit(solution)/shard_map/all_to_all | solution.py:241
  92.1 0.7 shard_map.58
Async XLA Ops:
  0.0 0.7 copy-start.1
  0.0 0.7 copy-start.2
  0.0 0.7 copy-start.3
  0.0 0.7 copy-start.4
  0.7 1.0 %copy-start = (bf16[128,1024]{1,0:T(8,128)(2,1)S(1)}, bf16[128,1024]{1,0:T(8,128)(2,1)}, u32[]{:S(2)}) copy-start(bf16[128,1024]{1,0:T(8,128)(2,1)} %x_ref.1) | copy-start | bytes 786436
  43.0 13.3 %collective-permute-start.1 = (bf16[256,1152]{1,0:T(8,128)(2,1)S(1)}, bf16[256,1152]{1,0:T(8,128)(2,1)S(1)}, u32[]{:S(2)}, u32[]{:S(2)}) collective-permute-start(bf16[256,1152]{1,0:T(8,128)(2,1)S(1)} %reshape.28.own_ref), channel_id=1, source_target_pairs={{0,1},{1,0},{4,5},{5,4},{3,2},{2,3},{7,6},{6,7},{11,10},{10,11},{1... | collective-permute-start | bytes 1769480 | tf_op jit(solution)/shard_map/ppermute | solution.py:227
  44.9 17.6 %collective-permute-start.3 = (bf16[256,1152]{1,0:T(8,128)(2,1)S(1)}, bf16[256,1152]{1,0:T(8,128)(2,1)S(1)}, u32[]{:S(2)}, u32[]{:S(2)}) collective-permute-start(bf16[256,1152]{1,0:T(8,128)(2,1)S(1)} %reshape.28.own_ref), channel_id=1, source_target_pairs={{0,448},{1,449},{4,452},{5,453},{3,0},{2,1},{7,4},{6,5},{11,3},{10... | collective-permute-start | bytes 1769480 | tf_op jit(solution)/shard_map/ppermute | solution.py:228
  47.0 16.7 %collective-permute-start = (bf16[256,1152]{1,0:T(8,128)(2,1)S(1)}, bf16[256,1152]{1,0:T(8,128)(2,1)S(1)}, u32[]{:S(2)}, u32[]{:S(2)}) collective-permute-start(bf16[256,1152]{1,0:T(8,128)(2,1)S(1)} %reshape.28.own_ref), channel_id=1, source_target_pairs={{0,4},{1,5},{4,0},{5,1},{3,7},{2,6},{7,3},{6,2},{11,15},{10,14},{1... | collective-permute-start | bytes 1769480 | tf_op jit(solution)/shard_map/ppermute | solution.py:229
  56.3 7.8 %collective-permute-start.2 = (bf16[256,1152]{1,0:T(8,128)(2,1)S(1)}, bf16[256,1152]{1,0:T(8,128)(2,1)S(1)}, u32[]{:S(2)}, u32[]{:S(2)}) collective-permute-start(bf16[256,1152]{1,0:T(8,128)(2,1)S(1)} %collective-permute-done.1.far_ref), channel_id=1, source_target_pairs={{0,4},{1,5},{4,0},{5,1},{3,7},{2,6},{7,3},{6,2},{11,15},{10,14},{1... | collective-permute-start | bytes 1769480 | tf_op jit(solution)/shard_map/ppermute | solution.py:230

commit v8 on v7

--- a/solution.py
+++ b/solution.py
@@ -13,7 +13,6 @@
 LANES = 128
 WIDE = D + LANES
 QUART = 2 * OWNERS
-CHIPS = OWNERS // 2
 F32, BF16 = jnp.float32, jnp.bfloat16
 
 
@@ -27,6 +26,7 @@
 
 
 QUARTERS = [(core, half) for core in range(2) for half in range(2)]
+OWNED = [[device_of(o, c, h) for c, h in QUARTERS] for o in range(OWNERS)]
 GROUPS = [sorted(device_of(o, c, h) for o in range(OWNERS)) for c, h in QUARTERS]
 
 
@@ -115,23 +115,10 @@
     return jnp.where(related & (key[0] < order), scores, -1.0)
 
 
-def place_rows(out_ref, flip, pairs):
-    device = lax.axis_index("shard") * X + lax.axis_index("rep")
-    core = ((device >> 2) & 1) ^ (flip >> 1)
-    half = ((device >> 1) & 1) ^ (device & 1) ^ (flip & 1)
-    for pair, values in enumerate(pairs):
-        at = 4 * core + 2 * pair + (half ^ pair)
-        out_ref[pl.ds(at, CHIPS, stride=8), :] = values
-
-
-def lanes_of(ref, first, base):
-    lane = iota((CHIPS, LANES), 1)
-    out = []
-    for pair in range(2):
-        even, odd = (ref[pl.ds(2 * pair + k, CHIPS, stride=4), :] for k in range(2))
-        rest = base[pair] if base is not None else -1.0
-        out.append(jnp.where(lane == first, even, jnp.where(lane == first + 1, odd, rest)))
-    return out
+def into_lanes(ref, first, base):
+    lane = iota((OWNERS, LANES), 1)
+    even, odd = (ref[pl.ds(k, OWNERS, stride=2), :] for k in range(2))
+    return jnp.where(lane == first, even, jnp.where(lane == first + 1, odd, base))
 
 
 def score_part(query, own_ref, own_key, high_ref, high_key, turn_ref):
@@ -148,52 +135,58 @@
     best = jnp.max(best, axis=1, keepdims=True)
     upper = jnp.max(masked(scores, high_key, meta), axis=0, keepdims=True)
     turn_ref[...] = jnp.broadcast_to(best, (QUART, LANES))
-    return lanes_of(turn_ref, 0, None), upper
+    return upper
 
 
 def early_kernel(own_ref, far_ref, high_ref, out_ref, upper_ref, turn_ref):
     own_key, high_key = key_meta(own_ref), key_meta(high_ref)
-    upper = None
+    upper, found = None, -1.0
     for flip, query in enumerate((own_ref, far_ref)):
-        pairs, over = score_part(query, own_ref, own_key, high_ref, high_key, turn_ref)
-        for pair, values in enumerate(pairs):
-            out_ref[pl.ds((2 * flip + pair) * CHIPS, CHIPS), :] = values
+        over = score_part(query, own_ref, own_key, high_ref, high_key, turn_ref)
+        found = into_lanes(turn_ref, 2 * flip, found)
         upper = over if upper is None else jnp.maximum(upper, over)
+    out_ref[...] = found
     upper_ref[...] = jnp.broadcast_to(upper, (8, QUART))
 
 
 def late_kernel(
-    own_ref, core_ref, both_ref, high_ref, early_ref, upper_ref, out_ref, turn_ref, top_ref
+    own_ref, core_ref, both_ref, high_ref, early_ref, over_ref, out_ref, upper_ref, turn_ref
 ):
     own_key, high_key = key_meta(own_ref), key_meta(high_ref)
-    upper = upper_ref[0:1, :]
+    upper, found = over_ref[0:1, :], early_ref[...]
     for flip, query in ((2, core_ref), (3, both_ref)):
-        pairs, over = score_part(query, own_ref, own_key, high_ref, high_key, turn_ref)
-        place_rows(out_ref, flip, pairs)
+        over = score_part(query, own_ref, own_key, high_ref, high_key, turn_ref)
+        found = into_lanes(turn_ref, 2 * flip, found)
         upper = jnp.maximum(upper, over)
-    own, far = (
-        [early_ref[pl.ds((2 * flip + pair) * CHIPS, CHIPS), :] for pair in range(2)]
-        for flip in range(2)
-    )
-    place_rows(out_ref, 1, far)
-    top_ref[...] = jnp.broadcast_to(upper, (LANES, QUART)).T
-    place_rows(out_ref, 0, lanes_of(top_ref, 2, own))
+    turn_ref[...] = jnp.broadcast_to(upper, (LANES, QUART)).T
+    rows = into_lanes(turn_ref, 8, found).T
+    upper_ref[...] = rows[8:16, :]
+    device = lax.axis_index("shard") * X + lax.axis_index("rep")
+    mine = ((device >> 2) & 1) * 2 + (((device >> 1) ^ device) & 1)
+    for q in range(4):
+        part = rows[0:2, :]
+        for flip in range(1, 4):
+            part = jnp.where((mine ^ q) == flip, rows[2 * flip : 2 * flip + 2, :], part)
+        out_ref[pl.ds(8 * q, 8), :] = jnp.concatenate([part] * 4, axis=0)
+
+
+def merge_kernel(got_ref, upper_ref, out_ref):
+    best = got_ref[0:8, :]
+    for q in range(1, 4):
+        best = jnp.maximum(best, got_ref[pl.ds(8 * q, 8), :])
+    rows = jnp.concatenate([best[0:2, :], upper_ref[0:2, :], best[0:4, :]], axis=0)
+    out_ref[...] = jnp.concatenate([rows] * (OWNERS // 8), axis=0).T
 
 
 def pick_kernel(got_ref, place_ref, out_ref):
     owner, lower, rank = place_ref[0:1, :], place_ref[1:2, :], place_ref[2:3, :]
-    found = jnp.full((1, LOAD), -1.0, F32)
-    for pair in range(2):
-        best = None
-        for at in (0, 1, 4, 5):
-            part = got_ref[pl.ds(2 * pair + at, CHIPS, stride=8), :]
-            best = part if best is None else jnp.maximum(best, part)
-        here = (iota((CHIPS, LOAD), 0) * 2 + pair).astype(F32)
-        for target, lane in ((owner, 0), (lower, 2)):
-            values = jnp.where(rank == 0.0, best[:, lane : lane + 1], best[:, lane + 1 : lane + 2])
-            values = jnp.where(target == here, values, -1.0)
-            found = jnp.maximum(found, jnp.max(values, axis=0, keepdims=True))
-    out_ref[...] = found
+    here = iota((OWNERS, LOAD), 0).astype(F32)
+    best = got_ref[...]
+    found = jnp.full((OWNERS, LOAD), -1.0, F32)
+    for target, lane in ((owner, 0), (lower, 2)):
+        values = jnp.where(rank == 0.0, best[:, lane : lane + 1], best[:, lane + 1 : lane + 2])
+        found = jnp.maximum(found, jnp.where(target == here, values, -1.0))
+    out_ref[...] = jnp.max(found, axis=0, keepdims=True)
 
 
 def call(kernel, outs, scratch=(), flops=0, size=1 << 20):
@@ -228,19 +221,25 @@
     high = lax.ppermute(own, AXES, DOWN)
     core = lax.ppermute(own, AXES, C_SWAP)
     both = lax.ppermute(far, AXES, C_SWAP)
-    turn = [pltpu.VMEM((QUART, LANES), F32)] * 2
-    early, upper = call(
+    turn = [pltpu.VMEM((QUART, LANES), F32)]
+    early, over = call(
         early_kernel,
-        [shape((2 * OWNERS, LANES), F32), shape((8, QUART), F32)],
-        turn[:1],
+        [shape((OWNERS, LANES), F32), shape((8, QUART), F32)],
+        turn,
         6 * 10**8,
     )(own, far, high)
-    best = call(late_kernel, shape((4 * OWNERS, LANES), F32), turn, 6 * 10**8)(
-        own, core, both, high, early, upper
-    )
-    back = lax.all_to_all(best.reshape(4 * OWNERS, 1, LANES), AXES, 0, 0, tiled=True)
+    best, upper = call(
+        late_kernel, [shape((32, LANES), F32), shape((8, LANES), F32)], turn, 6 * 10**8
+    )(own, core, both, high, early, over)
+    met = lax.all_to_all(
+        best.reshape(4, 8, LANES), AXES, 0, 0, axis_index_groups=OWNED, tiled=True
+    )
+    best = call(merge_kernel, shape((OWNERS, LANES), F32))(met.reshape(32, LANES), upper)
+    back = lax.all_to_all(
+        best.reshape(OWNERS, 1, LANES), AXES, 0, 0, axis_index_groups=GROUPS, tiled=True
+    )
     return call(pick_kernel, shape((1, LOAD), F32))(
-        back.reshape(4 * OWNERS, LANES), place
+        back.reshape(OWNERS, LANES), place
     ).reshape(LOAD)
 
 

time: 93.1 us -> 93.1 us (level)
    all_to_all x1 -> x2, blocking collectives: 26.7 us -> 26.6 us  [the longest x1 20.3 us: body(): lax.all_to_all(best.reshape(OWNERS, 1, LANES), AXES, 0, 0, axis_index_gro...]
    pallas_call x3 -> x4, Pallas kernels: 3.04 us -> 3.15 us  [the longest x1 1.24 us: body(): call(late_kernel, [shape((32, LANES), F32), shape((8, LANES), F32)], turn...]
where the time goes in v8:
time: 93.1 us; the launch traced here: 92.8 us
  blocking collectives  66.9 us (72%)
  starting transfers between devices  16.3 us (18%)
  Pallas kernels  3.72 us (4%)
  waiting for transfers between devices  3.7 us (4%)
  local copies, waits for them, and re-layouts  2.08 us (2%)
    all_to_all x1, blocking collectives, body(): lax.all_to_all(packed.reshape(OWNERS, 2, WIDE), AXES, 0, 0, axis_index_gr...  40.3 us
    all_to_all x1, blocking collectives, body(): lax.all_to_all(best.reshape(OWNERS, 1, LANES), AXES, 0, 0, axis_index_gro...  20.3 us
    all_to_all x1, blocking collectives, body(): lax.all_to_all(best.reshape(4, 8, LANES), AXES, 0, 0, axis_index_groups=O...  6.25 us
    ppermute x1, starting transfers between devices, body(): both = lax.ppermute(far, AXES, C_SWAP)  6.23 us
    ppermute x1, starting transfers between devices, body(): core = lax.ppermute(own, AXES, C_SWAP)  6.03 us
    ppermute x1, waiting for transfers between devices, body(): far = lax.ppermute(own, AXES, X_SWAP)  3.26 us
    ppermute x1, starting transfers between devices, body(): high = lax.ppermute(own, AXES, DOWN)  2.07 us
    ppermute x1, starting transfers between devices, body(): far = lax.ppermute(own, AXES, X_SWAP)  1.92 us
  transfers between devices with their start and end apart: 4, of which 2 were waited for; matrix products, arithmetic and copies ran while one was open for 0% of the time, Pallas kernels for 1%

profile of v8, /device:TPU:1, one launch (start us, length us, event | category | flops | bytes accessed | tf_op | source)
XLA Modules:
  0.0 92.8 jit_solution(2861478192669160332)
XLA Ops:
  0.0 0.0 copy-start.1
  0.0 0.0 copy-start.2
  0.0 0.0 copy-start.3
  0.0 0.0 copy-start.4
  0.0 0.7 copy-done.1
  0.7 0.0 copy-done.2
  0.7 0.0 copy-done.3
  0.7 0.0 copy-done.4
  0.7 0.0 copy-start
  0.7 0.9 %copy-done = bf16[128,1024]{1,0:T(8,128)(2,1)S(1)} copy-done((bf16[128,1024]{1,0:T(8,128)(2,1)S(1)}, bf16[128,1024]{1,0:T(8,128)(2,1)}, u32[]{:S(2)}) %copy-start) | copy-done | bytes 262168
  1.7 0.6 shard_map.55
  2.2 0.2 reshape.33
  2.5 40.3 %all_to_all.15 = bf16[128,2,1152]{2,1,0:T(2,128)(2,1)S(1)} all-to-all(bf16[128,2,1152]{2,1,0:T(2,128)(2,1)S(1)} %reshape.33), channel_id=1, replica_groups={{0,3,8,11,16,19,24,27,32,35,40,43,48,51,56,59,64,67,72,75,80,83,88,91,9..., dimensions={0} | all-to-all | bytes 1179648 | tf_op jit(solution)/shard_map/all_to_all | solution.py:216
  42.8 0.2 reshape.34.own_ref
  43.0 1.9 %collective-permute-start.1 = (bf16[256,1152]{1,0:T(8,128)(2,1)S(1)}, bf16[256,1152]{1,0:T(8,128)(2,1)S(1)}, u32[]{:S(2)}, u32[]{:S(2)}) collective-permute-start(bf16[256,1152]{1,0:T(8,128)(2,1)S(1)} %reshape.34.own_ref), channel_id=1, source_target_pairs={{0,1},{1,0},{4,5},{5,4},{3,2},{2,3},{7,6},{6,7},{11,10},{10,11},{1... | collective-permute-start | bytes 1769480 | tf_op jit(solution)/shard_map/ppermute | solution.py:220
  44.9 2.1 %collective-permute-start.3 = (bf16[256,1152]{1,0:T(8,128)(2,1)S(1)}, bf16[256,1152]{1,0:T(8,128)(2,1)S(1)}, u32[]{:S(2)}, u32[]{:S(2)}) collective-permute-start(bf16[256,1152]{1,0:T(8,128)(2,1)S(1)} %reshape.34.own_ref), channel_id=1, source_target_pairs={{0,448},{1,449},{4,452},{5,453},{3,0},{2,1},{7,4},{6,5},{11,3},{10... | collective-permute-start | bytes 1769480 | tf_op jit(solution)/shard_map/ppermute | solution.py:221
  47.0 6.0 %collective-permute-start = (bf16[256,1152]{1,0:T(8,128)(2,1)S(1)}, bf16[256,1152]{1,0:T(8,128)(2,1)S(1)}, u32[]{:S(2)}, u32[]{:S(2)}) collective-permute-start(bf16[256,1152]{1,0:T(8,128)(2,1)S(1)} %reshape.34.own_ref), channel_id=1, source_target_pairs={{0,4},{1,5},{4,0},{5,1},{3,7},{2,6},{7,3},{6,2},{11,15},{10,14},{1... | collective-permute-start | bytes 1769480 | tf_op jit(solution)/shard_map/ppermute | solution.py:222
  53.1 3.3 %collective-permute-done.1.far_ref = bf16[256,1152]{1,0:T(8,128)(2,1)S(1)} collective-permute-done((bf16[256,1152]{1,0:T(8,128)(2,1)S(1)}, bf16[256,1152]{1,0:T(8,128)(2,1)S(1)}, u32[]{:S(2)}, u32[]{:S(2)}) %collective-permute-start.1) | collective-permute-done | bytes 589856 | tf_op jit(solution)/shard_map/ppermute | solution.py:220
  56.3 6.2 %collective-permute-start.2 = (bf16[256,1152]{1,0:T(8,128)(2,1)S(1)}, bf16[256,1152]{1,0:T(8,128)(2,1)S(1)}, u32[]{:S(2)}, u32[]{:S(2)}) collective-permute-start(bf16[256,1152]{1,0:T(8,128)(2,1)S(1)} %collective-permute-done.1.far_ref), channel_id=1, source_target_pairs={{0,4},{1,5},{4,0},{5,1},{3,7},{2,6},{7,3},{6,2},{11,15},{10,14},{1... | collective-permute-start | bytes 1769480 | tf_op jit(solution)/shard_map/ppermute | solution.py:223
  62.6 0.0 collective-permute-done.3.high_ref
  62.6 1.2 %shard_map.56 = (f32[128,128]{1,0:T(8,128)S(1)}, f32[8,256]{1,0:T(8,128)S(1)}) custom-call(bf16[256,1152]{1,0:T(8,128)(2,1)S(1)} %reshape.34.own_ref, bf16[256,1152]{1,0:T(8,128)(2,1)S(1)} %collective-permute-done.1.far_ref, bf16[256,1152]{1,0:T(8,128)(2,1)S(1)} %collective-permute-done.3.high_ref), custom_call_target="tpu_custom_call" | custom-call | flops 600000000 | bytes 1048576 | tf_op jit(solution)/shard_map/pallas_call | solution.py:225
  63.7 0.0 collective-permute-done.core_ref
  63.7 0.4 collective-permute-done.2.both_ref
  64.2 1.2 %shard_map.57 = (f32[32,128]{1,0:T(8,128)S(1)}, f32[8,128]{1,0:T(8,128)S(1)}) custom-call(bf16[256,1152]{1,0:T(8,128)(2,1)S(1)} %reshape.34.own_ref, bf16[256,1152]{1,0:T(8,128)(2,1)S(1)} %collective-permute-done.core_ref, bf16[256,1152]{1,0:T(8,128)(2,1)S(1)} %collective-permute-done.2.both_ref, bf16[256,1152]{1,0:T(8,128)(2,1)S(1)} %collective-permute-done.3.high_ref, ...), custom_call_target="tpu_custom_call" | custom-call | flops 600000000 | bytes 1048576 | tf_op jit(solution)/shard_map/pallas_call | solution.py:231
  65.4 6.3 %all_to_all.16 = f32[4,8,128]{2,1,0:T(8,128)S(1)} all-to-all(f32[4,8,128]{2,1,0:T(8,128)S(1)} %bitcast.14), channel_id=1, replica_groups={{0,1,4,5},{3,2,7,6},{11,10,15,14},{8,9,12,13},{16,17,20,21},{19,18,23,2..., dimensions={0} | all-to-all | bytes 32768 | tf_op jit(solution)/shard_map/all_to_all | solution.py:234
  71.7 0.1 shard_map.58
  71.8 20.3 %all_to_all.17 = f32[128,1,128]{2,1,0:T(1,128)S(1)} all-to-all(f32[128,1,128]{2,1,0:T(1,128)S(1)} %bitcast.12), channel_id=1, replica_groups={{0,3,8,11,16,19,24,27,32,35,40,43,48,51,56,59,64,67,72,75,80,83,88,91,9..., dimensions={0} | all-to-all | bytes 131072 | tf_op jit(solution)/shard_map/all_to_all | solution.py:238
  92.1 0.7 shard_map.59
Async XLA Ops:
  0.0 0.7 copy-start.1
  0.0 0.7 copy-start.2
  0.0 0.7 copy-start.3
  0.0 0.7 copy-start.4
  0.7 1.0 %copy-start = (bf16[128,1024]{1,0:T(8,128)(2,1)S(1)}, bf16[128,1024]{1,0:T(8,128)(2,1)}, u32[]{:S(2)}) copy-start(bf16[128,1024]{1,0:T(8,128)(2,1)} %x_ref.1) | copy-start | bytes 786436
  43.0 13.3 %collective-permute-start.1 = (bf16[256,1152]{1,0:T(8,128)(2,1)S(1)}, bf16[256,1152]{1,0:T(8,128)(2,1)S(1)}, u32[]{:S(2)}, u32[]{:S(2)}) collective-permute-start(bf16[256,1152]{1,0:T(8,128)(2,1)S(1)} %reshape.34.own_ref), channel_id=1, source_target_pairs={{0,1},{1,0},{4,5},{5,4},{3,2},{2,3},{7,6},{6,7},{11,10},{10,11},{1... | collective-permute-start | bytes 1769480 | tf_op jit(solution)/shard_map/ppermute | solution.py:220
  44.9 17.6 %collective-permute-start.3 = (bf16[256,1152]{1,0:T(8,128)(2,1)S(1)}, bf16[256,1152]{1,0:T(8,128)(2,1)S(1)}, u32[]{:S(2)}, u32[]{:S(2)}) collective-permute-start(bf16[256,1152]{1,0:T(8,128)(2,1)S(1)} %reshape.34.own_ref), channel_id=1, source_target_pairs={{0,448},{1,449},{4,452},{5,453},{3,0},{2,1},{7,4},{6,5},{11,3},{10... | collective-permute-start | bytes 1769480 | tf_op jit(solution)/shard_map/ppermute | solution.py:221
  47.0 16.7 %collective-permute-start = (bf16[256,1152]{1,0:T(8,128)(2,1)S(1)}, bf16[256,1152]{1,0:T(8,128)(2,1)S(1)}, u32[]{:S(2)}, u32[]{:S(2)}) collective-permute-start(bf16[256,1152]{1,0:T(8,128)(2,1)S(1)} %reshape.34.own_ref), channel_id=1, source_target_pairs={{0,4},{1,5},{4,0},{5,1},{3,7},{2,6},{7,3},{6,2},{11,15},{10,14},{1... | collective-permute-start | bytes 1769480 | tf_op jit(solution)/shard_map/ppermute | solution.py:222
  56.3 7.8 %collective-permute-start.2 = (bf16[256,1152]{1,0:T(8,128)(2,1)S(1)}, bf16[256,1152]{1,0:T(8,128)(2,1)S(1)}, u32[]{:S(2)}, u32[]{:S(2)}) collective-permute-start(bf16[256,1152]{1,0:T(8,128)(2,1)S(1)} %collective-permute-done.1.far_ref), channel_id=1, source_target_pairs={{0,4},{1,5},{4,0},{5,1},{3,7},{2,6},{7,3},{6,2},{11,15},{10,14},{1... | collective-permute-start | bytes 1769480 | tf_op jit(solution)/shard_map/ppermute | solution.py:223

commit v9 on v5

--- a/solution.py
+++ b/solution.py
@@ -26,8 +26,10 @@
 
 
 QUARTERS = [(core, half) for core in range(2) for half in range(2)]
-GROUPS = [[device_of(o, c, h) for o in range(OWNERS)] for c, h in QUARTERS]
-EVERY = [[device_of(o, c, h) for o in range(OWNERS) for c, h in QUARTERS]]
+GROUPS = [
+    sorted((device_of(o, c, h) for o in range(OWNERS)), reverse=c == 1) for c, h in QUARTERS
+]
+EVERY = [[group[at] for at in range(OWNERS) for group in GROUPS]]
 
 
 def moves(shift, core, half):
@@ -41,6 +43,13 @@
 X_SWAP = moves(0, 0, 1)
 C_SWAP = moves(0, 1, 0)
 DOWN = moves(-1, 0, 0)
+
+
+def rank_of(owner):
+    step = owner >> 1
+    y = step >> 3
+    z = (step & 7) ^ (7 * (y & 1))
+    return ((y * Z + z) << 1) | ((owner ^ step) & 1)
 
 
 def iota(shape, dim):
@@ -62,7 +71,9 @@
     onehot = ones_where(iota((count, LOAD), 0) == clusters)
     first, second = nbr_ref[0:1, :], nbr_ref[1:2, :]
     row = iota((16, count), 0)
-    table = jnp.where(row == 0, map_ref[...], 0)
+    owners = map_ref[...]
+    table = jnp.where(row == 0, rank_of(owners), 0)
+    table = jnp.where(row == 1, rank_of((owners + OWNERS - 1) & (OWNERS - 1)), table)
     for at, value in enumerate((first >> 8, first & 255, second >> 8, second & 255)):
         table = jnp.where(row == 4 + at, value, table)
     looked = jnp.dot(table.astype(F32).astype(BF16), onehot, preferred_element_type=F32)
@@ -83,12 +94,13 @@
     unit = (scaled * factor).astype(BF16)
 
     slot = iota((QUART, LOAD), 0)
-    pick = (owner == (slot >> 1).astype(F32)) & (rank == (slot & 1).astype(F32))
+    target = (slot >> 1) ^ ((lax.axis_index("shard") & 1) * (OWNERS - 1))
+    pick = (owner == target.astype(F32)) & (rank == (slot & 1).astype(F32))
     pick = ones_where(pick)
     out_ref[:, 0:D] = jnp.dot(pick, unit, preferred_element_type=F32).astype(BF16)
     out_ref[:, D:WIDE] = nt(pick, meta).astype(BF16)
     row = iota((8, LOAD), 0)
-    place_ref[...] = jnp.where(row == 0, owner, rank)
+    place_ref[...] = jnp.where(row == 0, owner, jnp.where(row == 1, looked[1:2, :], rank))
 
 
 def key_meta(key_ref):
@@ -166,18 +178,19 @@
 
 
 def pick_kernel(got_ref, place_ref, out_ref):
-    best = got_ref[pl.ds(0, OWNERS, stride=4), :]
-    for q in range(1, 4):
-        best = jnp.maximum(best, got_ref[pl.ds(q, OWNERS, stride=4), :])
-    owner, rank = place_ref[0:1, :], place_ref[1:2, :]
-    mine = owner == iota((OWNERS, LOAD), 0).astype(F32)
-    lower = pltpu.roll(best, 1, 0)
-    values = jnp.where(
-        rank == 0.0,
-        jnp.maximum(best[:, 0:1], lower[:, 2:3]),
-        jnp.maximum(best[:, 1:2], lower[:, 3:4]),
-    )
-    out_ref[...] = jnp.max(jnp.where(mine, values, -2.0), axis=0, keepdims=True)
+    owner, lower, rank = place_ref[0:1, :], place_ref[1:2, :], place_ref[2:3, :]
+    at = iota((OWNERS, LOAD), 0)
+    found = jnp.full((OWNERS, LOAD), -1.0, F32)
+    for core in range(2):
+        best = jnp.maximum(
+            got_ref[pl.ds(2 * core, OWNERS, stride=4), :],
+            got_ref[pl.ds(2 * core + 1, OWNERS, stride=4), :],
+        )
+        here = (at ^ (core * (OWNERS - 1))).astype(F32)
+        for target, lane in ((owner, 0), (lower, 2)):
+            values = jnp.where(rank == 0.0, best[:, lane : lane + 1], best[:, lane + 1 : lane + 2])
+            found = jnp.maximum(found, jnp.where(target == here, values, -1.0))
+    out_ref[...] = jnp.max(found, axis=0, keepdims=True)
 
 
 def call(kernel, outs, scratch=(), flops=0, size=1 << 20):

time: 94.5 us -> 91.8 us (0.971)
  blocking collectives: 68.4 us -> 65.7 us
  starting transfers between devices: 16.6 us -> 15.2 us
  waiting for transfers between devices: 3.32 us -> 4.72 us
    all_to_all x1, blocking collectives: 41.1 us -> 36.7 us  [body(): lax.all_to_all(packed.reshape(OWNERS, 2, WIDE), AXES, 0, 0, axis_index_gr...]
    all_to_all x1, blocking collectives: 27.3 us -> 29 us  [body(): lax.all_to_all(best.reshape(4 * OWNERS, 1, LANES), AXES, 0, 0, axis_index...]
    ppermute x1, waiting for transfers between devices: 2.87 us -> 4.27 us  [body(): far = lax.ppermute(own, AXES, X_SWAP)]
    ppermute x1, starting transfers between devices: 3.03 us -> 1.92 us  [body(): high = lax.ppermute(own, AXES, DOWN)]
    ppermute x1, starting transfers between devices: 6.14 us -> 5.08 us  [body(): both = lax.ppermute(far, AXES, C_SWAP)]
where the time goes in v9:
time: 91.8 us; the launch traced here: 91.5 us
  blocking collectives  65.7 us (72%)
  starting transfers between devices  15.2 us (17%)
  waiting for transfers between devices  4.72 us (5%)
  Pallas kernels  3.67 us (4%)
  local copies, waits for them, and re-layouts  2.08 us (2%)
    all_to_all x1, blocking collectives, body(): lax.all_to_all(packed.reshape(OWNERS, 2, WIDE), AXES, 0, 0, axis_index_gr...  36.7 us
    all_to_all x1, blocking collectives, body(): lax.all_to_all(best.reshape(4 * OWNERS, 1, LANES), AXES, 0, 0, axis_index...  29 us
    ppermute x1, starting transfers between devices, body(): core = lax.ppermute(own, AXES, C_SWAP)  6.32 us
    ppermute x1, starting transfers between devices, body(): both = lax.ppermute(far, AXES, C_SWAP)  5.08 us
    ppermute x1, waiting for transfers between devices, body(): far = lax.ppermute(own, AXES, X_SWAP)  4.27 us
    ppermute x1, starting transfers between devices, body(): far = lax.ppermute(own, AXES, X_SWAP)  1.92 us
    ppermute x1, starting transfers between devices, body(): high = lax.ppermute(own, AXES, DOWN)  1.92 us
  transfers between devices with their start and end apart: 4, of which 2 were waited for; matrix products, arithmetic and copies ran while one was open for 0% of the time, Pallas kernels for 1%

profile of v9, /device:TPU:1, one launch (start us, length us, event | category | flops | bytes accessed | tf_op | source)
XLA Modules:
  0.0 91.5 jit_solution(8737341592679592308)
XLA Ops:
  0.0 0.0 copy-start.1
  0.0 0.0 copy-start.2
  0.0 0.0 copy-start.3
  0.0 0.0 copy-start.4
  0.0 0.7 copy-done.1
  0.7 0.0 copy-done.2
  0.7 0.0 copy-done.3
  0.7 0.0 copy-done.4
  0.7 0.0 copy-start
  0.7 0.9 %copy-done = bf16[128,1024]{1,0:T(8,128)(2,1)S(1)} copy-done((bf16[128,1024]{1,0:T(8,128)(2,1)S(1)}, bf16[128,1024]{1,0:T(8,128)(2,1)}, u32[]{:S(2)}) %copy-start) | copy-done | bytes 262168
  1.7 0.6 shard_map.55
  2.2 0.2 reshape.27
  2.5 36.7 %all_to_all.10 = bf16[128,2,1152]{2,1,0:T(2,128)(2,1)S(1)} all-to-all(bf16[128,2,1152]{2,1,0:T(2,128)(2,1)S(1)} %reshape.27), channel_id=1, replica_groups={{0,3,8,11,16,19,24,27,32,35,40,43,48,51,56,59,64,67,72,75,80,83,88,91,9..., dimensions={0} | all-to-all | bytes 1179648 | tf_op jit(solution)/shard_map/all_to_all | solution.py:220
  39.1 0.2 reshape.28.own_ref
  39.4 1.9 %collective-permute-start.1 = (bf16[256,1152]{1,0:T(8,128)(2,1)S(1)}, bf16[256,1152]{1,0:T(8,128)(2,1)S(1)}, u32[]{:S(2)}, u32[]{:S(2)}) collective-permute-start(bf16[256,1152]{1,0:T(8,128)(2,1)S(1)} %reshape.28.own_ref), channel_id=1, source_target_pairs={{0,1},{1,0},{4,5},{5,4},{3,2},{2,3},{7,6},{6,7},{11,10},{10,11},{1... | collective-permute-start | bytes 1769480 | tf_op jit(solution)/shard_map/ppermute | solution.py:224
  41.3 1.9 %collective-permute-start.3 = (bf16[256,1152]{1,0:T(8,128)(2,1)S(1)}, bf16[256,1152]{1,0:T(8,128)(2,1)S(1)}, u32[]{:S(2)}, u32[]{:S(2)}) collective-permute-start(bf16[256,1152]{1,0:T(8,128)(2,1)S(1)} %reshape.28.own_ref), channel_id=1, source_target_pairs={{0,448},{1,449},{4,452},{5,453},{3,0},{2,1},{7,4},{6,5},{11,3},{10... | collective-permute-start | bytes 1769480 | tf_op jit(solution)/shard_map/ppermute | solution.py:225
  43.2 6.3 %collective-permute-start = (bf16[256,1152]{1,0:T(8,128)(2,1)S(1)}, bf16[256,1152]{1,0:T(8,128)(2,1)S(1)}, u32[]{:S(2)}, u32[]{:S(2)}) collective-permute-start(bf16[256,1152]{1,0:T(8,128)(2,1)S(1)} %reshape.28.own_ref), channel_id=1, source_target_pairs={{0,4},{1,5},{4,0},{5,1},{3,7},{2,6},{7,3},{6,2},{11,15},{10,14},{1... | collective-permute-start | bytes 1769480 | tf_op jit(solution)/shard_map/ppermute | solution.py:226
  49.5 4.3 %collective-permute-done.1.far_ref = bf16[256,1152]{1,0:T(8,128)(2,1)S(1)} collective-permute-done((bf16[256,1152]{1,0:T(8,128)(2,1)S(1)}, bf16[256,1152]{1,0:T(8,128)(2,1)S(1)}, u32[]{:S(2)}, u32[]{:S(2)}) %collective-permute-start.1) | collective-permute-done | bytes 589856 | tf_op jit(solution)/shard_map/ppermute | solution.py:224
  53.8 5.1 %collective-permute-start.2 = (bf16[256,1152]{1,0:T(8,128)(2,1)S(1)}, bf16[256,1152]{1,0:T(8,128)(2,1)S(1)}, u32[]{:S(2)}, u32[]{:S(2)}) collective-permute-start(bf16[256,1152]{1,0:T(8,128)(2,1)S(1)} %collective-permute-done.1.far_ref), channel_id=1, source_target_pairs={{0,4},{1,5},{4,0},{5,1},{3,7},{2,6},{7,3},{6,2},{11,15},{10,14},{1... | collective-permute-start | bytes 1769480 | tf_op jit(solution)/shard_map/ppermute | solution.py:227
  58.9 0.0 collective-permute-done.3.high_ref
  58.9 1.1 %shard_map.56 = (f32[256,128]{1,0:T(8,128)S(1)}, f32[8,256]{1,0:T(8,128)S(1)}) custom-call(bf16[256,1152]{1,0:T(8,128)(2,1)S(1)} %reshape.28.own_ref, bf16[256,1152]{1,0:T(8,128)(2,1)S(1)} %collective-permute-done.1.far_ref, bf16[256,1152]{1,0:T(8,128)(2,1)S(1)} %collective-permute-done.3.high_ref), custom_call_target="tpu_custom_call" | custom-call | flops 600000000 | bytes 1048576 | tf_op jit(solution)/shard_map/pallas_call | solution.py:229
  60.1 0.0 collective-permute-done.core_ref
  60.1 0.4 collective-permute-done.2.both_ref
  60.5 1.2 %shard_map.57 = f32[512,128]{1,0:T(8,128)S(1)} custom-call(bf16[256,1152]{1,0:T(8,128)(2,1)S(1)} %reshape.28.own_ref, bf16[256,1152]{1,0:T(8,128)(2,1)S(1)} %collective-permute-done.core_ref, bf16[256,1152]{1,0:T(8,128)(2,1)S(1)} %collective-permute-done.2.both_ref, bf16[256,1152]{1,0:T(8,128)(2,1)S(1)} %collective-permute-done.3.high_ref, ...), custom_call_target="tpu_custom_call" | custom-call | flops 600000000 | bytes 1048576 | tf_op jit(solution)/shard_map/pallas_call | solution.py:235
  61.7 29.0 %all_to_all.11 = f32[512,1,128]{2,1,0:T(1,128)S(1)} all-to-all(f32[512,1,128]{2,1,0:T(1,128)S(1)} %bitcast.10), channel_id=1, replica_groups={{0,1,511,510,3,2,508,509,8,9,503,502,11,10,500,501,16,17,495,494,19,18,..., dimensions={0} | all-to-all | bytes 524288 | tf_op jit(solution)/shard_map/all_to_all | solution.py:238
  90.7 0.7 shard_map.58
Async XLA Ops:
  0.0 0.7 copy-start.1
  0.0 0.7 copy-start.2
  0.0 0.7 copy-start.3
  0.0 0.7 copy-start.4
  0.7 1.0 %copy-start = (bf16[128,1024]{1,0:T(8,128)(2,1)S(1)}, bf16[128,1024]{1,0:T(8,128)(2,1)}, u32[]{:S(2)}) copy-start(bf16[128,1024]{1,0:T(8,128)(2,1)} %x_ref.1) | copy-start | bytes 786436
  39.4 14.4 %collective-permute-start.1 = (bf16[256,1152]{1,0:T(8,128)(2,1)S(1)}, bf16[256,1152]{1,0:T(8,128)(2,1)S(1)}, u32[]{:S(2)}, u32[]{:S(2)}) collective-permute-start(bf16[256,1152]{1,0:T(8,128)(2,1)S(1)} %reshape.28.own_ref), channel_id=1, source_target_pairs={{0,1},{1,0},{4,5},{5,4},{3,2},{2,3},{7,6},{6,7},{11,10},{10,11},{1... | collective-permute-start | bytes 1769480 | tf_op jit(solution)/shard_map/ppermute | solution.py:224
  41.3 17.6 %collective-permute-start.3 = (bf16[256,1152]{1,0:T(8,128)(2,1)S(1)}, bf16[256,1152]{1,0:T(8,128)(2,1)S(1)}, u32[]{:S(2)}, u32[]{:S(2)}) collective-permute-start(bf16[256,1152]{1,0:T(8,128)(2,1)S(1)} %reshape.28.own_ref), channel_id=1, source_target_pairs={{0,448},{1,449},{4,452},{5,453},{3,0},{2,1},{7,4},{6,5},{11,3},{10... | collective-permute-start | bytes 1769480 | tf_op jit(solution)/shard_map/ppermute | solution.py:225
  43.2 16.8 %collective-permute-start = (bf16[256,1152]{1,0:T(8,128)(2,1)S(1)}, bf16[256,1152]{1,0:T(8,128)(2,1)S(1)}, u32[]{:S(2)}, u32[]{:S(2)}) collective-permute-start(bf16[256,1152]{1,0:T(8,128)(2,1)S(1)} %reshape.28.own_ref), channel_id=1, source_target_pairs={{0,4},{1,5},{4,0},{5,1},{3,7},{2,6},{7,3},{6,2},{11,15},{10,14},{1... | collective-permute-start | bytes 1769480 | tf_op jit(solution)/shard_map/ppermute | solution.py:226
  53.8 6.7 %collective-permute-start.2 = (bf16[256,1152]{1,0:T(8,128)(2,1)S(1)}, bf16[256,1152]{1,0:T(8,128)(2,1)S(1)}, u32[]{:S(2)}, u32[]{:S(2)}) collective-permute-start(bf16[256,1152]{1,0:T(8,128)(2,1)S(1)} %collective-permute-done.1.far_ref), channel_id=1, source_target_pairs={{0,4},{1,5},{4,0},{5,1},{3,7},{2,6},{7,3},{6,2},{11,15},{10,14},{1... | collective-permute-start | bytes 1769480 | tf_op jit(solution)/shard_map/ppermute | solution.py:227

commit v10 on v8

--- a/solution.py
+++ b/solution.py
@@ -27,7 +27,9 @@
 
 QUARTERS = [(core, half) for core in range(2) for half in range(2)]
 OWNED = [[device_of(o, c, h) for c, h in QUARTERS] for o in range(OWNERS)]
-GROUPS = [sorted(device_of(o, c, h) for o in range(OWNERS)) for c, h in QUARTERS]
+GROUPS = [
+    sorted((device_of(o, c, h) for o in range(OWNERS)), reverse=c == 1) for c, h in QUARTERS
+]
 
 
 def moves(shift, core, half):
@@ -48,6 +50,10 @@
     y = step >> 3
     z = (step & 7) ^ (7 * (y & 1))
     return ((y * Z + z) << 1) | ((owner ^ step) & 1)
+
+
+def turned():
+    return (lax.axis_index("shard") & 1) * (OWNERS - 1)
 
 
 def iota(shape, dim):
@@ -92,7 +98,8 @@
     unit = (scaled * factor).astype(BF16)
 
     slot = iota((QUART, LOAD), 0)
-    pick = (owner == (slot >> 1).astype(F32)) & (rank == (slot & 1).astype(F32))
+    target = (slot >> 1) ^ turned()
+    pick = (owner == target.astype(F32)) & (rank == (slot & 1).astype(F32))
     pick = ones_where(pick)
     out_ref[:, 0:D] = jnp.dot(pick, unit, preferred_element_type=F32).astype(BF16)
     out_ref[:, D:WIDE] = nt(pick, meta).astype(BF16)
@@ -180,7 +187,7 @@
 
 def pick_kernel(got_ref, place_ref, out_ref):
     owner, lower, rank = place_ref[0:1, :], place_ref[1:2, :], place_ref[2:3, :]
-    here = iota((OWNERS, LOAD), 0).astype(F32)
+    here = (iota((OWNERS, LOAD), 0) ^ turned()).astype(F32)
     best = got_ref[...]
     found = jnp.full((OWNERS, LOAD), -1.0, F32)
     for target, lane in ((owner, 0), (lower, 2)):

time: 93.1 us -> 91.6 us (0.984)
  the two profiles are of different devices: /device:TPU:1 before, /device:TPU:8 now
where the time goes in v10:
time: 91.6 us; the launch traced here: 91.2 us
  blocking collectives  67.8 us (74%)
  starting transfers between devices  9.66 us (11%)
  waiting for transfers between devices  7.91 us (9%)
  Pallas kernels  3.72 us (4%)
  local copies, waits for them, and re-layouts  2.08 us (2%)
    all_to_all x1, blocking collectives, body(): lax.all_to_all(packed.reshape(OWNERS, 2, WIDE), AXES, 0, 0, axis_index_gr...  36.8 us
    all_to_all x1, blocking collectives, body(): lax.all_to_all(best.reshape(OWNERS, 1, LANES), AXES, 0, 0, axis_index_gro...  24.8 us
    ppermute x1, waiting for transfers between devices, body(): far = lax.ppermute(own, AXES, X_SWAP)  7.09 us
    all_to_all x1, blocking collectives, body(): lax.all_to_all(best.reshape(4, 8, LANES), AXES, 0, 0, axis_index_groups=O...  6.2 us
    ppermute x1, starting transfers between devices, body(): high = lax.ppermute(own, AXES, DOWN)  3.91 us
    ppermute x1, starting transfers between devices, body(): far = lax.ppermute(own, AXES, X_SWAP)  1.92 us
    ppermute x1, starting transfers between devices, body(): core = lax.ppermute(own, AXES, C_SWAP)  1.92 us
    ppermute x1, starting transfers between devices, body(): both = lax.ppermute(far, AXES, C_SWAP)  1.91 us
  transfers between devices with their start and end apart: 4, of which 2 were waited for; matrix products, arithmetic and copies ran while one was open for 0% of the time, Pallas kernels for 1%

profile of v10, /device:TPU:8, one launch (start us, length us, event | category | flops | bytes accessed | tf_op | source)
XLA Modules:
  0.0 91.2 jit_solution(4908924554308979592)
XLA Ops:
  0.0 0.0 copy-start.1
  0.0 0.0 copy-start.2
  0.0 0.0 copy-start.3
  0.0 0.0 copy-start.4
  0.0 0.7 copy-done.1
  0.7 0.0 copy-done.2
  0.7 0.0 copy-done.3
  0.7 0.0 copy-done.4
  0.7 0.0 copy-start
  0.7 0.9 %copy-done = bf16[128,1024]{1,0:T(8,128)(2,1)S(1)} copy-done((bf16[128,1024]{1,0:T(8,128)(2,1)S(1)}, bf16[128,1024]{1,0:T(8,128)(2,1)}, u32[]{:S(2)}) %copy-start) | copy-done | bytes 262168
  1.7 0.6 shard_map.55
  2.2 0.2 reshape.33
  2.5 36.8 %all_to_all.15 = bf16[128,2,1152]{2,1,0:T(2,128)(2,1)S(1)} all-to-all(bf16[128,2,1152]{2,1,0:T(2,128)(2,1)S(1)} %reshape.33), channel_id=1, replica_groups={{0,3,8,11,16,19,24,27,32,35,40,43,48,51,56,59,64,67,72,75,80,83,88,91,9..., dimensions={0} | all-to-all | bytes 1179648 | tf_op jit(solution)/shard_map/all_to_all | solution.py:223
  39.2 0.2 reshape.34.own_ref
  39.5 1.9 %collective-permute-start.1 = (bf16[256,1152]{1,0:T(8,128)(2,1)S(1)}, bf16[256,1152]{1,0:T(8,128)(2,1)S(1)}, u32[]{:S(2)}, u32[]{:S(2)}) collective-permute-start(bf16[256,1152]{1,0:T(8,128)(2,1)S(1)} %reshape.34.own_ref), channel_id=1, source_target_pairs={{0,1},{1,0},{4,5},{5,4},{3,2},{2,3},{7,6},{6,7},{11,10},{10,11},{1... | collective-permute-start | bytes 1769480 | tf_op jit(solution)/shard_map/ppermute | solution.py:227
  41.4 3.9 %collective-permute-start.3 = (bf16[256,1152]{1,0:T(8,128)(2,1)S(1)}, bf16[256,1152]{1,0:T(8,128)(2,1)S(1)}, u32[]{:S(2)}, u32[]{:S(2)}) collective-permute-start(bf16[256,1152]{1,0:T(8,128)(2,1)S(1)} %reshape.34.own_ref), channel_id=1, source_target_pairs={{0,448},{1,449},{4,452},{5,453},{3,0},{2,1},{7,4},{6,5},{11,3},{10... | collective-permute-start | bytes 1769480 | tf_op jit(solution)/shard_map/ppermute | solution.py:228
  45.3 1.9 %collective-permute-start = (bf16[256,1152]{1,0:T(8,128)(2,1)S(1)}, bf16[256,1152]{1,0:T(8,128)(2,1)S(1)}, u32[]{:S(2)}, u32[]{:S(2)}) collective-permute-start(bf16[256,1152]{1,0:T(8,128)(2,1)S(1)} %reshape.34.own_ref), channel_id=1, source_target_pairs={{0,4},{1,5},{4,0},{5,1},{3,7},{2,6},{7,3},{6,2},{11,15},{10,14},{1... | collective-permute-start | bytes 1769480 | tf_op jit(solution)/shard_map/ppermute | solution.py:229
  47.2 7.1 %collective-permute-done.1.far_ref = bf16[256,1152]{1,0:T(8,128)(2,1)S(1)} collective-permute-done((bf16[256,1152]{1,0:T(8,128)(2,1)S(1)}, bf16[256,1152]{1,0:T(8,128)(2,1)S(1)}, u32[]{:S(2)}, u32[]{:S(2)}) %collective-permute-start.1) | collective-permute-done | bytes 589856 | tf_op jit(solution)/shard_map/ppermute | solution.py:227
  54.3 1.9 %collective-permute-start.2 = (bf16[256,1152]{1,0:T(8,128)(2,1)S(1)}, bf16[256,1152]{1,0:T(8,128)(2,1)S(1)}, u32[]{:S(2)}, u32[]{:S(2)}) collective-permute-start(bf16[256,1152]{1,0:T(8,128)(2,1)S(1)} %collective-permute-done.1.far_ref), channel_id=1, source_target_pairs={{0,4},{1,5},{4,0},{5,1},{3,7},{2,6},{7,3},{6,2},{11,15},{10,14},{1... | collective-permute-start | bytes 1769480 | tf_op jit(solution)/shard_map/ppermute | solution.py:230
  56.3 0.0 collective-permute-done.3.high_ref
  56.3 1.1 %shard_map.56 = (f32[128,128]{1,0:T(8,128)S(1)}, f32[8,256]{1,0:T(8,128)S(1)}) custom-call(bf16[256,1152]{1,0:T(8,128)(2,1)S(1)} %reshape.34.own_ref, bf16[256,1152]{1,0:T(8,128)(2,1)S(1)} %collective-permute-done.1.far_ref, bf16[256,1152]{1,0:T(8,128)(2,1)S(1)} %collective-permute-done.3.high_ref), custom_call_target="tpu_custom_call" | custom-call | flops 600000000 | bytes 1048576 | tf_op jit(solution)/shard_map/pallas_call | solution.py:232
  57.4 0.0 collective-permute-done.core_ref
  57.4 0.8 collective-permute-done.2.both_ref
  58.2 1.2 %shard_map.57 = (f32[32,128]{1,0:T(8,128)S(1)}, f32[8,128]{1,0:T(8,128)S(1)}) custom-call(bf16[256,1152]{1,0:T(8,128)(2,1)S(1)} %reshape.34.own_ref, bf16[256,1152]{1,0:T(8,128)(2,1)S(1)} %collective-permute-done.core_ref, bf16[256,1152]{1,0:T(8,128)(2,1)S(1)} %collective-permute-done.2.both_ref, bf16[256,1152]{1,0:T(8,128)(2,1)S(1)} %collective-permute-done.3.high_ref, ...), custom_call_target="tpu_custom_call" | custom-call | flops 600000000 | bytes 1048576 | tf_op jit(solution)/shard_map/pallas_call | solution.py:238
  59.5 6.2 %all_to_all.16 = f32[4,8,128]{2,1,0:T(8,128)S(1)} all-to-all(f32[4,8,128]{2,1,0:T(8,128)S(1)} %bitcast.14), channel_id=1, replica_groups={{0,1,4,5},{3,2,7,6},{11,10,15,14},{8,9,12,13},{16,17,20,21},{19,18,23,2..., dimensions={0} | all-to-all | bytes 32768 | tf_op jit(solution)/shard_map/all_to_all | solution.py:241
  65.7 0.1 shard_map.58
  65.8 24.8 %all_to_all.17 = f32[128,1,128]{2,1,0:T(1,128)S(1)} all-to-all(f32[128,1,128]{2,1,0:T(1,128)S(1)} %bitcast.12), channel_id=1, replica_groups={{0,3,8,11,16,19,24,27,32,35,40,43,48,51,56,59,64,67,72,75,80,83,88,91,9..., dimensions={0} | all-to-all | bytes 131072 | tf_op jit(solution)/shard_map/all_to_all | solution.py:245
  90.6 0.7 shard_map.59
Async XLA Ops:
  0.0 0.7 copy-start.1
  0.0 0.7 copy-start.2
  0.0 0.7 copy-start.3
  0.0 0.7 copy-start.4
  0.7 1.0 %copy-start = (bf16[128,1024]{1,0:T(8,128)(2,1)S(1)}, bf16[128,1024]{1,0:T(8,128)(2,1)}, u32[]{:S(2)}) copy-start(bf16[128,1024]{1,0:T(8,128)(2,1)} %x_ref.1) | copy-start | bytes 786436
  39.5 14.9 %collective-permute-start.1 = (bf16[256,1152]{1,0:T(8,128)(2,1)S(1)}, bf16[256,1152]{1,0:T(8,128)(2,1)S(1)}, u32[]{:S(2)}, u32[]{:S(2)}) collective-permute-start(bf16[256,1152]{1,0:T(8,128)(2,1)S(1)} %reshape.34.own_ref), channel_id=1, source_target_pairs={{0,1},{1,0},{4,5},{5,4},{3,2},{2,3},{7,6},{6,7},{11,10},{10,11},{1... | collective-permute-start | bytes 1769480 | tf_op jit(solution)/shard_map/ppermute | solution.py:227
  41.4 14.9 %collective-permute-start.3 = (bf16[256,1152]{1,0:T(8,128)(2,1)S(1)}, bf16[256,1152]{1,0:T(8,128)(2,1)S(1)}, u32[]{:S(2)}, u32[]{:S(2)}) collective-permute-start(bf16[256,1152]{1,0:T(8,128)(2,1)S(1)} %reshape.34.own_ref), channel_id=1, source_target_pairs={{0,448},{1,449},{4,452},{5,453},{3,0},{2,1},{7,4},{6,5},{11,3},{10... | collective-permute-start | bytes 1769480 | tf_op jit(solution)/shard_map/ppermute | solution.py:228
  45.3 12.1 %collective-permute-start = (bf16[256,1152]{1,0:T(8,128)(2,1)S(1)}, bf16[256,1152]{1,0:T(8,128)(2,1)S(1)}, u32[]{:S(2)}, u32[]{:S(2)}) collective-permute-start(bf16[256,1152]{1,0:T(8,128)(2,1)S(1)} %reshape.34.own_ref), channel_id=1, source_target_pairs={{0,4},{1,5},{4,0},{5,1},{3,7},{2,6},{7,3},{6,2},{11,15},{10,14},{1... | collective-permute-start | bytes 1769480 | tf_op jit(solution)/shard_map/ppermute | solution.py:229
  54.3 3.9 %collective-permute-start.2 = (bf16[256,1152]{1,0:T(8,128)(2,1)S(1)}, bf16[256,1152]{1,0:T(8,128)(2,1)S(1)}, u32[]{:S(2)}, u32[]{:S(2)}) collective-permute-start(bf16[256,1152]{1,0:T(8,128)(2,1)S(1)} %collective-permute-done.1.far_ref), channel_id=1, source_target_pairs={{0,4},{1,5},{4,0},{5,1},{3,7},{2,6},{7,3},{6,2},{11,15},{10,14},{1... | collective-permute-start | bytes 1769480 | tf_op jit(solution)/shard_map/ppermute | solution.py:230

commit v11 on v8

--- a/solution.py
+++ b/solution.py
@@ -27,7 +27,20 @@
 
 QUARTERS = [(core, half) for core in range(2) for half in range(2)]
 OWNED = [[device_of(o, c, h) for c, h in QUARTERS] for o in range(OWNERS)]
-GROUPS = [sorted(device_of(o, c, h) for o in range(OWNERS)) for c, h in QUARTERS]
+
+
+def rank_of(owner, core):
+    step = owner >> 1
+    y = step >> 3
+    z = (step & 7) ^ (7 * (y & 1))
+    major, minor = y + core * (z - y), z + core * (y - z)
+    return (((major * Z + minor) << 1) | ((owner ^ step) & 1)) ^ (core * (OWNERS - 1))
+
+
+GROUPS = [
+    [device_of(o, c, h) for o in sorted(range(OWNERS), key=lambda o, c=c: rank_of(o, c))]
+    for c, h in QUARTERS
+]
 
 
 def moves(shift, core, half):
@@ -41,13 +54,6 @@
 X_SWAP = moves(0, 0, 1)
 C_SWAP = moves(0, 1, 0)
 DOWN = moves(-1, 0, 0)
-
-
-def rank_of(owner):
-    step = owner >> 1
-    y = step >> 3
-    z = (step & 7) ^ (7 * (y & 1))
-    return ((y * Z + z) << 1) | ((owner ^ step) & 1)
 
 
 def iota(shape, dim):
@@ -70,8 +76,9 @@
     first, second = nbr_ref[0:1, :], nbr_ref[1:2, :]
     row = iota((16, count), 0)
     owners = map_ref[...]
-    table = jnp.where(row == 0, rank_of(owners), 0)
-    table = jnp.where(row == 1, rank_of((owners + OWNERS - 1) & (OWNERS - 1)), table)
+    core = lax.axis_index("shard") & 1
+    table = jnp.where(row == 0, rank_of(owners, core), 0)
+    table = jnp.where(row == 1, rank_of((owners + OWNERS - 1) & (OWNERS - 1), core), table)
     for at, value in enumerate((first >> 8, first & 255, second >> 8, second & 255)):
         table = jnp.where(row == 4 + at, value, table)
     looked = jnp.dot(table.astype(F32).astype(BF16), onehot, preferred_element_type=F32)
@@ -92,7 +99,8 @@
     unit = (scaled * factor).astype(BF16)
 
     slot = iota((QUART, LOAD), 0)
-    pick = (owner == (slot >> 1).astype(F32)) & (rank == (slot & 1).astype(F32))
+    target = slot >> 1
+    pick = (owner == target.astype(F32)) & (rank == (slot & 1).astype(F32))
     pick = ones_where(pick)
     out_ref[:, 0:D] = jnp.dot(pick, unit, preferred_element_type=F32).astype(BF16)
     out_ref[:, D:WIDE] = nt(pick, meta).astype(BF16)

time: 93.1 us -> 91.4 us (0.982)
  the two profiles are of different devices: /device:TPU:1 before, /device:TPU:8 now
where the time goes in v11:
time: 91.4 us; the launch traced here: 91.1 us
  blocking collectives  68.7 us (75%)
  starting transfers between devices  9.56 us (10%)
  waiting for transfers between devices  6.87 us (8%)
  Pallas kernels  3.72 us (4%)
  local copies, waits for them, and re-layouts  2.08 us (2%)
    all_to_all x1, blocking collectives, body(): lax.all_to_all(packed.reshape(OWNERS, 2, WIDE), AXES, 0, 0, axis_index_gr...  36.7 us
    all_to_all x1, blocking collectives, body(): lax.all_to_all(best.reshape(OWNERS, 1, LANES), AXES, 0, 0, axis_index_gro...  25.8 us
    all_to_all x1, blocking collectives, body(): lax.all_to_all(best.reshape(4, 8, LANES), AXES, 0, 0, axis_index_groups=O...  6.2 us
    ppermute x1, waiting for transfers between devices, body(): far = lax.ppermute(own, AXES, X_SWAP)  6.04 us
    ppermute x1, starting transfers between devices, body(): high = lax.ppermute(own, AXES, DOWN)  3.81 us
    ppermute x1, starting transfers between devices, body(): far = lax.ppermute(own, AXES, X_SWAP)  1.92 us
    ppermute x1, starting transfers between devices, body(): core = lax.ppermute(own, AXES, C_SWAP)  1.92 us
    ppermute x1, starting transfers between devices, body(): both = lax.ppermute(far, AXES, C_SWAP)  1.91 us
  transfers between devices with their start and end apart: 4, of which 3 were waited for; matrix products, arithmetic and copies ran while one was open for 0% of the time, Pallas kernels for 1%

profile of v11, /device:TPU:8, one launch (start us, length us, event | category | flops | bytes accessed | tf_op | source)
XLA Modules:
  0.0 91.1 jit_solution(1829090572932429541)
XLA Ops:
  0.0 0.0 copy-start.1
  0.0 0.0 copy-start.2
  0.0 0.0 copy-start.3
  0.0 0.0 copy-start.4
  0.0 0.7 copy-done.1
  0.7 0.0 copy-done.2
  0.7 0.0 copy-done.3
  0.7 0.0 copy-done.4
  0.7 0.0 copy-start
  0.7 0.9 %copy-done = bf16[128,1024]{1,0:T(8,128)(2,1)S(1)} copy-done((bf16[128,1024]{1,0:T(8,128)(2,1)S(1)}, bf16[128,1024]{1,0:T(8,128)(2,1)}, u32[]{:S(2)}) %copy-start) | copy-done | bytes 262168
  1.7 0.6 shard_map.55
  2.2 0.2 reshape.33
  2.5 36.7 %all_to_all.15 = bf16[128,2,1152]{2,1,0:T(2,128)(2,1)S(1)} all-to-all(bf16[128,2,1152]{2,1,0:T(2,128)(2,1)S(1)} %reshape.33), channel_id=1, replica_groups={{0,3,8,11,16,19,24,27,32,35,40,43,48,51,56,59,64,67,72,75,80,83,88,91,9..., dimensions={0} | all-to-all | bytes 1179648 | tf_op jit(solution)/shard_map/all_to_all | solution.py:224
  39.2 0.2 reshape.34.own_ref
  39.4 1.9 %collective-permute-start.1 = (bf16[256,1152]{1,0:T(8,128)(2,1)S(1)}, bf16[256,1152]{1,0:T(8,128)(2,1)S(1)}, u32[]{:S(2)}, u32[]{:S(2)}) collective-permute-start(bf16[256,1152]{1,0:T(8,128)(2,1)S(1)} %reshape.34.own_ref), channel_id=1, source_target_pairs={{0,1},{1,0},{4,5},{5,4},{3,2},{2,3},{7,6},{6,7},{11,10},{10,11},{1... | collective-permute-start | bytes 1769480 | tf_op jit(solution)/shard_map/ppermute | solution.py:228
  41.4 3.8 %collective-permute-start.3 = (bf16[256,1152]{1,0:T(8,128)(2,1)S(1)}, bf16[256,1152]{1,0:T(8,128)(2,1)S(1)}, u32[]{:S(2)}, u32[]{:S(2)}) collective-permute-start(bf16[256,1152]{1,0:T(8,128)(2,1)S(1)} %reshape.34.own_ref), channel_id=1, source_target_pairs={{0,448},{1,449},{4,452},{5,453},{3,0},{2,1},{7,4},{6,5},{11,3},{10... | collective-permute-start | bytes 1769480 | tf_op jit(solution)/shard_map/ppermute | solution.py:229
  45.2 1.9 %collective-permute-start = (bf16[256,1152]{1,0:T(8,128)(2,1)S(1)}, bf16[256,1152]{1,0:T(8,128)(2,1)S(1)}, u32[]{:S(2)}, u32[]{:S(2)}) collective-permute-start(bf16[256,1152]{1,0:T(8,128)(2,1)S(1)} %reshape.34.own_ref), channel_id=1, source_target_pairs={{0,4},{1,5},{4,0},{5,1},{3,7},{2,6},{7,3},{6,2},{11,15},{10,14},{1... | collective-permute-start | bytes 1769480 | tf_op jit(solution)/shard_map/ppermute | solution.py:230
  47.1 6.0 %collective-permute-done.1.far_ref = bf16[256,1152]{1,0:T(8,128)(2,1)S(1)} collective-permute-done((bf16[256,1152]{1,0:T(8,128)(2,1)S(1)}, bf16[256,1152]{1,0:T(8,128)(2,1)S(1)}, u32[]{:S(2)}, u32[]{:S(2)}) %collective-permute-start.1) | collective-permute-done | bytes 589856 | tf_op jit(solution)/shard_map/ppermute | solution.py:228
  53.1 1.9 %collective-permute-start.2 = (bf16[256,1152]{1,0:T(8,128)(2,1)S(1)}, bf16[256,1152]{1,0:T(8,128)(2,1)S(1)}, u32[]{:S(2)}, u32[]{:S(2)}) collective-permute-start(bf16[256,1152]{1,0:T(8,128)(2,1)S(1)} %collective-permute-done.1.far_ref), channel_id=1, source_target_pairs={{0,4},{1,5},{4,0},{5,1},{3,7},{2,6},{7,3},{6,2},{11,15},{10,14},{1... | collective-permute-start | bytes 1769480 | tf_op jit(solution)/shard_map/ppermute | solution.py:231
  55.1 0.6 collective-permute-done.3.high_ref
  55.6 1.1 %shard_map.56 = (f32[128,128]{1,0:T(8,128)S(1)}, f32[8,256]{1,0:T(8,128)S(1)}) custom-call(bf16[256,1152]{1,0:T(8,128)(2,1)S(1)} %reshape.34.own_ref, bf16[256,1152]{1,0:T(8,128)(2,1)S(1)} %collective-permute-done.1.far_ref, bf16[256,1152]{1,0:T(8,128)(2,1)S(1)} %collective-permute-done.3.high_ref), custom_call_target="tpu_custom_call" | custom-call | flops 600000000 | bytes 1048576 | tf_op jit(solution)/shard_map/pallas_call | solution.py:233
  56.8 0.0 collective-permute-done.core_ref
  56.8 0.2 collective-permute-done.2.both_ref
  57.0 1.2 %shard_map.57 = (f32[32,128]{1,0:T(8,128)S(1)}, f32[8,128]{1,0:T(8,128)S(1)}) custom-call(bf16[256,1152]{1,0:T(8,128)(2,1)S(1)} %reshape.34.own_ref, bf16[256,1152]{1,0:T(8,128)(2,1)S(1)} %collective-permute-done.core_ref, bf16[256,1152]{1,0:T(8,128)(2,1)S(1)} %collective-permute-done.2.both_ref, bf16[256,1152]{1,0:T(8,128)(2,1)S(1)} %collective-permute-done.3.high_ref, ...), custom_call_target="tpu_custom_call" | custom-call | flops 600000000 | bytes 1048576 | tf_op jit(solution)/shard_map/pallas_call | solution.py:239
  58.3 6.2 %all_to_all.16 = f32[4,8,128]{2,1,0:T(8,128)S(1)} all-to-all(f32[4,8,128]{2,1,0:T(8,128)S(1)} %bitcast.14), channel_id=1, replica_groups={{0,1,4,5},{3,2,7,6},{11,10,15,14},{8,9,12,13},{16,17,20,21},{19,18,23,2..., dimensions={0} | all-to-all | bytes 32768 | tf_op jit(solution)/shard_map/all_to_all | solution.py:242
  64.5 0.1 shard_map.58
  64.6 25.8 %all_to_all.17 = f32[128,1,128]{2,1,0:T(1,128)S(1)} all-to-all(f32[128,1,128]{2,1,0:T(1,128)S(1)} %bitcast.12), channel_id=1, replica_groups={{0,3,8,11,16,19,24,27,32,35,40,43,48,51,56,59,64,67,72,75,80,83,88,91,9..., dimensions={0} | all-to-all | bytes 131072 | tf_op jit(solution)/shard_map/all_to_all | solution.py:246
  90.4 0.7 shard_map.59
Async XLA Ops:
  0.0 0.7 copy-start.1
  0.0 0.7 copy-start.2
  0.0 0.7 copy-start.3
  0.0 0.7 copy-start.4
  0.7 1.0 %copy-start = (bf16[128,1024]{1,0:T(8,128)(2,1)S(1)}, bf16[128,1024]{1,0:T(8,128)(2,1)}, u32[]{:S(2)}) copy-start(bf16[128,1024]{1,0:T(8,128)(2,1)} %x_ref.1) | copy-start | bytes 786436
  39.4 13.7 %collective-permute-start.1 = (bf16[256,1152]{1,0:T(8,128)(2,1)S(1)}, bf16[256,1152]{1,0:T(8,128)(2,1)S(1)}, u32[]{:S(2)}, u32[]{:S(2)}) collective-permute-start(bf16[256,1152]{1,0:T(8,128)(2,1)S(1)} %reshape.34.own_ref), channel_id=1, source_target_pairs={{0,1},{1,0},{4,5},{5,4},{3,2},{2,3},{7,6},{6,7},{11,10},{10,11},{1... | collective-permute-start | bytes 1769480 | tf_op jit(solution)/shard_map/ppermute | solution.py:228
  41.4 14.3 %collective-permute-start.3 = (bf16[256,1152]{1,0:T(8,128)(2,1)S(1)}, bf16[256,1152]{1,0:T(8,128)(2,1)S(1)}, u32[]{:S(2)}, u32[]{:S(2)}) collective-permute-start(bf16[256,1152]{1,0:T(8,128)(2,1)S(1)} %reshape.34.own_ref), channel_id=1, source_target_pairs={{0,448},{1,449},{4,452},{5,453},{3,0},{2,1},{7,4},{6,5},{11,3},{10... | collective-permute-start | bytes 1769480 | tf_op jit(solution)/shard_map/ppermute | solution.py:229
  45.2 11.6 %collective-permute-start = (bf16[256,1152]{1,0:T(8,128)(2,1)S(1)}, bf16[256,1152]{1,0:T(8,128)(2,1)S(1)}, u32[]{:S(2)}, u32[]{:S(2)}) collective-permute-start(bf16[256,1152]{1,0:T(8,128)(2,1)S(1)} %reshape.34.own_ref), channel_id=1, source_target_pairs={{0,4},{1,5},{4,0},{5,1},{3,7},{2,6},{7,3},{6,2},{11,15},{10,14},{1... | collective-permute-start | bytes 1769480 | tf_op jit(solution)/shard_map/ppermute | solution.py:230
  53.1 3.9 %collective-permute-start.2 = (bf16[256,1152]{1,0:T(8,128)(2,1)S(1)}, bf16[256,1152]{1,0:T(8,128)(2,1)S(1)}, u32[]{:S(2)}, u32[]{:S(2)}) collective-permute-start(bf16[256,1152]{1,0:T(8,128)(2,1)S(1)} %collective-permute-done.1.far_ref), channel_id=1, source_target_pairs={{0,4},{1,5},{4,0},{5,1},{3,7},{2,6},{7,3},{6,2},{11,15},{10,14},{1... | collective-permute-start | bytes 1769480 | tf_op jit(solution)/shard_map/ppermute | solution.py:231

commit v12 on v11

--- a/solution.py
+++ b/solution.py
@@ -68,7 +68,22 @@
     return jnp.where(mask, 1.0, 0.0).astype(BF16)
 
 
-def pack_kernel(x_ref, cl_ref, ord_ref, map_ref, nbr_ref, out_ref, place_ref):
+def pack_kernel(
+    x_hbm, cl_hbm, ord_hbm, map_hbm, nbr_hbm, out_ref, place_ref,
+    x_ref, cl_ref, ord_ref, map_ref, nbr_ref, sems,
+):
+    pairs = (
+        (cl_hbm, cl_ref),
+        (map_hbm, map_ref),
+        (nbr_hbm, nbr_ref),
+        (ord_hbm, ord_ref),
+        (x_hbm, x_ref),
+    )
+    copies = [pltpu.make_async_copy(a, b, sems.at[j]) for j, (a, b) in enumerate(pairs)]
+    for copy in copies[::-1]:
+        copy.start()
+    for copy in copies[:4]:
+        copy.wait()
     clusters = cl_ref[...]
     orders = ord_ref[...]
     count = map_ref.shape[1]
@@ -93,6 +108,7 @@
         meta = jnp.where(row == at, value.astype(F32), meta)
     meta = jnp.concatenate([meta, jnp.zeros((LANES - 16, LOAD), F32)], axis=0).astype(BF16)
 
+    copies[4].wait()
     scaled = x_ref[...].astype(F32)
     mean_square = jnp.mean(scaled * scaled, axis=-1, keepdims=True)
     factor = lax.rsqrt(mean_square + 1e-06) * D ** (-0.5)
@@ -197,13 +213,14 @@
     out_ref[...] = jnp.max(found, axis=0, keepdims=True)
 
 
-def call(kernel, outs, scratch=(), flops=0, size=1 << 20):
+def call(kernel, outs, scratch=(), flops=0, vmem=24, **more):
     return pl.pallas_call(
         kernel,
+        **more,
         out_shape=outs,
         scratch_shapes=list(scratch),
-        compiler_params=pltpu.CompilerParams(vmem_limit_bytes=24 << 20),
-        cost_estimate=pl.CostEstimate(flops=flops, bytes_accessed=size, transcendentals=0),
+        compiler_params=pltpu.CompilerParams(vmem_limit_bytes=vmem << 20),
+        cost_estimate=pl.CostEstimate(flops=flops, bytes_accessed=1 << 20, transcendentals=0),
     )
 
 
@@ -212,15 +229,21 @@
 
 
 def body(embeds, clusters, orders, owner_map, neighbours):
-    packed, place = call(
-        pack_kernel, [shape((QUART, WIDE), BF16), shape((8, LOAD), F32)], (), 10**8
-    )(
+    held = (
         embeds,
         clusters.reshape(1, LOAD),
         orders.reshape(1, LOAD),
         owner_map.reshape(1, -1),
         neighbours.T,
     )
+    packed, place = call(
+        pack_kernel,
+        [shape((QUART, WIDE), BF16), shape((8, LOAD), F32)],
+        [pltpu.VMEM(a.shape, a.dtype) for a in held] + [pltpu.SemaphoreType.DMA((5,))],
+        10**8,
+        vmem=60,
+        in_specs=[pl.BlockSpec(memory_space=pltpu.HBM)] * 5,
+    )(*held)
     got = lax.all_to_all(
         packed.reshape(OWNERS, 2, WIDE), AXES, 0, 0, axis_index_groups=GROUPS, tiled=True
     )

time: 91.4 us -> 93.3 us (1.021)
  Pallas kernels: 3.72 us -> 5.53 us
    pallas_call x1, Pallas kernels: 0.58 us -> 2.37 us  [body(): call(pack_kernel, [shape((QUART, WIDE), BF16), shape((8, LOAD), F32)], [p...]
    reshape x1, local copies, waits for them, and re-layouts: 0.22 us -> 1.9 us  [body(): packed.reshape(OWNERS, 2, WIDE)]
    unnamed x10 -> x2, local copies, waits for them, and re-layouts: 1.64 us -> 0.01 us
where the time goes in v12:
time: 93.3 us; the launch traced here: 92.9 us
  blocking collectives  68.7 us (74%)
  starting transfers between devices  9.58 us (10%)
  waiting for transfers between devices  6.85 us (7%)
  Pallas kernels  5.53 us (6%)
  local copies, waits for them, and re-layouts  2.13 us (2%)
    all_to_all x1, blocking collectives, body(): lax.all_to_all(packed.reshape(OWNERS, 2, WIDE), AXES, 0, 0, axis_index_gr...  36.7 us
    all_to_all x1, blocking collectives, body(): lax.all_to_all(best.reshape(OWNERS, 1, LANES), AXES, 0, 0, axis_index_gro...  25.8 us
    all_to_all x1, blocking collectives, body(): lax.all_to_all(best.reshape(4, 8, LANES), AXES, 0, 0, axis_index_groups=O...  6.2 us
    ppermute x1, waiting for transfers between devices, body(): far = lax.ppermute(own, AXES, X_SWAP)  6.03 us
    ppermute x1, starting transfers between devices, body(): high = lax.ppermute(own, AXES, DOWN)  3.83 us
    pallas_call x1, Pallas kernels, body(): call(pack_kernel, [shape((QUART, WIDE), BF16), shape((8, LOAD), F32)], [p...  2.37 us
    ppermute x1, starting transfers between devices, body(): far = lax.ppermute(own, AXES, X_SWAP)  1.92 us
    ppermute x1, starting transfers between devices, body(): core = lax.ppermute(own, AXES, C_SWAP)  1.92 us
  transfers between devices with their start and end apart: 4, of which 3 were waited for; matrix products, arithmetic and copies ran while one was open for 0% of the time, Pallas kernels for 1%

profile of v12, /device:TPU:8, one launch (start us, length us, event | category | flops | bytes accessed | tf_op | source)
XLA Modules:
  0.0 92.9 jit_solution(13403831997572216923)
XLA Ops:
  0.0 2.4 %shard_map.55 = (bf16[256,1152]{1,0:T(8,128)(2,1)}, f32[8,128]{1,0:T(8,128)}) custom-call(bf16[128,1024]{1,0:T(8,128)(2,1)} %x_hbm.1, s32[1,128]{1,0:T(1,128)} %bitcast.17, s32[1,128]{1,0:T(1,128)} %bitcast.18, s32[1,512]{1,0:T(1,128)} %bitcast.16, s32[2,512]{1,0:T(2,128)} %bitcast.15), custom_call_target="tpu_custom_call" | custom-call | flops 100000000 | bytes 1048576 | tf_op jit(solution)/shard_map/pallas_call | solution.py:239
  2.4 1.9 %reshape.33 = bf16[128,2,1152]{2,1,0:T(2,128)(2,1)S(1)} reshape(bf16[256,1152]{1,0:T(8,128)(2,1)} %get-tuple-element.11) | data formatting | bytes 1179648 | tf_op jit(solution)/shard_map/reshape | solution.py:248
  4.3 36.7 %all_to_all.15 = bf16[128,2,1152]{2,1,0:T(2,128)(2,1)S(1)} all-to-all(bf16[128,2,1152]{2,1,0:T(2,128)(2,1)S(1)} %reshape.33), channel_id=1, replica_groups={{0,3,8,11,16,19,24,27,32,35,40,43,48,51,56,59,64,67,72,75,80,83,88,91,9..., dimensions={0} | all-to-all | bytes 1179648 | tf_op jit(solution)/shard_map/all_to_all | solution.py:247
  41.0 0.2 reshape.34.own_ref
  41.3 1.9 %collective-permute-start.1 = (bf16[256,1152]{1,0:T(8,128)(2,1)S(1)}, bf16[256,1152]{1,0:T(8,128)(2,1)S(1)}, u32[]{:S(2)}, u32[]{:S(2)}) collective-permute-start(bf16[256,1152]{1,0:T(8,128)(2,1)S(1)} %reshape.34.own_ref), channel_id=1, source_target_pairs={{0,1},{1,0},{4,5},{5,4},{3,2},{2,3},{7,6},{6,7},{11,10},{10,11},{1... | collective-permute-start | bytes 1769480 | tf_op jit(solution)/shard_map/ppermute | solution.py:251
  43.2 3.8 %collective-permute-start.3 = (bf16[256,1152]{1,0:T(8,128)(2,1)S(1)}, bf16[256,1152]{1,0:T(8,128)(2,1)S(1)}, u32[]{:S(2)}, u32[]{:S(2)}) collective-permute-start(bf16[256,1152]{1,0:T(8,128)(2,1)S(1)} %reshape.34.own_ref), channel_id=1, source_target_pairs={{0,448},{1,449},{4,452},{5,453},{3,0},{2,1},{7,4},{6,5},{11,3},{10... | collective-permute-start | bytes 1769480 | tf_op jit(solution)/shard_map/ppermute | solution.py:252
  47.0 1.9 %collective-permute-start = (bf16[256,1152]{1,0:T(8,128)(2,1)S(1)}, bf16[256,1152]{1,0:T(8,128)(2,1)S(1)}, u32[]{:S(2)}, u32[]{:S(2)}) collective-permute-start(bf16[256,1152]{1,0:T(8,128)(2,1)S(1)} %reshape.34.own_ref), channel_id=1, source_target_pairs={{0,4},{1,5},{4,0},{5,1},{3,7},{2,6},{7,3},{6,2},{11,15},{10,14},{1... | collective-permute-start | bytes 1769480 | tf_op jit(solution)/shard_map/ppermute | solution.py:253
  48.9 6.0 %collective-permute-done.1.far_ref = bf16[256,1152]{1,0:T(8,128)(2,1)S(1)} collective-permute-done((bf16[256,1152]{1,0:T(8,128)(2,1)S(1)}, bf16[256,1152]{1,0:T(8,128)(2,1)S(1)}, u32[]{:S(2)}, u32[]{:S(2)}) %collective-permute-start.1) | collective-permute-done | bytes 589856 | tf_op jit(solution)/shard_map/ppermute | solution.py:251
  55.0 1.9 %collective-permute-start.2 = (bf16[256,1152]{1,0:T(8,128)(2,1)S(1)}, bf16[256,1152]{1,0:T(8,128)(2,1)S(1)}, u32[]{:S(2)}, u32[]{:S(2)}) collective-permute-start(bf16[256,1152]{1,0:T(8,128)(2,1)S(1)} %collective-permute-done.1.far_ref), channel_id=1, source_target_pairs={{0,4},{1,5},{4,0},{5,1},{3,7},{2,6},{7,3},{6,2},{11,15},{10,14},{1... | collective-permute-start | bytes 1769480 | tf_op jit(solution)/shard_map/ppermute | solution.py:254
  56.9 0.6 collective-permute-done.3.high_ref
  57.5 1.1 %shard_map.56 = (f32[128,128]{1,0:T(8,128)S(1)}, f32[8,256]{1,0:T(8,128)S(1)}) custom-call(bf16[256,1152]{1,0:T(8,128)(2,1)S(1)} %reshape.34.own_ref, bf16[256,1152]{1,0:T(8,128)(2,1)S(1)} %collective-permute-done.1.far_ref, bf16[256,1152]{1,0:T(8,128)(2,1)S(1)} %collective-permute-done.3.high_ref), custom_call_target="tpu_custom_call" | custom-call | flops 600000000 | bytes 1048576 | tf_op jit(solution)/shard_map/pallas_call | solution.py:256
  58.6 0.0 collective-permute-done.core_ref
  58.6 0.2 collective-permute-done.2.both_ref
  58.9 1.2 %shard_map.57 = (f32[32,128]{1,0:T(8,128)S(1)}, f32[8,128]{1,0:T(8,128)S(1)}) custom-call(bf16[256,1152]{1,0:T(8,128)(2,1)S(1)} %reshape.34.own_ref, bf16[256,1152]{1,0:T(8,128)(2,1)S(1)} %collective-permute-done.core_ref, bf16[256,1152]{1,0:T(8,128)(2,1)S(1)} %collective-permute-done.2.both_ref, bf16[256,1152]{1,0:T(8,128)(2,1)S(1)} %collective-permute-done.3.high_ref, ...), custom_call_target="tpu_custom_call" | custom-call | flops 600000000 | bytes 1048576 | tf_op jit(solution)/shard_map/pallas_call | solution.py:262
  60.1 6.2 %all_to_all.16 = f32[4,8,128]{2,1,0:T(8,128)S(1)} all-to-all(f32[4,8,128]{2,1,0:T(8,128)S(1)} %bitcast.14), channel_id=1, replica_groups={{0,1,4,5},{3,2,7,6},{11,10,15,14},{8,9,12,13},{16,17,20,21},{19,18,23,2..., dimensions={0} | all-to-all | bytes 32768 | tf_op jit(solution)/shard_map/all_to_all | solution.py:265
  66.3 0.1 shard_map.58
  66.4 0.0 copy-start
  66.4 25.8 %all_to_all.17 = f32[128,1,128]{2,1,0:T(1,128)S(1)} all-to-all(f32[128,1,128]{2,1,0:T(1,128)S(1)} %bitcast.12), channel_id=1, replica_groups={{0,3,8,11,16,19,24,27,32,35,40,43,48,51,56,59,64,67,72,75,80,83,88,91,9..., dimensions={0} | all-to-all | bytes 131072 | tf_op jit(solution)/shard_map/all_to_all | solution.py:269
  92.2 0.0 copy-done
  92.2 0.7 shard_map.59
Async XLA Ops:
  41.3 13.7 %collective-permute-start.1 = (bf16[256,1152]{1,0:T(8,128)(2,1)S(1)}, bf16[256,1152]{1,0:T(8,128)(2,1)S(1)}, u32[]{:S(2)}, u32[]{:S(2)}) collective-permute-start(bf16[256,1152]{1,0:T(8,128)(2,1)S(1)} %reshape.34.own_ref), channel_id=1, source_target_pairs={{0,1},{1,0},{4,5},{5,4},{3,2},{2,3},{7,6},{6,7},{11,10},{10,11},{1... | collective-permute-start | bytes 1769480 | tf_op jit(solution)/shard_map/ppermute | solution.py:251
  43.2 14.3 %collective-permute-start.3 = (bf16[256,1152]{1,0:T(8,128)(2,1)S(1)}, bf16[256,1152]{1,0:T(8,128)(2,1)S(1)}, u32[]{:S(2)}, u32[]{:S(2)}) collective-permute-start(bf16[256,1152]{1,0:T(8,128)(2,1)S(1)} %reshape.34.own_ref), channel_id=1, source_target_pairs={{0,448},{1,449},{4,452},{5,453},{3,0},{2,1},{7,4},{6,5},{11,3},{10... | collective-permute-start | bytes 1769480 | tf_op jit(solution)/shard_map/ppermute | solution.py:252
  47.0 11.6 %collective-permute-start = (bf16[256,1152]{1,0:T(8,128)(2,1)S(1)}, bf16[256,1152]{1,0:T(8,128)(2,1)S(1)}, u32[]{:S(2)}, u32[]{:S(2)}) collective-permute-start(bf16[256,1152]{1,0:T(8,128)(2,1)S(1)} %reshape.34.own_ref), channel_id=1, source_target_pairs={{0,4},{1,5},{4,0},{5,1},{3,7},{2,6},{7,3},{6,2},{11,15},{10,14},{1... | collective-permute-start | bytes 1769480 | tf_op jit(solution)/shard_map/ppermute | solution.py:253
  55.0 3.9 %collective-permute-start.2 = (bf16[256,1152]{1,0:T(8,128)(2,1)S(1)}, bf16[256,1152]{1,0:T(8,128)(2,1)S(1)}, u32[]{:S(2)}, u32[]{:S(2)}) collective-permute-start(bf16[256,1152]{1,0:T(8,128)(2,1)S(1)} %collective-permute-done.1.far_ref), channel_id=1, source_target_pairs={{0,4},{1,5},{4,0},{5,1},{3,7},{2,6},{7,3},{6,2},{11,15},{10,14},{1... | collective-permute-start | bytes 1769480 | tf_op jit(solution)/shard_map/ppermute | solution.py:254
  66.4 25.8 %copy-start = (f32[8,128]{1,0:T(8,128)S(1)}, f32[8,128]{1,0:T(8,128)}, u32[]{:S(2)}) copy-start(f32[8,128]{1,0:T(8,128)} %get-tuple-element.16.place_ref) | copy-start | bytes 12292
